TPU v7x, 32 devices: a whole 2x2x4 slice. The times are simulated.
32 devices in a mesh: blk: 16 (over z, y, core), event: 2 (over x).
Axes of the slice: x: 2, y: 2, z: 4, core: 2. Of those that a mesh axis runs over, the one named last changes fastest.
Arguments:
- adjoint_now: float32 [2, 3, 128, 64, 128], P('event', None, 'blk'), may hold values from -6 to 6
- adjoint_prev: float32 [2, 3, 128, 64, 128], P('event', None, 'blk'), may hold values from -6 to 6
- forward_field: float32 [2, 2, 3, 128, 64, 128], P('event', None, None, 'blk'), may hold values from -6 to 6
- density: float32 [128, 64, 128], P('blk'), may hold values from 0.5 to 2
- lame_first: float32 [128, 64, 128], P('blk'), may hold values from 0.5 to 2
- shear_modulus: float32 [128, 64, 128], P('blk'), may hold values from 0.3 to 1.2
Outputs:
- adjoint_field: float32 [2, 3, 128, 64, 128], P('event', None, 'blk')
- shear_kernel: float32 [128, 64, 128], P('blk', 'event')
- bulk_kernel: float32 [128, 64, 128], P('blk', 'event')
All inputs are finite; a program needn't handle non-finite values.
Results may differ from a plain program's by a relative error of at most 0.00002.
Values sent between devices are 32-bit elements; how exact they have to be, the bound alone decides.
No kernel may reach another device: no remote copies, remote signals or barrier semaphores. Data moves between devices by JAX's collectives and lax.ppermute only.
A program may use at most 64 MiB of HBM per device.

v0:
```python
import jax
import jax.numpy as jnp
from jax import lax
from jax.sharding import PartitionSpec as P

time_step = 0.3


def with_halo(block, sides, width):
    for axis, dim in sides:
        count = lax.axis_size(axis)
        forward = [(i, i + 1) for i in range(count - 1)]
        forward.append((count - 1, 0))
        backward = [(target, source) for source, target in forward]
        low = lax.ppermute(
            lax.slice_in_dim(block, block.shape[dim] - width, None, axis=dim), axis, forward
        )
        high = lax.ppermute(lax.slice_in_dim(block, 0, width, axis=dim), axis, backward)
        block = jnp.concatenate([low, block, high], axis=dim)
    return block


def slope_long(values):
    return (values[2:] - values[:-2]) * 0.5


def slope_mid(values, axis):
    padded = jnp.pad(values, [(1, 1) if dimension == axis else (0, 0) for dimension in range(3)])
    upper = lax.slice_in_dim(padded, 2, padded.shape[axis], axis=axis)
    lower = lax.slice_in_dim(padded, 0, padded.shape[axis] - 2, axis=axis)
    return (upper - lower) * 0.5


def gradient(field):
    table = [[None, None, None], [None, None, None], [None, None, None]]
    for second in range(3):
        component = field[second]
        middle = component[1:-1]
        table[0][second] = slope_long(component)
        table[1][second] = slope_mid(middle, 1)
        table[2][second] = slope_mid(middle, 2)
    return table


def strain_of(table):
    strain = [
        [0.5 * (table[first][second] + table[second][first]) for second in range(3)]
        for first in range(3)
    ]
    trace = strain[0][0] + strain[1][1] + strain[2][2]
    return (strain, trace)


def stress_of(strain, trace, first_lame, shear_part):
    stress = []
    for first in range(3):
        stress_row = []
        for second in range(3):
            entry = 2.0 * shear_part * strain[first][second]
            if first == second:
                entry = entry + first_lame * trace
            stress_row.append(entry)
        stress.append(stress_row)
    return stress


def divergence(stress):
    result = []
    for second in range(3):
        total = slope_long(stress[0][second])
        total = total + slope_mid(stress[1][second], 1)[1:-1]
        total = total + slope_mid(stress[2][second], 2)[1:-1]
        result.append(total)
    return result


def crop(values, count, axis):
    return lax.slice_in_dim(values, count, values.shape[axis] - count, axis=axis)


def kernel_terms(strain, trace, forward_strain, forward_trace, first_lame, shear_part):
    contracted = strain[0][0] * forward_strain[0][0]
    for first in range(3):
        for second in range(3):
            if first + second > 0:
                contracted = contracted + strain[first][second] * forward_strain[first][second]
    shear_term = -2.0 * time_step * shear_part * (contracted - trace * forward_trace / 3.0)
    bulk_term = -time_step * (first_lame + 2.0 * shear_part / 3.0) * trace * forward_trace
    return (shear_term, bulk_term)


def advance(wide, prev_cut, model_cut, dens_cut, forward_wide, slab_cells):
    strain, trace = strain_of(gradient(wide))
    stress = stress_of(strain, trace, model_cut[0], model_cut[1])
    accel = jnp.stack(divergence(stress))
    updated = 2.0 * crop(wide, 2, 1) - prev_cut + time_step * time_step * accel / dens_cut
    margin = (wide.shape[1] - slab_cells) // 2
    inner = [[crop(entry, margin - 1, 0) for entry in strain_row] for strain_row in strain]
    inner_trace = crop(trace, margin - 1, 0)
    forward_strain, forward_trace = strain_of(gradient(forward_wide))
    model_margin = (model_cut.shape[1] - slab_cells) // 2
    first_lame = crop(model_cut[0], model_margin, 0)
    shear_part = crop(model_cut[1], model_margin, 0)
    return (
        updated,
        kernel_terms(inner, inner_trace, forward_strain, forward_trace, first_lame, shear_part),
    )


def local(adjoint_now, adjoint_prev, forward_field, density, lame_first, shear_modulus):
    slab_cells = density.shape[0]
    current = adjoint_now[0]
    former = adjoint_prev[0]
    forward = forward_field[0]
    step_count = forward.shape[0]
    forward_wide = with_halo(forward, (("blk", 2),), 1)
    moduli = jnp.stack([lame_first, shear_modulus])
    shear_total = jnp.zeros(density.shape, jnp.float32)
    bulk_total = jnp.zeros(density.shape, jnp.float32)
    band_shear = None
    band_bulk = None
    model_wide = with_halo(moduli, (("blk", 1),), 1)
    for step in range(step_count):
        wide = with_halo(current, (("blk", 1),), 2)
        updated, terms = advance(wide, former, model_wide, density, forward_wide[step], slab_cells)
        shear_total = shear_total + terms[0]
        bulk_total = bulk_total + terms[1]
        former = current
        current = updated
    band_shear, band_bulk = (
        lax.psum_scatter(shear_total, "event", scatter_dimension=1, tiled=True),
        lax.psum_scatter(bulk_total, "event", scatter_dimension=1, tiled=True),
    )
    return (current[None], band_shear, band_bulk)


def solution(mesh):
    in_specs = (
        P("event", None, "blk", None, None),
        P("event", None, "blk", None, None),
        P("event", None, None, "blk", None, None),
        P("blk", None, None),
        P("blk", None, None),
        P("blk", None, None),
    )
    out_specs = (
        P("event", None, "blk", None, None),
        P("blk", "event", None),
        P("blk", "event", None),
    )
    return jax.shard_map(local, mesh=mesh, in_specs=in_specs, out_specs=out_specs, check_vma=False)
```

profile of v0, /device:TPU:0, one launch (start us, length us, event | category | flops | bytes accessed | tf_op | source)
XLA Modules:
  0.0 78.5 jit_solution(4601876021660620575)
XLA Ops:
  7.2 0.0 reduce-scatter.3.cloned.1.call-start
  7.2 0.9 %pad_maximum_fusion.12 = (f32[2,1,64,128]{3,2,1,0:T(8,128)S(1)}, f32[2,1,64,128]{3,2,1,0:T(8,128)S(1)}) fusion(f32[1,8,64,128]{3,2,1,0:T(8,128)} %bitcast.197, f32[1,8,64,128]{3,2,1,0:T(8,128)} %bitcast.199), kind=kLoop, calls=%fused_computation.331 | loop fusion | flops 32768 | bytes 655360 | tf_op jit(solution)/shard_map/slice | solution.py:16
  8.1 5.5 %collective-permute-start.1 = (f32[2,1,64,128]{3,2,1,0:T(8,128)S(1)}, f32[2,1,64,128]{3,2,1,0:T(8,128)S(1)}, u32[]{:S(2)}, u32[]{:S(2)}) collective-permute-start(f32[2,1,64,128]{3,2,1,0:T(8,128)S(1)} %get-tuple-element.66), channel_id=1, source_target_pairs={{2,0},{4,2},{6,4},{8,6},{10,8},{12,10},{14,12},{16,14},{18,16},{20... | collective-permute-start | bytes 196616 | tf_op jit(solution)/shard_map/ppermute | solution.py:18
  13.6 1.0 %fusion.197 = (f32[3,2,64,128]{3,2,1,0:T(8,128)S(1)}, f32[3,2,64,128]{3,2,1,0:T(8,128)S(1)}) fusion(f32[3,8,64,128]{3,2,1,0:T(8,128)} %bitcast.189), kind=kLoop, calls=%fused_computation.340 | loop fusion | bytes 786432 | tf_op jit(solution)/shard_map/slice | solution.py:18
  14.7 0.1 collective-permute-start.3
  14.7 4.5 %collective-permute-start.2 = (f32[3,2,64,128]{3,2,1,0:T(8,128)S(1)}, f32[3,2,64,128]{3,2,1,0:T(8,128)S(1)}, u32[]{:S(2)}, u32[]{:S(2)}) collective-permute-start(f32[3,2,64,128]{3,2,1,0:T(8,128)S(1)} %get-tuple-element.59), channel_id=1, source_target_pairs={{2,0},{4,2},{6,4},{8,6},{10,8},{12,10},{14,12},{16,14},{18,16},{20... | collective-permute-start | bytes 589832 | tf_op jit(solution)/shard_map/ppermute | solution.py:18
  19.2 1.0 %fusion.195 = (f32[2,3,1,64,128]{4,3,2,1,0:T(8,128)S(1)}, f32[2,3,1,64,128]{4,3,2,1,0:T(8,128)S(1)}) fusion(f32[2,3,8,64,128]{4,3,2,1,0:T(8,128)} %bitcast.193), kind=kLoop, calls=%fused_computation.338 | loop fusion | bytes 786432 | tf_op jit(solution)/shard_map/slice | solution.py:18
  20.3 0.1 collective-permute-start.7
  20.4 4.4 %collective-permute-start.6 = (f32[2,3,1,64,128]{4,3,2,1,0:T(8,128)S(1)}, f32[2,3,1,64,128]{4,3,2,1,0:T(8,128)S(1)}, u32[]{:S(2)}, u32[]{:S(2)}) collective-permute-start(f32[2,3,1,64,128]{4,3,2,1,0:T(8,128)S(1)} %get-tuple-element.35), channel_id=1, source_target_pairs={{2,0},{4,2},{6,4},{8,6},{10,8},{12,10},{14,12},{16,14},{18,16},{20... | collective-permute-start | bytes 589832 | tf_op jit(solution)/shard_map/ppermute | solution.py:18
  24.8 0.1 pad_maximum_fusion
  24.9 0.1 fusion.63
  25.0 0.5 fusion.178
  25.5 0.2 pad_slice_fusion.31
  25.7 0.4 fusion.180
  26.1 0.4 pad_slice_fusion.29
  26.5 0.1 pad_slice_fusion.69
  26.7 0.1 fusion.161
  26.8 0.1 fusion.166
  26.9 0.1 fusion.171
  27.1 0.4 copy-done.11
  27.5 0.7 copy-done.7
  28.2 0.1 copy-done.31
  28.3 0.3 fusion.6
  28.6 0.1 collective-permute-start.5
  28.7 4.4 %collective-permute-start.4 = (f32[3,2,64,128]{3,2,1,0:T(8,128)S(1)}, f32[3,2,64,128]{3,2,1,0:T(8,128)S(1)}, u32[]{:S(2)}, u32[]{:S(2)}) collective-permute-start(f32[3,2,64,128]{3,2,1,0:T(8,128)S(1)} %get-tuple-element.57), channel_id=1, source_target_pairs={{2,0},{4,2},{6,4},{8,6},{10,8},{12,10},{14,12},{16,14},{18,16},{20... | collective-permute-start | bytes 589832 | tf_op jit(solution)/shard_map/ppermute | solution.py:18
  33.1 0.2 slice_bitcast_fusion.7
  33.3 3.1 %collective-permute-done.5 = f32[3,2,64,128]{3,2,1,0:T(8,128)S(1)} collective-permute-done((f32[3,2,64,128]{3,2,1,0:T(8,128)S(1)}, f32[3,2,64,128]{3,2,1,0:T(8,128)S(1)}, u32[]{:S(2)}, u32[]{:S(2)}) %collective-permute-start.5) | collective-permute-done | bytes 196640 | tf_op jit(solution)/shard_map/ppermute | solution.py:15
  36.4 0.1 fusion.60
  36.5 1.3 %fusion.175 = (f32[10,64,128]{2,1,0:T(8,128)}, f32[10,64,128]{2,1,0:T(8,128)S(1)}, f32[10,64,128]{2,1,0:T(8,128)}, f32[10,64,128]{2,1,0:T(8,128)S(1)}, f32[10,64...) fusion(f32[2,10,64,128]{3,2,1,0:T(8,128)S(1)} %pad_maximum_fusion, ...), kind=kLoop, calls=%fused_computation.332 | loop fusion | flops 1802240 | bytes 4784128 | tf_op jit(solution)/shard_map/mul | solution.py:59
  37.8 0.4 fusion.177
  38.3 1.1 %pad_slice_fusion.17 = (f32[10,64,128]{2,1,0:T(8,128)}, f32[10,64,128]{2,1,0:T(8,128)}) fusion(f32[10,64,128]{2,1,0:T(8,128)S(1)} %get-tuple-element.61), kind=kLoop, calls=%fused_computation.29 | loop fusion | bytes 983040 | tf_op jit(solution)/shard_map/slice | solution.py:29
  39.4 0.9 %pad_slice_fusion.57 = (f32[10,64,128]{2,1,0:T(8,128)}, f32[10,64,128]{2,1,0:T(8,128)}) fusion(f32[10,64,128]{2,1,0:T(8,128)S(1)} %get-tuple-element.62), kind=kLoop, calls=%fused_computation.70 | loop fusion | bytes 983040 | tf_op jit(solution)/shard_map/slice | solution.py:29
  40.3 1.1 %pad_slice_fusion.23 = (f32[10,64,128]{2,1,0:T(8,128)}, f32[10,64,128]{2,1,0:T(8,128)}) fusion(f32[10,64,128]{2,1,0:T(8,128)S(1)} %get-tuple-element.25), kind=kLoop, calls=%fused_computation.35 | loop fusion | bytes 983040 | tf_op jit(solution)/shard_map/slice | solution.py:29
  41.5 0.6 copy-done.33
  42.1 2.0 %fusion.112 = f32[8,64,128]{2,1,0:T(8,128)} fusion(f32[10,64,128]{2,1,0:T(8,128)S(1)} %get-tuple-element.39, f32[10,64,128]{2,1,0:T(8,128)S(1)} %get-tuple-element.40, f32[8,64,128]{2,1,0:T(8,128)S(1)} %get-tuple-element.31, f32[8,64,128]{2,1,0:T(8,128)S(1)} %get-tuple-element.30, f32[10,64,128]{2,1,0:T(8,128)S(1)} %get-tuple-element.13, ...), kind=kLoop, calls=%fused_computation.228 | loop fusion | flops 6225920 | bytes 7733248 | tf_op jit(solution)/shard_map/add | solution.py:126
  44.1 0.0 reduce-scatter.5.cloned.1.call-start
  44.2 0.9 %pad_slice_fusion.59 = (f32[10,64,128]{2,1,0:T(8,128)}, f32[10,64,128]{2,1,0:T(8,128)}) fusion(f32[10,64,128]{2,1,0:T(8,128)S(1)} %get-tuple-element.8), kind=kLoop, calls=%fused_computation.72 | loop fusion | bytes 983040 | tf_op jit(solution)/shard_map/slice | solution.py:29
  45.1 2.8 %pad_slice_fusion.19 = (f32[10,64,128]{2,1,0:T(8,128)}, f32[10,64,128]{2,1,0:T(8,128)}, f32[10,64,128]{2,1,0:T(8,128)}, f32[10,64,128]{2,1,0:T(8,128)}) fusion(f32[10,64,128]{2,1,0:T(8,128)} %get-tuple-element.12), kind=kLoop, calls=%fused_computation.31 | loop fusion | bytes 1638400 | tf_op jit(solution)/shard_map/slice | solution.py:29
  48.0 1.1 %multiply_add_fusion.4 = f32[8,64,128]{2,1,0:T(8,128)} fusion(f32[8,64,128]{2,1,0:T(8,128)S(1)} %copy-done.10, f32[8,64,128]{2,1,0:T(8,128)S(1)} %copy-done.6, f32[2,3,8,64,128]{4,3,2,1,0:T(8,128)S(1)} %bitcast.196, f32[2,3,1,64,128]{4,3,2,1,0:T(8,128)S(1)} %collective-permute-done.7, f32[2,3,1,64,128]{4,3,2,1,0:T(8,128)S(1)} %copy-done.34, ...), kind=kLoop, calls=%fused_computation.327 | loop fusion | flops 2228224 | bytes 4325376 | tf_op jit(solution)/shard_map/add | solution.py:127
  49.2 1.4 %fusion.144 = f32[1,1,8,64,128]{4,3,2,1,0:T(8,128)S(1)} fusion(f32[10,64,128]{2,1,0:T(8,128)} %get-tuple-element.78, f32[10,64,128]{2,1,0:T(8,128)} %get-tuple-element.77, f32[10,64,128]{2,1,0:T(8,128)} %get-tuple-element.74, f32[10,64,128]{2,1,0:T(8,128)} %get-tuple-element.76, f32[10,64,128]{2,1,0:T(8,128)S(1)} %get-tuple-element.25), kind=kLoop, calls=%fused_computation.279 | loop fusion | flops 524288 | bytes 1835008 | tf_op jit(solution)/shard_map/stack | solution.py:95
  50.7 1.4 %fusion.150 = f32[1,1,8,64,128]{4,3,2,1,0:T(8,128)S(1)} fusion(f32[10,64,128]{2,1,0:T(8,128)} %get-tuple-element.75, f32[10,64,128]{2,1,0:T(8,128)} %get-tuple-element.73, f32[10,64,128]{2,1,0:T(8,128)} %get-tuple-element.72, f32[10,64,128]{2,1,0:T(8,128)S(1)} %copy-done.28, f32[10,64,128]{2,1,0:T(8,128)S(1)} %get-tuple-element.8), kind=kLoop, calls=%fused_computation.288 | loop fusion | flops 524288 | bytes 1835008 | tf_op jit(solution)/shard_map/stack | solution.py:95
  52.1 0.1 fusion.156
  52.2 0.0 copy-done.14
  52.3 0.1 copy-done.16
  52.3 0.1 copy-done.32
  52.4 1.2 %fusion.4 = f32[1,3,8,64,128]{4,3,2,1,0:T(8,128)} fusion(f32[1,3,8,64,128]{4,3,2,1,0:T(8,128)S(1)} %copy-done, f32[1,1,8,64,128]{4,3,2,1,0:T(8,128)S(1)} %bitcast.202, f32[1,1,8,64,128]{4,3,2,1,0:T(8,128)S(1)} %bitcast.204, f32[1,1,8,64,128]{4,3,2,1,0:T(8,128)S(1)} %bitcast.206, f32[1,1,8,64,128]{4,3,2,1,0:T(8,128)S(1)} %fusion.144, ...), kind=kLoop, calls=%fused_computation.21 | loop fusion | flops 2752512 | bytes 4194304 | tf_op jit(solution)/shard_map/add | solution.py:96
  53.7 3.4 %reduce-scatter.3.cloned.1.call-done = f32[8,32,128]{2,1,0:T(8,128)} async-done(((f32[8,64,128]{2,1,0:T(8,128)}), f32[8,32,128]{2,1,0:T(8,128)}) %reduce-scatter.3.cloned.1.call-update) | async-done | bytes 131088 | tf_op jit(solution)/shard_map/reduce_scatter | solution.py:131
  57.1 14.6 %reduce-scatter.5.cloned.1.call-done = f32[8,32,128]{2,1,0:T(8,128)} async-done(((f32[8,64,128]{2,1,0:T(8,128)}), f32[8,32,128]{2,1,0:T(8,128)}) %reduce-scatter.5.cloned.1.call-update) | async-done | bytes 131088 | tf_op jit(solution)/shard_map/reduce_scatter | solution.py:132
  (74 shorter events, 0.2 us)
Async XLA Ops:
  7.2 17.6 %copy-start.4 = (f32[8,64,128]{2,1,0:T(8,128)S(1)}, f32[8,64,128]{2,1,0:T(8,128)}, u32[]{:S(2)}) copy-start(f32[8,64,128]{2,1,0:T(8,128)} %param.11) | copy-start | bytes 786436
  7.2 17.6 %copy-start.9 = (f32[8,64,128]{2,1,0:T(8,128)S(1)}, f32[8,64,128]{2,1,0:T(8,128)}, u32[]{:S(2)}) copy-start(f32[8,64,128]{2,1,0:T(8,128)} %param.10) | copy-start | bytes 786436
  7.2 49.9 %reduce-scatter.3.cloned.1.call-start = ((), (), s32[]{:S(2)}) async-start(), calls=%async_computation.2 | async-start | bytes 393216 | tf_op jit(solution)/shard_map/reduce_scatter | solution.py:131
  8.1 16.8 %copy-start = (f32[1,3,8,64,128]{4,3,2,1,0:T(8,128)S(1)}, f32[1,3,8,64,128]{4,3,2,1,0:T(8,128)}, u32[]{:S(2)}) copy-start(f32[1,3,8,64,128]{4,3,2,1,0:T(8,128)} %param.6) | copy-start | bytes 2359300
  8.1 12.2 %collective-permute-start.1 = (f32[2,1,64,128]{3,2,1,0:T(8,128)S(1)}, f32[2,1,64,128]{3,2,1,0:T(8,128)S(1)}, u32[]{:S(2)}, u32[]{:S(2)}) collective-permute-start(f32[2,1,64,128]{3,2,1,0:T(8,128)S(1)} %get-tuple-element.66), channel_id=1, source_target_pairs={{2,0},{4,2},{6,4},{8,6},{10,8},{12,10},{14,12},{16,14},{18,16},{20... | collective-permute-start | bytes 196616 | tf_op jit(solution)/shard_map/ppermute | solution.py:18
  13.6 11.2 %collective-permute-start = (f32[2,1,64,128]{3,2,1,0:T(8,128)S(1)}, f32[2,1,64,128]{3,2,1,0:T(8,128)S(1)}, u32[]{:S(2)}, u32[]{:S(2)}) collective-permute-start(f32[2,1,64,128]{3,2,1,0:T(8,128)S(1)} %get-tuple-element.65), channel_id=1, source_target_pairs={{0,2},{2,4},{4,6},{6,8},{8,10},{10,12},{12,14},{14,16},{16,18},{18... | collective-permute-start | bytes 196616 | tf_op jit(solution)/shard_map/ppermute | solution.py:15
  14.7 10.2 %collective-permute-start.3 = (f32[3,2,64,128]{3,2,1,0:T(8,128)S(1)}, f32[3,2,64,128]{3,2,1,0:T(8,128)S(1)}, u32[]{:S(2)}, u32[]{:S(2)}) collective-permute-start(f32[3,2,64,128]{3,2,1,0:T(8,128)S(1)} %get-tuple-element.60), channel_id=1, source_target_pairs={{0,2},{2,4},{4,6},{6,8},{8,10},{10,12},{12,14},{14,16},{16,18},{18... | collective-permute-start | bytes 589832 | tf_op jit(solution)/shard_map/ppermute | solution.py:15
  14.7 10.1 %collective-permute-start.2 = (f32[3,2,64,128]{3,2,1,0:T(8,128)S(1)}, f32[3,2,64,128]{3,2,1,0:T(8,128)S(1)}, u32[]{:S(2)}, u32[]{:S(2)}) collective-permute-start(f32[3,2,64,128]{3,2,1,0:T(8,128)S(1)} %get-tuple-element.59), channel_id=1, source_target_pairs={{2,0},{4,2},{6,4},{8,6},{10,8},{12,10},{14,12},{16,14},{18,16},{20... | collective-permute-start | bytes 589832 | tf_op jit(solution)/shard_map/ppermute | solution.py:18
  20.3 21.1 %collective-permute-start.7 = (f32[2,3,1,64,128]{4,3,2,1,0:T(8,128)S(1)}, f32[2,3,1,64,128]{4,3,2,1,0:T(8,128)S(1)}, u32[]{:S(2)}, u32[]{:S(2)}) collective-permute-start(f32[2,3,1,64,128]{4,3,2,1,0:T(8,128)S(1)} %get-tuple-element.36), channel_id=1, source_target_pairs={{0,2},{2,4},{4,6},{6,8},{8,10},{10,12},{12,14},{14,16},{16,18},{18... | collective-permute-start | bytes 589832 | tf_op jit(solution)/shard_map/ppermute | solution.py:15
  20.4 21.1 %collective-permute-start.6 = (f32[2,3,1,64,128]{4,3,2,1,0:T(8,128)S(1)}, f32[2,3,1,64,128]{4,3,2,1,0:T(8,128)S(1)}, u32[]{:S(2)}, u32[]{:S(2)}) collective-permute-start(f32[2,3,1,64,128]{4,3,2,1,0:T(8,128)S(1)} %get-tuple-element.35), channel_id=1, source_target_pairs={{2,0},{4,2},{6,4},{8,6},{10,8},{12,10},{14,12},{16,14},{18,16},{20... | collective-permute-start | bytes 589832 | tf_op jit(solution)/shard_map/ppermute | solution.py:18
  26.8 0.7 copy-start.11
  26.8 1.4 %copy-start.7 = (f32[1,3,8,64,128]{4,3,2,1,0:T(8,128)S(1)}, f32[1,3,8,64,128]{4,3,2,1,0:T(8,128)}, u32[]{:S(2)}) copy-start(f32[1,3,8,64,128]{4,3,2,1,0:T(8,128)} %param.7) | copy-start | bytes 2359300
  26.8 1.5 %copy-start.31 = (f32[8,64,128]{2,1,0:T(8,128)S(1)}, f32[8,64,128]{2,1,0:T(8,128)}, u32[]{:S(2)}) copy-start(f32[8,64,128]{2,1,0:T(8,128)} %param.9) | copy-start | bytes 786436
  26.9 1.6 %copy-start.13 = (f32[8,64,128]{2,1,0:T(8,128)}, f32[8,64,128]{2,1,0:T(8,128)S(1)}, u32[]{:S(2)}) copy-start(f32[8,64,128]{2,1,0:T(8,128)S(1)} %fusion.166) | copy-start | bytes 786436
  27.1 1.5 %copy-start.15 = (f32[8,64,128]{2,1,0:T(8,128)}, f32[8,64,128]{2,1,0:T(8,128)S(1)}, u32[]{:S(2)}) copy-start(f32[8,64,128]{2,1,0:T(8,128)S(1)} %fusion.171) | copy-start | bytes 786436
  28.3 4.8 %copy-start.1 = (f32[1,2,3,8,64,128]{5,4,3,2,1,0:T(8,128)S(1)}, f32[1,2,3,8,64,128]{5,4,3,2,1,0:T(8,128)}, u32[]{:S(2)}) copy-start(f32[1,2,3,8,64,128]{5,4,3,2,1,0:T(8,128)} %param.8) | copy-start | bytes 4718596
  28.6 7.8 %collective-permute-start.5 = (f32[3,2,64,128]{3,2,1,0:T(8,128)S(1)}, f32[3,2,64,128]{3,2,1,0:T(8,128)S(1)}, u32[]{:S(2)}, u32[]{:S(2)}) collective-permute-start(f32[3,2,64,128]{3,2,1,0:T(8,128)S(1)} %get-tuple-element.58), channel_id=1, source_target_pairs={{0,2},{2,4},{4,6},{6,8},{8,10},{10,12},{12,14},{14,16},{16,18},{18... | collective-permute-start | bytes 589832 | tf_op jit(solution)/shard_map/ppermute | solution.py:15
  28.7 7.8 %collective-permute-start.4 = (f32[3,2,64,128]{3,2,1,0:T(8,128)S(1)}, f32[3,2,64,128]{3,2,1,0:T(8,128)S(1)}, u32[]{:S(2)}, u32[]{:S(2)}) collective-permute-start(f32[3,2,64,128]{3,2,1,0:T(8,128)S(1)} %get-tuple-element.57), channel_id=1, source_target_pairs={{2,0},{4,2},{6,4},{8,6},{10,8},{12,10},{14,12},{16,14},{18,16},{20... | collective-permute-start | bytes 589832 | tf_op jit(solution)/shard_map/ppermute | solution.py:18
  33.3 8.2 %copy-start.17 = (f32[8,64,128]{2,1,0:T(8,128)}, f32[8,64,128]{2,1,0:T(8,128)S(1)}, u32[]{:S(2)}) copy-start(f32[8,64,128]{2,1,0:T(8,128)S(1)} %get-tuple-element.30) | copy-start | bytes 786436
  33.3 8.2 %copy-start.19 = (f32[8,64,128]{2,1,0:T(8,128)}, f32[8,64,128]{2,1,0:T(8,128)S(1)}, u32[]{:S(2)}) copy-start(f32[8,64,128]{2,1,0:T(8,128)S(1)} %get-tuple-element.31) | copy-start | bytes 786436
  33.3 8.2 %copy-start.21 = (f32[8,64,128]{2,1,0:T(8,128)}, f32[8,64,128]{2,1,0:T(8,128)S(1)}, u32[]{:S(2)}) copy-start(f32[8,64,128]{2,1,0:T(8,128)S(1)} %get-tuple-element.33) | copy-start | bytes 786436
  33.3 8.2 %copy-start.23 = (f32[8,64,128]{2,1,0:T(8,128)}, f32[8,64,128]{2,1,0:T(8,128)S(1)}, u32[]{:S(2)}) copy-start(f32[8,64,128]{2,1,0:T(8,128)S(1)} %get-tuple-element.34) | copy-start | bytes 786436
  37.8 3.6 %copy-start.2 = (f32[10,64,128]{2,1,0:T(8,128)}, f32[10,64,128]{2,1,0:T(8,128)S(1)}, u32[]{:S(2)}) copy-start(f32[10,64,128]{2,1,0:T(8,128)S(1)} %get-tuple-element.38) | copy-start | bytes 983044
  38.3 3.8 %copy-start.5 = (f32[8,64,128]{2,1,0:T(8,128)S(1)}, f32[8,64,128]{2,1,0:T(8,128)}, u32[]{:S(2)}) copy-start(f32[8,64,128]{2,1,0:T(8,128)} %param.11) | copy-start | bytes 786436
  41.4 0.7 copy-start.33
  44.1 27.6 %reduce-scatter.5.cloned.1.call-start = ((), (), s32[]{:S(2)}) async-start(), calls=%async_computation.3 | async-start | bytes 393216 | tf_op jit(solution)/shard_map/reduce_scatter | solution.py:132
  44.1 3.8 %copy-start.3 = (f32[10,64,128]{2,1,0:T(8,128)S(1)}, f32[10,64,128]{2,1,0:T(8,128)}, u32[]{:S(2)}) copy-start(f32[10,64,128]{2,1,0:T(8,128)} %copy-done.2) | copy-start | bytes 983044
  44.2 3.8 %copy-start.6 = (f32[8,64,128]{2,1,0:T(8,128)S(1)}, f32[8,64,128]{2,1,0:T(8,128)}, u32[]{:S(2)}) copy-start(f32[8,64,128]{2,1,0:T(8,128)} %param.11) | copy-start | bytes 786436
  44.2 3.8 %copy-start.10 = (f32[8,64,128]{2,1,0:T(8,128)S(1)}, f32[8,64,128]{2,1,0:T(8,128)}, u32[]{:S(2)}) copy-start(f32[8,64,128]{2,1,0:T(8,128)} %param.10) | copy-start | bytes 786436
  44.2 3.8 %copy-start.18 = (f32[8,64,128]{2,1,0:T(8,128)S(1)}, f32[8,64,128]{2,1,0:T(8,128)}, u32[]{:S(2)}) copy-start(f32[8,64,128]{2,1,0:T(8,128)} %copy-done.17) | copy-start | bytes 786436
  44.2 3.8 %copy-start.20 = (f32[8,64,128]{2,1,0:T(8,128)S(1)}, f32[8,64,128]{2,1,0:T(8,128)}, u32[]{:S(2)}) copy-start(f32[8,64,128]{2,1,0:T(8,128)} %copy-done.19) | copy-start | bytes 786436
  44.2 3.8 %copy-start.22 = (f32[8,64,128]{2,1,0:T(8,128)S(1)}, f32[8,64,128]{2,1,0:T(8,128)}, u32[]{:S(2)}) copy-start(f32[8,64,128]{2,1,0:T(8,128)} %copy-done.21) | copy-start | bytes 786436
  44.2 3.8 %copy-start.24 = (f32[8,64,128]{2,1,0:T(8,128)S(1)}, f32[8,64,128]{2,1,0:T(8,128)}, u32[]{:S(2)}) copy-start(f32[8,64,128]{2,1,0:T(8,128)} %copy-done.23) | copy-start | bytes 786436
  44.2 3.8 %copy-start.34 = (f32[2,3,1,64,128]{4,3,2,1,0:T(8,128)S(1)}, f32[2,3,1,64,128]{4,3,2,1,0:T(8,128)}, u32[]{:S(2)}) copy-start(f32[2,3,1,64,128]{4,3,2,1,0:T(8,128)} %copy-done.33) | copy-start | bytes 589828
  49.1 1.5 %copy-start.28 = (f32[10,64,128]{2,1,0:T(8,128)S(1)}, f32[10,64,128]{2,1,0:T(8,128)}, u32[]{:S(2)}) copy-start(f32[10,64,128]{2,1,0:T(8,128)} %get-tuple-element.71) | copy-start | bytes 983044
  49.2 2.9 %copy-start.25 = (f32[10,64,128]{2,1,0:T(8,128)S(1)}, f32[10,64,128]{2,1,0:T(8,128)}, u32[]{:S(2)}) copy-start(f32[10,64,128]{2,1,0:T(8,128)} %get-tuple-element.37) | copy-start | bytes 983044
  49.2 2.9 %copy-start.26 = (f32[10,64,128]{2,1,0:T(8,128)S(1)}, f32[10,64,128]{2,1,0:T(8,128)}, u32[]{:S(2)}) copy-start(f32[10,64,128]{2,1,0:T(8,128)} %get-tuple-element.69) | copy-start | bytes 983044
  49.2 2.9 %copy-start.27 = (f32[10,64,128]{2,1,0:T(8,128)S(1)}, f32[10,64,128]{2,1,0:T(8,128)}, u32[]{:S(2)}) copy-start(f32[10,64,128]{2,1,0:T(8,128)} %get-tuple-element.70) | copy-start | bytes 983044
  49.2 2.9 %copy-start.29 = (f32[10,64,128]{2,1,0:T(8,128)S(1)}, f32[10,64,128]{2,1,0:T(8,128)}, u32[]{:S(2)}) copy-start(f32[10,64,128]{2,1,0:T(8,128)} %get-tuple-element.67) | copy-start | bytes 983044
  49.2 2.9 %copy-start.30 = (f32[10,64,128]{2,1,0:T(8,128)S(1)}, f32[10,64,128]{2,1,0:T(8,128)}, u32[]{:S(2)}) copy-start(f32[10,64,128]{2,1,0:T(8,128)} %get-tuple-element.68) | copy-start | bytes 983044
  50.6 1.6 %copy-start.8 = (f32[1,3,8,64,128]{4,3,2,1,0:T(8,128)S(1)}, f32[1,3,8,64,128]{4,3,2,1,0:T(8,128)}, u32[]{:S(2)}) copy-start(f32[1,3,8,64,128]{4,3,2,1,0:T(8,128)} %param.7) | copy-start | bytes 2359300
  50.7 1.6 %copy-start.12 = (f32[8,64,128]{2,1,0:T(8,128)S(1)}, f32[8,64,128]{2,1,0:T(8,128)}, u32[]{:S(2)}) copy-start(f32[8,64,128]{2,1,0:T(8,128)} %copy-done.11) | copy-start | bytes 786436
  50.7 1.6 %copy-start.14 = (f32[8,64,128]{2,1,0:T(8,128)S(1)}, f32[8,64,128]{2,1,0:T(8,128)}, u32[]{:S(2)}) copy-start(f32[8,64,128]{2,1,0:T(8,128)} %copy-done.13) | copy-start | bytes 786436
  50.7 1.7 %copy-start.16 = (f32[8,64,128]{2,1,0:T(8,128)S(1)}, f32[8,64,128]{2,1,0:T(8,128)}, u32[]{:S(2)}) copy-start(f32[8,64,128]{2,1,0:T(8,128)} %copy-done.15) | copy-start | bytes 786436
  50.7 1.7 %copy-start.32 = (f32[8,64,128]{2,1,0:T(8,128)S(1)}, f32[8,64,128]{2,1,0:T(8,128)}, u32[]{:S(2)}) copy-start(f32[8,64,128]{2,1,0:T(8,128)} %param.9) | copy-start | bytes 786436
Sparse Core Ops, SparseCore 0:
  44.2 12.8 reduce-scatter.2
  60.0 11.6 reduce-scatter.4
where the time goes:
time: 78.8 us; the launch traced here: 78.5 us
  waiting for transfers between devices  21.2 us (27%)
  starting transfers between devices  19.1 us (24%)
  between operations  14.6 us (19%)
  local copies, waits for them, and re-layouts  12.1 us (15%)
  other arithmetic  11.5 us (15%)
    ppermute x4, starting transfers between devices, with_halo(): lax.ppermute(lax.slice_in_dim(block, 0, width, axis=dim), axis, backward)  18.8 us
    reduce_scatter x1, waiting for transfers between devices, local(): lax.psum_scatter(bulk_total, 'event', scatter_dimension=1, tiled=True)  14.6 us
    slice x8, local copies, waits for them, and re-layouts, slope_mid(): upper = lax.slice_in_dim(padded, 2, padded.shape[axis], axis=axis)  7.63 us
    reduce_scatter x1, waiting for transfers between devices, local(): lax.psum_scatter(shear_total, 'event', scatter_dimension=1, tiled=True)  3.43 us
    ppermute x4, waiting for transfers between devices, with_halo(): lax.ppermute(lax.slice_in_dim(block, block.shape[dim] - width, None, axis...  3.14 us
    another operation x3, other arithmetic, advance(): accel = jnp.stack(divergence(stress))  2.87 us
    mul x4, other arithmetic, stress_of(): entry = 2.0 * shear_part * strain[first][second]  2.57 us
    unnamed x70, local copies, waits for them, and re-layouts  2.15 us
  transfers between devices with their start and end apart: 10, of which 3 were waited for; matrix products, arithmetic and copies ran while one was open for 24% of the time, Pallas kernels for 0%

commit v1 on v0

v1 whole, which is shorter than its diff:
```python
import jax
import jax.numpy as jnp
from jax import lax
from jax.experimental import pallas as pl
from jax.experimental.pallas import tpu as pltpu
from jax.sharding import PartitionSpec as P

time_step = 0.3
step_squared = time_step * time_step


def difference_tools(rows, lanes):
    row = lax.broadcasted_iota(jnp.int32, (rows, lanes), 0)
    lane = lax.broadcasted_iota(jnp.int32, (rows, lanes), 1)

    def along_rows(values):
        upper = jnp.where(row == rows - 1, 0.0, pltpu.roll(values, rows - 1, 0))
        lower = jnp.where(row == 0, 0.0, pltpu.roll(values, 1, 0))
        return upper - lower

    def along_lanes(values):
        upper = jnp.where(lane == lanes - 1, 0.0, pltpu.roll(values, lanes - 1, 1))
        lower = jnp.where(lane == 0, 0.0, pltpu.roll(values, 1, 1))
        return upper - lower

    return along_rows, along_lanes


def strain_parts(before, middle, after, tools):
    along_rows, along_lanes = tools
    first = after[0] - before[0]
    second = along_rows(middle[1])
    third = along_lanes(middle[2])
    pair_12 = (after[1] - before[1]) + along_rows(middle[0])
    pair_13 = (after[2] - before[2]) + along_lanes(middle[0])
    pair_23 = along_rows(middle[2]) + along_lanes(middle[1])
    return (first, second, third, pair_12, pair_13, pair_23, first + second + third)


def normal_stress(parts, lame, shear):
    return (2.0 * shear * parts[0] + lame * parts[6], shear * parts[3], shear * parts[4])


def cross_force(parts, normal, lame, shear, tools):
    along_rows, along_lanes = tools
    pressure = lame * parts[6]
    twice = 2.0 * shear
    s_22 = twice * parts[1] + pressure
    s_33 = twice * parts[2] + pressure
    s_23 = shear * parts[5]
    return (
        along_rows(normal[1]) + along_lanes(normal[2]),
        along_rows(s_22) + along_lanes(s_23),
        along_rows(s_23) + along_lanes(s_33),
    )


def term_pair(parts, other, lame, shear):
    straight = parts[0] * other[0] + parts[1] * other[1] + parts[2] * other[2]
    mixed = parts[3] * other[3] + parts[4] * other[4] + parts[5] * other[5]
    traces = parts[6] * other[6]
    shear_term = shear * (
        (-0.5 * time_step) * straight - (0.25 * time_step) * mixed + (time_step / 6.0) * traces
    )
    bulk_term = (-0.25 * time_step) * (lame + (2.0 / 3.0) * shear) * traces
    return shear_term, bulk_term


def call(kernel, outs, args, in_spaces, out_spaces, scratch=(), vmem=40 << 20):
    shapes = [
        pltpu.VMEM(shape, jnp.float32) if space is pltpu.VMEM else jax.ShapeDtypeStruct(shape, jnp.float32)
        for shape, space in zip(outs, out_spaces)
    ]
    out_spaces = [space or pltpu.VMEM for space in out_spaces]
    return pl.pallas_call(
        kernel,
        out_shape=shapes,
        in_specs=[pl.BlockSpec(memory_space=space) for space in in_spaces],
        out_specs=[pl.BlockSpec(memory_space=space) for space in out_spaces],
        scratch_shapes=list(scratch),
        compiler_params=pltpu.CompilerParams(vmem_limit_bytes=vmem),
    )(*args)


def local(adjoint_now, adjoint_prev, forward_field, density, lame_first, shear_modulus):
    slabs = lax.axis_size("blk")
    events = lax.axis_size("event")
    cells, rows, lanes = density.shape
    steps = forward_field.shape[1]
    last = cells - 1
    band = rows // events
    plane = (rows, lanes)
    VM, SM, ANY = pltpu.VMEM, pltpu.SMEM, pl.ANY

    odd = lax.rem(lax.axis_index("blk"), 2)
    mine = lax.axis_index("event")
    place = jnp.stack([odd, mine]).astype(jnp.int32)
    near = [(i, i + 1 - 2 * (i % 2)) for i in range(slabs)]
    far = [(i, (i - 1 + 2 * (i % 2)) % slabs) for i in range(slabs)]
    others = [
        [(i, (i + shift) % events) for i in range(events)] for shift in range(1, events)
    ]

    now, prev, forward = adjoint_now[0], adjoint_prev[0], forward_field[0]

    def layer(place_ref, t):
        return t + place_ref[0] * (last - 2 * t)

    def sign(place_ref):
        return (1 - 2 * place_ref[0]).astype(jnp.float32)

    def pack(place_ref, now_ref, forward_ref, lame_ref, shear_ref, near_ref, far_ref, far_fwd_ref, sem):
        copies = []

        def face(t, step, out, fwd_out, fwd_base):
            for slot in range(2):
                copies.append((now_ref.at[:, layer(place_ref, t + slot * step)], out.at[pl.ds(3 * slot, 3)]))
            copies.append((lame_ref.at[layer(place_ref, t)], out.at[6]))
            copies.append((shear_ref.at[layer(place_ref, t)], out.at[7]))
            for k in range(steps):
                copies.append(
                    (forward_ref.at[k, :, layer(place_ref, t)], fwd_out.at[pl.ds(fwd_base + 3 * k, 3)])
                )

        face(0, 1, far_ref, far_fwd_ref, 0)
        face(last, -1, near_ref, near_ref, 8)
        started = [pltpu.make_async_copy(src, dst, sem.at[i]) for i, (src, dst) in enumerate(copies)]
        for copy in started:
            copy.start()
        for copy in started:
            copy.wait()

    near_out, far_out, far_fwd_out = call(
        pack,
        [(8 + 3 * steps, *plane), (8, *plane), (3 * steps, *plane)],
        (place, now, forward, lame_first, shear_modulus),
        [SM, ANY, ANY, ANY, ANY],
        [VM, VM, VM],
        [pltpu.SemaphoreType.DMA((8 + 2 * steps,))],
    )
    near_in = lax.ppermute(near_out, "blk", near)
    far_in = lax.ppermute(far_out, "blk", far)
    far_fwd_in = lax.ppermute(far_fwd_out, "blk", far)

    def first(
        place_ref, now_ref, prev_ref, forward_ref, dens_ref, lame_ref, shear_ref, near_ref,
        now_v, fwd_v, lame_v, shear_v, scale_v, next_v, near_next, terms_v,
        prev_v, dens_v, normal_v, sem,
    ):
        moves = [
            pltpu.make_async_copy(src, dst, sem.at[i])
            for i, (src, dst) in enumerate(
                [(now_ref, now_v), (lame_ref, lame_v), (shear_ref, shear_v), (forward_ref, fwd_v),
                 (prev_ref, prev_v), (dens_ref, dens_v)]
            )
        ]
        for move in moves:
            move.start()
        for move in moves:
            move.wait()
        sigma = sign(place_ref)
        tools = difference_tools(*plane)

        def at(t):
            return layer(place_ref, t)

        def field(t):
            if t <= last:
                return (now_v[0, at(t)] * sigma, now_v[1, at(t)], now_v[2, at(t)])
            base = 3 * (t - cells)
            return (near_ref[base] * sigma, near_ref[base + 1], near_ref[base + 2])

        def fwd(k, t):
            if t <= last:
                return (fwd_v[k, 0, at(t)] * sigma, fwd_v[k, 1, at(t)], fwd_v[k, 2, at(t)])
            base = 8 + 3 * k
            return (near_ref[base] * sigma, near_ref[base + 1], near_ref[base + 2])

        for t in range(cells):
            scale_v[t] = (0.25 * step_squared) / dens_v[at(t)]
        for t in range(1, cells + 1):
            parts = strain_parts(field(t - 1), field(t), field(t + 1), tools)
            if t <= last:
                lame, shear = lame_v[at(t)], shear_v[at(t)]
            else:
                lame, shear = near_ref[6], near_ref[7]
            normal = normal_stress(parts, lame, shear)
            for b in range(3):
                normal_v[b, t] = normal[b]
            if t <= last:
                force = cross_force(parts, normal, lame, shear, tools)
                for b in range(3):
                    next_v[b, t] = force[b]
                other = strain_parts(fwd(0, t - 1), fwd(0, t), fwd(0, t + 1), tools)
                pair = term_pair(parts, other, lame, shear)
                terms_v[0, t] = pair[0]
                terms_v[1, t] = pair[1]
        for t in range(cells):
            for b in range(3):
                force = normal_v[b, t + 1]
                if t > 0:
                    force = force + next_v[b, t]
                if t > 1:
                    force = force - normal_v[b, t - 1]
                old = prev_v[b, at(t)]
                if b == 0:
                    old = old * sigma
                new = 2.0 * field(t)[b] - old + scale_v[t] * force
                next_v[b, t] = new
                if t >= last - 1:
                    near_next[3 * (last - t) + b] = new

    now_v, fwd_v, lame_v, shear_v, scale_v, next_v, near_next, terms_v = call(
        first,
        [now.shape, forward.shape, density.shape, density.shape, density.shape, now.shape,
         (6, *plane), (2, cells, *plane)],
        (place, now, prev, forward, density, lame_first, shear_modulus, near_in),
        [SM] + [ANY] * 6 + [VM],
        [VM] * 8,
        [pltpu.VMEM(now.shape, jnp.float32), pltpu.VMEM(density.shape, jnp.float32),
         pltpu.VMEM((3, cells + 1, *plane), jnp.float32), pltpu.SemaphoreType.DMA((6,))],
    )
    near_next_in = lax.ppermute(near_next, "blk", near)

    def far_first(place_ref, now_v, lame_v, shear_v, scale_v, next_v, far_ref, far_next):
        sigma = sign(place_ref)
        tools = difference_tools(*plane)

        def at(t):
            return layer(place_ref, t)

        def field(t):
            if t >= 0:
                return (now_v[0, at(t)] * sigma, now_v[1, at(t)], now_v[2, at(t)])
            base = 3 * (-1 - t)
            return (far_ref[base] * sigma, far_ref[base + 1], far_ref[base + 2])

        outer = normal_stress(strain_parts(field(-2), field(-1), field(0), tools), far_ref[6], far_ref[7])
        lame, shear = lame_v[at(0)], shear_v[at(0)]
        parts = strain_parts(field(-1), field(0), field(1), tools)
        normal = normal_stress(parts, lame, shear)
        force = cross_force(parts, normal, lame, shear, tools)
        for b in range(3):
            far_next[b] = next_v[b, 0] + scale_v[0] * (force[b] - outer[b])
            far_next[3 + b] = next_v[b, 1] - scale_v[1] * normal[b]

    (far_next,) = call(
        far_first,
        [(6, *plane)],
        (place, now_v, lame_v, shear_v, scale_v, next_v, far_in),
        [SM] + [VM] * 6,
        [VM],
    )
    far_next_in = lax.ppermute(far_next, "blk", far)

    def second(
        place_ref, now_v, fwd_v, lame_v, shear_v, scale_v, next_v, terms_v, far_next_ref, near_next_ref,
        near_ref, far_ref, far_fwd_ref,
        final_v, keep_ref, send_ref, normal_v, total_v,
    ):
        sigma = sign(place_ref)
        tools = difference_tools(*plane)

        def at(t):
            return layer(place_ref, t)

        def start(t):
            if t >= 0:
                return (now_v[0, at(t)] * sigma, now_v[1, at(t)], now_v[2, at(t)])
            return (far_ref[0] * sigma, far_ref[1], far_ref[2])

        def field(t):
            if t < 2:
                return tuple(far_next_ref[3 * t + b] for b in range(3))
            if t <= last:
                return tuple(next_v[b, t] for b in range(3))
            base = 3 * (t - cells)
            return (-near_next_ref[base], near_next_ref[base + 1], near_next_ref[base + 2])

        def fwd(k, t):
            if t < 0:
                return (far_fwd_ref[3 * k] * sigma, far_fwd_ref[3 * k + 1], far_fwd_ref[3 * k + 2])
            if t <= last:
                return (fwd_v[k, 0, at(t)] * sigma, fwd_v[k, 1, at(t)], fwd_v[k, 2, at(t)])
            base = 8 + 3 * k
            return (near_ref[base] * sigma, near_ref[base + 1], near_ref[base + 2])

        for t in range(1, cells + 1):
            parts = strain_parts(field(t - 1), field(t), field(t + 1), tools)
            if t <= last:
                lame, shear = lame_v[at(t)], shear_v[at(t)]
            else:
                lame, shear = near_ref[6], near_ref[7]
            normal = normal_stress(parts, lame, shear)
            for b in range(3):
                normal_v[b, t] = normal[b]
            if t <= last:
                force = cross_force(parts, normal, lame, shear, tools)
                for b in range(3):
                    final_v[b, t] = force[b]
                other = strain_parts(fwd(1, t - 1), fwd(1, t), fwd(1, t + 1), tools)
                pair = term_pair(parts, other, lame, shear)
                for k in range(2):
                    total_v[k, t] = terms_v[k, t] + pair[k]
        for t in range(cells):
            for b in range(3):
                force = normal_v[b, t + 1]
                if t > 0:
                    force = force + final_v[b, t]
                if t > 1:
                    force = force - normal_v[b, t - 1]
                old = now_v[b, at(t)]
                if b == 0:
                    old = old * sigma
                final_v[b, t] = 2.0 * field(t)[b] - old + scale_v[t] * force
        parts = strain_parts(start(-1), start(0), start(1), tools)
        other = strain_parts(fwd(0, -1), fwd(0, 0), fwd(0, 1), tools)
        pair = term_pair(parts, other, lame_v[at(0)], shear_v[at(0)])
        for k in range(2):
            total_v[k, 0] = pair[k]
        own = place_ref[1]
        keep_ref[...] = total_v[:, :, pl.ds(pl.multiple_of(own * band, 8), band)]
        for shift in range(1, events):
            target = lax.rem(own + shift, events)
            send_ref[shift - 1] = total_v[:, :, pl.ds(pl.multiple_of(target * band, 8), band)]

    final_v, keep, send = call(
        second,
        [now.shape, (2, cells, band, lanes), (events - 1, 2, cells, band, lanes)],
        (place, now_v, fwd_v, lame_v, shear_v, scale_v, next_v, terms_v, far_next, near_next_in,
         near_in, far_in, far_fwd_in),
        [SM] + [VM] * 12,
        [VM] * 3,
        [pltpu.VMEM((3, cells + 1, *plane), jnp.float32), pltpu.VMEM((2, cells, *plane), jnp.float32)],
    )
    shared = [lax.ppermute(send[i], "event", others[i]) for i in range(events - 1)]

    def far_second(
        place_ref, now_v, fwd_v, lame_v, shear_v, scale_v, final_v, far_next_ref, next_v, far_ref, far_fwd_ref,
        far_next_in_ref,
        out_ref, keep_ref, send_ref, total_v,
    ):
        sigma = sign(place_ref)
        tools = difference_tools(*plane)

        def at(t):
            return layer(place_ref, t)

        def field(t):
            if t < 0:
                base = 3 * (-1 - t)
                return (-far_next_in_ref[base], far_next_in_ref[base + 1], far_next_in_ref[base + 2])
            return tuple(far_next_ref[3 * t + b] for b in range(3))

        def fwd(k, t):
            if t < 0:
                return (far_fwd_ref[3 * k] * sigma, far_fwd_ref[3 * k + 1], far_fwd_ref[3 * k + 2])
            return (fwd_v[k, 0, at(t)] * sigma, fwd_v[k, 1, at(t)], fwd_v[k, 2, at(t)])

        outer = normal_stress(strain_parts(field(-2), field(-1), field(0), tools), far_ref[6], far_ref[7])
        lame, shear = lame_v[at(0)], shear_v[at(0)]
        parts = strain_parts(field(-1), field(0), field(1), tools)
        normal = normal_stress(parts, lame, shear)
        force = cross_force(parts, normal, lame, shear, tools)
        other = strain_parts(fwd(1, -1), fwd(1, 0), fwd(1, 1), tools)
        pair = term_pair(parts, other, lame, shear)
        for k in range(2):
            total_v[k] = pair[k]
        own = place_ref[1]
        keep_ref[...] = total_v[:, pl.ds(pl.multiple_of(own * band, 8), band)]
        for shift in range(1, events):
            target = lax.rem(own + shift, events)
            send_ref[shift - 1] = total_v[:, pl.ds(pl.multiple_of(target * band, 8), band)]
        for t in range(cells):
            for b in range(3):
                value = final_v[b, t]
                if t == 0:
                    value = value + scale_v[0] * (force[b] - outer[b])
                if t == 1:
                    value = value - scale_v[1] * normal[b]
                if b == 0:
                    value = value * sigma
                out_ref[b, at(t)] = value

    result, far_keep, far_send = call(
        far_second,
        [now.shape, (2, band, lanes), (events - 1, 2, band, lanes)],
        (place, now_v, fwd_v, lame_v, shear_v, scale_v, final_v, far_next, next_v, far_in, far_fwd_in,
         far_next_in),
        [SM] + [VM] * 11,
        [None, VM, VM],
        [pltpu.VMEM((2, *plane), jnp.float32)],
    )
    far_shared = [lax.ppermute(far_send[i], "event", others[i]) for i in range(events - 1)]

    def finish(place_ref, keep_ref, far_keep_ref, *rest):
        parts = rest[: 2 * (events - 1)]
        outs = rest[2 * (events - 1) :]
        for k in range(2):
            for t in range(cells):
                value = keep_ref[k, t]
                for i in range(events - 1):
                    value = value + parts[i][k, t]
                if t == 0:
                    value = value + far_keep_ref[k]
                    for i in range(events - 1):
                        value = value + parts[events - 1 + i][k]
                outs[k][layer(place_ref, t)] = value

    band_shear, band_bulk = call(
        finish,
        [(cells, band, lanes)] * 2,
        (place, keep, far_keep, *shared, *far_shared),
        [SM] + [VM] * (2 + 2 * (events - 1)),
        [None] * 2,
    )
    return (result[None], band_shear, band_bulk)


def solution(mesh):
    in_specs = (
        P("event", None, "blk", None, None),
        P("event", None, "blk", None, None),
        P("event", None, None, "blk", None, None),
        P("blk", None, None),
        P("blk", None, None),
        P("blk", None, None),
    )
    out_specs = (
        P("event", None, "blk", None, None),
        P("blk", "event", None),
        P("blk", "event", None),
    )
    return jax.shard_map(local, mesh=mesh, in_specs=in_specs, out_specs=out_specs, check_vma=False)
```

time: 78.8 us -> 39.5 us (0.50)
  between operations: 14.6 us -> 0.69 us
  other arithmetic: 11.5 us -> 0.08 us
  Pallas kernels: 0 us -> 10.2 us
  starting transfers between devices: 19.1 us -> 10.8 us
  waiting for transfers between devices: 21.2 us -> 13 us
  local copies, waits for them, and re-layouts: 12.1 us -> 4.45 us
    reduce_scatter x2 -> x0, waiting for transfers between devices: 18 us -> none  [the longest x1 14.6 us: local(): lax.psum_scatter(bulk_total, 'event', scatter_dimension=1, tiled=True)]
    pallas_call x0 -> x6, Pallas kernels: none -> 10.2 us  [call(): pl.pallas_call(kernel, out_shape=shapes, in_specs=[pl.BlockSpec(memory_sp...]
    slice x12 -> x0, local copies, waits for them, and re-layouts: 9.92 us -> none  [the longest x8 7.63 us: slope_mid(): upper = lax.slice_in_dim(padded, 2, padded.shape[axis], axis=axis)]
    ppermute x8 -> x7, waiting for transfers between devices: 3.15 us -> 13 us  [the longest x1 5.33 us: local(): far_next_in = lax.ppermute(far_next, 'blk', far)]
    ppermute x8 -> x7, starting transfers between devices: 19 us -> 10.8 us  [the longest x1 5.67 us: local(): far_in = lax.ppermute(far_out, 'blk', far)]
    add x7 -> x0, other arithmetic: 4.97 us -> none  [the longest x1 1.98 us: local(): shear_total = shear_total + terms[0]]
    another operation x3 -> x1, other arithmetic: 2.87 us -> 0.08 us  [local(): place = jnp.stack([odd, mine]).astype(jnp.int32)]
    mul x4 -> x0, other arithmetic: 2.57 us -> none  [stress_of(): entry = 2.0 * shear_part * strain[first][second]]
  transfers between devices with their start and end apart: 10 -> 7, of which waited for: 3 -> 4; matrix products, arithmetic and copies ran while one was open for 24% -> 0% of each run, Pallas kernels for 0% -> 13%
where the time goes in v1:
time: 39.5 us; the launch traced here: 39.3 us
  waiting for transfers between devices  13 us (33%)
  starting transfers between devices  10.8 us (27%)
  Pallas kernels  10.2 us (26%)
  local copies, waits for them, and re-layouts  4.45 us (11%)
  between operations  0.69 us (2%)
    pallas_call x6, Pallas kernels, call(): pl.pallas_call(kernel, out_shape=shapes, in_specs=[pl.BlockSpec(memory_sp...  10.2 us
    ppermute x1, starting transfers between devices, local(): far_in = lax.ppermute(far_out, 'blk', far)  5.67 us
    ppermute x1, waiting for transfers between devices, local(): far_next_in = lax.ppermute(far_next, 'blk', far)  5.33 us
    unnamed x12, local copies, waits for them, and re-layouts  4.45 us
    ppermute x1, waiting for transfers between devices, local(): lax.ppermute(far_send[i], 'event', others[i])  3.43 us
    ppermute x1, waiting for transfers between devices, local(): far_fwd_in = lax.ppermute(far_fwd_out, 'blk', far)  2.92 us
    ppermute x1, starting transfers between devices, local(): far_next_in = lax.ppermute(far_next, 'blk', far)  2.53 us
    ppermute x1, starting transfers between devices, local(): lax.ppermute(send[i], 'event', others[i])  1.54 us
  transfers between devices with their start and end apart: 7, of which 4 were waited for; matrix products, arithmetic and copies ran while one was open for 0% of the time, Pallas kernels for 13%

profile of v1, /device:TPU:0, one launch (start us, length us, event | category | flops | bytes accessed | tf_op | source)
XLA Modules:
  0.0 39.3 jit_solution(3202140292924762255)
XLA Ops:
  0.6 0.1 pad_add_fusion.place_ref
  0.7 0.0 copy-start
  0.7 1.4 %copy-done = f32[1,2,3,8,64,128]{5,4,3,2,1,0:T(8,128)S(1)} copy-done((f32[1,2,3,8,64,128]{5,4,3,2,1,0:T(8,128)S(1)}, f32[1,2,3,8,64,128]{5,4,3,2,1,0:T(8,128)}, u32[]{:S(2)}) %copy-start) | copy-done | bytes 1572888
  2.1 0.0 copy-start.1
  2.1 1.1 %copy-done.1 = f32[1,3,8,64,128]{4,3,2,1,0:T(8,128)S(1)} copy-done((f32[1,3,8,64,128]{4,3,2,1,0:T(8,128)S(1)}, f32[1,3,8,64,128]{4,3,2,1,0:T(8,128)}, u32[]{:S(2)}) %copy-start.1) | copy-done | bytes 786456
  3.3 0.0 copy-start.2
  3.3 0.9 %copy-done.2 = f32[8,64,128]{2,1,0:T(8,128)S(1)} copy-done((f32[8,64,128]{2,1,0:T(8,128)S(1)}, f32[8,64,128]{2,1,0:T(8,128)}, u32[]{:S(2)}) %copy-start.2) | copy-done | bytes 262168
  4.2 0.0 copy-start.3
  4.2 0.9 %copy-done.3 = f32[8,64,128]{2,1,0:T(8,128)S(1)} copy-done((f32[8,64,128]{2,1,0:T(8,128)S(1)}, f32[8,64,128]{2,1,0:T(8,128)}, u32[]{:S(2)}) %copy-start.3) | copy-done | bytes 262168
  5.2 0.0 copy-start.4
  5.2 0.0 copy-start.5
  5.2 1.2 %shard_map.85 = (f32[14,64,128]{2,1,0:T(8,128)S(1)}, f32[8,64,128]{2,1,0:T(8,128)S(1)}, f32[6,64,128]{2,1,0:T(8,128)S(1)}) custom-call(s32[2]{0:T(128)S(1)} %pad_add_fusion.place_ref, f32[3,8,64,128]{3,2,1,0:T(8,128)S(1)} %bitcast.10, f32[2,3,8,64,128]{4,3,2,1,0:T(8,128)S(1)} %bitcast.8, f32[8,64,128]{2,1,0:T(8,128)S(1)} %copy-done.2, ...), custom_call_target="tpu_custom_call" | custom-call | tf_op jit(solution)/shard_map/pallas_call | solution.py:75
  6.3 0.5 %collective-permute-start = (f32[14,64,128]{2,1,0:T(8,128)S(1)}, f32[14,64,128]{2,1,0:T(8,128)S(1)}, u32[]{:S(2)}, u32[]{:S(2)}) collective-permute-start(f32[14,64,128]{2,1,0:T(8,128)S(1)} %get-tuple-element.22), channel_id=1, source_target_pairs={{0,2},{2,0},{4,6},{6,4},{8,10},{10,8},{12,14},{14,12},{16,18},{18,... | collective-permute-start | bytes 1376264 | tf_op jit(solution)/shard_map/ppermute | solution.py:141
  6.9 5.7 %collective-permute-start.1 = (f32[8,64,128]{2,1,0:T(8,128)S(1)}, f32[8,64,128]{2,1,0:T(8,128)S(1)}, u32[]{:S(2)}, u32[]{:S(2)}) collective-permute-start(f32[8,64,128]{2,1,0:T(8,128)S(1)} %get-tuple-element.30), channel_id=1, source_target_pairs={{0,30},{2,4},{4,2},{6,8},{8,6},{10,12},{12,10},{14,16},{16,14},{18... | collective-permute-start | bytes 786440 | tf_op jit(solution)/shard_map/ppermute | solution.py:142
  12.5 0.0 collective-permute-start.3
  12.6 0.0 collective-permute-done.near_ref
  12.6 0.0 copy-done.4
  12.6 0.0 copy-done.5
  12.6 2.7 %shard_map.86 = (f32[3,8,64,128]{3,2,1,0:T(8,128)S(1)}, f32[2,3,8,64,128]{4,3,2,1,0:T(8,128)S(1)}, f32[8,64,128]{2,1,0:T(8,128)S(1)}, f32[8,64,128]{2,1,0:T(8,12...) custom-call(s32[2]{0:T(128)S(1)} %pad_add_fusion.place_ref, ...), custom_call_target="tpu_custom_call" | custom-call | tf_op jit(solution)/shard_map/pallas_call | solution.py:75
  15.3 0.1 collective-permute-start.2
  15.3 1.3 %collective-permute-done.1.far_ref = f32[8,64,128]{2,1,0:T(8,128)S(1)} collective-permute-done((f32[8,64,128]{2,1,0:T(8,128)S(1)}, f32[8,64,128]{2,1,0:T(8,128)S(1)}, u32[]{:S(2)}, u32[]{:S(2)}) %collective-permute-start.1) | collective-permute-done | bytes 262176 | tf_op jit(solution)/shard_map/ppermute | solution.py:142
  16.7 0.8 %shard_map.87.far_next_ref = f32[6,64,128]{2,1,0:T(8,128)S(1)} custom-call(s32[2]{0:T(128)S(1)} %pad_add_fusion.place_ref, f32[3,8,64,128]{3,2,1,0:T(8,128)S(1)} %get-tuple-element.23.now_v, f32[8,64,128]{2,1,0:T(8,128)S(1)} %get-tuple-element.25.lame_v, f32[8,64,128]{2,1,0:T(8,128)S(1)} %get-tuple-element.26.shear_v, ...), custom_call_target="tpu_custom_call" | custom-call | tf_op jit(solution)/shard_map/pallas_call | solution.py:75
  17.5 2.9 %collective-permute-done.3.far_fwd_ref = f32[6,64,128]{2,1,0:T(8,128)S(1)} collective-permute-done((f32[6,64,128]{2,1,0:T(8,128)S(1)}, f32[6,64,128]{2,1,0:T(8,128)S(1)}, u32[]{:S(2)}, u32[]{:S(2)}) %collective-permute-start.3) | collective-permute-done | bytes 196640 | tf_op jit(solution)/shard_map/ppermute | solution.py:143
  20.4 0.0 collective-permute-done.2.near_next_ref
  20.4 2.5 %shard_map.88 = (f32[3,8,64,128]{3,2,1,0:T(8,128)S(1)}, f32[2,8,32,128]{3,2,1,0:T(8,128)S(1)}, f32[1,2,8,32,128]{4,3,2,1,0:T(8,128)S(1)}) custom-call(s32[2]{0:T(128)S(1)} %pad_add_fusion.place_ref, f32[3,8,64,128]{3,2,1,0:T(8,128)S(1)} %get-tuple-element.23.now_v, f32[2,3,8,64,128]{4,3,2,1,0:T(8,128)S(1)} %get-tuple-element.24.fwd_v, ...), custom_call_target="tpu_custom_call" | custom-call | tf_op jit(solution)/shard_map/pallas_call | solution.py:75
  22.9 1.5 %collective-permute-start.5 = (f32[2,8,32,128]{3,2,1,0:T(8,128)S(1)}, f32[2,8,32,128]{3,2,1,0:T(8,128)S(1)}, u32[]{:S(2)}, u32[]{:S(2)}) collective-permute-start(f32[2,8,32,128]{3,2,1,0:T(8,128)S(1)} %bitcast.13), channel_id=1, source_target_pairs={{0,1},{1,0},{2,3},{3,2},{4,5},{5,4},{6,7},{7,6},{8,9},{9,8},{10,11... | collective-permute-start | bytes 786440 | tf_op jit(solution)/shard_map/ppermute | solution.py:336
  24.5 2.5 %collective-permute-start.4 = (f32[6,64,128]{2,1,0:T(8,128)S(1)}, f32[6,64,128]{2,1,0:T(8,128)S(1)}, u32[]{:S(2)}, u32[]{:S(2)}) collective-permute-start(f32[6,64,128]{2,1,0:T(8,128)S(1)} %shard_map.87.far_next_ref), channel_id=1, source_target_pairs={{0,30},{2,4},{4,2},{6,8},{8,6},{10,12},{12,10},{14,16},{16,14},{18... | collective-permute-start | bytes 589832 | tf_op jit(solution)/shard_map/ppermute | solution.py:254
  27.0 5.3 %collective-permute-done.4.far_next_in_ref = f32[6,64,128]{2,1,0:T(8,128)S(1)} collective-permute-done((f32[6,64,128]{2,1,0:T(8,128)S(1)}, f32[6,64,128]{2,1,0:T(8,128)S(1)}, u32[]{:S(2)}, u32[]{:S(2)}) %collective-permute-start.4) | collective-permute-done | bytes 196640 | tf_op jit(solution)/shard_map/ppermute | solution.py:254
  32.3 1.8 %shard_map.89 = (f32[3,8,64,128]{3,2,1,0:T(8,128)}, f32[2,32,128]{2,1,0:T(8,128)S(1)}, f32[1,2,32,128]{3,2,1,0:T(8,128)S(1)}) custom-call(s32[2]{0:T(128)S(1)} %pad_add_fusion.place_ref, f32[3,8,64,128]{3,2,1,0:T(8,128)S(1)} %get-tuple-element.23.now_v, f32[2,3,8,64,128]{4,3,2,1,0:T(8,128)S(1)} %get-tuple-element.24.fwd_v, ...), custom_call_target="tpu_custom_call" | custom-call | tf_op jit(solution)/shard_map/pallas_call | solution.py:75
  34.1 0.5 %collective-permute-start.6 = (f32[2,32,128]{2,1,0:T(8,128)S(1)}, f32[2,32,128]{2,1,0:T(8,128)S(1)}, u32[]{:S(2)}, u32[]{:S(2)}) collective-permute-start(f32[2,32,128]{2,1,0:T(8,128)S(1)} %bitcast.14), channel_id=1, source_target_pairs={{0,1},{1,0},{2,3},{3,2},{4,5},{5,4},{6,7},{7,6},{8,9},{9,8},{10,11... | collective-permute-start | bytes 98312 | tf_op jit(solution)/shard_map/ppermute | solution.py:394
  34.6 3.4 %collective-permute-done.6.rest_1_ = f32[2,32,128]{2,1,0:T(8,128)S(1)} collective-permute-done((f32[2,32,128]{2,1,0:T(8,128)S(1)}, f32[2,32,128]{2,1,0:T(8,128)S(1)}, u32[]{:S(2)}, u32[]{:S(2)}) %collective-permute-start.6) | collective-permute-done | bytes 32800 | tf_op jit(solution)/shard_map/ppermute | solution.py:394
  38.0 0.0 collective-permute-done.5.rest_0_
  38.0 1.3 %shard_map.90 = (f32[8,32,128]{2,1,0:T(8,128)}, f32[8,32,128]{2,1,0:T(8,128)}) custom-call(s32[2]{0:T(128)S(1)} %pad_add_fusion.place_ref, f32[2,8,32,128]{3,2,1,0:T(8,128)S(1)} %get-tuple-element.35.keep_ref, f32[2,32,128]{2,1,0:T(8,128)S(1)} %get-tuple-element.36.far_keep_ref, f32[2,8,32,128]{3,2,1,0:T(8,128)S(1)} %collective-permute-done.5.rest_0_, ...), custom_call_target="tpu_custom_call" | custom-call | tf_op jit(solution)/shard_map/pallas_call | solution.py:75
Async XLA Ops:
  0.7 1.4 %copy-start = (f32[1,2,3,8,64,128]{5,4,3,2,1,0:T(8,128)S(1)}, f32[1,2,3,8,64,128]{5,4,3,2,1,0:T(8,128)}, u32[]{:S(2)}) copy-start(f32[1,2,3,8,64,128]{5,4,3,2,1,0:T(8,128)} %param.8) | copy-start | bytes 4718596
  2.1 1.1 %copy-start.1 = (f32[1,3,8,64,128]{4,3,2,1,0:T(8,128)S(1)}, f32[1,3,8,64,128]{4,3,2,1,0:T(8,128)}, u32[]{:S(2)}) copy-start(f32[1,3,8,64,128]{4,3,2,1,0:T(8,128)} %param.6) | copy-start | bytes 2359300
  3.3 0.9 %copy-start.2 = (f32[8,64,128]{2,1,0:T(8,128)S(1)}, f32[8,64,128]{2,1,0:T(8,128)}, u32[]{:S(2)}) copy-start(f32[8,64,128]{2,1,0:T(8,128)} %lame_ref.3) | copy-start | bytes 786436
  4.2 0.9 %copy-start.3 = (f32[8,64,128]{2,1,0:T(8,128)S(1)}, f32[8,64,128]{2,1,0:T(8,128)}, u32[]{:S(2)}) copy-start(f32[8,64,128]{2,1,0:T(8,128)} %shear_ref.3) | copy-start | bytes 786436
  5.2 7.4 %copy-start.4 = (f32[1,3,8,64,128]{4,3,2,1,0:T(8,128)S(1)}, f32[1,3,8,64,128]{4,3,2,1,0:T(8,128)}, u32[]{:S(2)}) copy-start(f32[1,3,8,64,128]{4,3,2,1,0:T(8,128)} %param.7) | copy-start | bytes 2359300
  5.2 7.4 %copy-start.5 = (f32[8,64,128]{2,1,0:T(8,128)S(1)}, f32[8,64,128]{2,1,0:T(8,128)}, u32[]{:S(2)}) copy-start(f32[8,64,128]{2,1,0:T(8,128)} %dens_ref.1) | copy-start | bytes 786436
  6.3 6.2 %collective-permute-start = (f32[14,64,128]{2,1,0:T(8,128)S(1)}, f32[14,64,128]{2,1,0:T(8,128)S(1)}, u32[]{:S(2)}, u32[]{:S(2)}) collective-permute-start(f32[14,64,128]{2,1,0:T(8,128)S(1)} %get-tuple-element.22), channel_id=1, source_target_pairs={{0,2},{2,0},{4,6},{6,4},{8,10},{10,8},{12,14},{14,12},{16,18},{18,... | collective-permute-start | bytes 1376264 | tf_op jit(solution)/shard_map/ppermute | solution.py:141
  6.9 9.8 %collective-permute-start.1 = (f32[8,64,128]{2,1,0:T(8,128)S(1)}, f32[8,64,128]{2,1,0:T(8,128)S(1)}, u32[]{:S(2)}, u32[]{:S(2)}) collective-permute-start(f32[8,64,128]{2,1,0:T(8,128)S(1)} %get-tuple-element.30), channel_id=1, source_target_pairs={{0,30},{2,4},{4,2},{6,8},{8,6},{10,12},{12,10},{14,16},{16,14},{18... | collective-permute-start | bytes 786440 | tf_op jit(solution)/shard_map/ppermute | solution.py:142
  12.5 7.9 %collective-permute-start.3 = (f32[6,64,128]{2,1,0:T(8,128)S(1)}, f32[6,64,128]{2,1,0:T(8,128)S(1)}, u32[]{:S(2)}, u32[]{:S(2)}) collective-permute-start(f32[6,64,128]{2,1,0:T(8,128)S(1)} %get-tuple-element.32), channel_id=1, source_target_pairs={{0,30},{2,4},{4,2},{6,8},{8,6},{10,12},{12,10},{14,16},{16,14},{18... | collective-permute-start | bytes 589832 | tf_op jit(solution)/shard_map/ppermute | solution.py:143
  15.3 5.2 %collective-permute-start.2 = (f32[6,64,128]{2,1,0:T(8,128)S(1)}, f32[6,64,128]{2,1,0:T(8,128)S(1)}, u32[]{:S(2)}, u32[]{:S(2)}) collective-permute-start(f32[6,64,128]{2,1,0:T(8,128)S(1)} %get-tuple-element.31), channel_id=1, source_target_pairs={{0,2},{2,0},{4,6},{6,4},{8,10},{10,8},{12,14},{14,12},{16,18},{18,... | collective-permute-start | bytes 589832 | tf_op jit(solution)/shard_map/ppermute | solution.py:223
  22.9 15.1 %collective-permute-start.5 = (f32[2,8,32,128]{3,2,1,0:T(8,128)S(1)}, f32[2,8,32,128]{3,2,1,0:T(8,128)S(1)}, u32[]{:S(2)}, u32[]{:S(2)}) collective-permute-start(f32[2,8,32,128]{3,2,1,0:T(8,128)S(1)} %bitcast.13), channel_id=1, source_target_pairs={{0,1},{1,0},{2,3},{3,2},{4,5},{5,4},{6,7},{7,6},{8,9},{9,8},{10,11... | collective-permute-start | bytes 786440 | tf_op jit(solution)/shard_map/ppermute | solution.py:336
  24.5 7.9 %collective-permute-start.4 = (f32[6,64,128]{2,1,0:T(8,128)S(1)}, f32[6,64,128]{2,1,0:T(8,128)S(1)}, u32[]{:S(2)}, u32[]{:S(2)}) collective-permute-start(f32[6,64,128]{2,1,0:T(8,128)S(1)} %shard_map.87.far_next_ref), channel_id=1, source_target_pairs={{0,30},{2,4},{4,2},{6,8},{8,6},{10,12},{12,10},{14,16},{16,14},{18... | collective-permute-start | bytes 589832 | tf_op jit(solution)/shard_map/ppermute | solution.py:254
  34.1 3.9 %collective-permute-start.6 = (f32[2,32,128]{2,1,0:T(8,128)S(1)}, f32[2,32,128]{2,1,0:T(8,128)S(1)}, u32[]{:S(2)}, u32[]{:S(2)}) collective-permute-start(f32[2,32,128]{2,1,0:T(8,128)S(1)} %bitcast.14), channel_id=1, source_target_pairs={{0,1},{1,0},{2,3},{3,2},{4,5},{5,4},{6,7},{7,6},{8,9},{9,8},{10,11... | collective-permute-start | bytes 98312 | tf_op jit(solution)/shard_map/ppermute | solution.py:394

commit v2 on v1

--- a/solution.py
+++ b/solution.py
@@ -101,7 +101,11 @@
         [(i, (i + shift) % events) for i in range(events)] for shift in range(1, events)
     ]
 
-    now, prev, forward = adjoint_now[0], adjoint_prev[0], forward_field[0]
+    in_hbm = [
+        pltpu.with_memory_space_constraint(x, pltpu.HBM)
+        for x in (adjoint_now[0], adjoint_prev[0], forward_field[0], density, lame_first, shear_modulus)
+    ]
+    now, prev, forward, density, lame_first, shear_modulus = in_hbm
 
     def layer(place_ref, t):
         return t + place_ref[0] * (last - 2 * t)
@@ -142,9 +146,19 @@
     far_in = lax.ppermute(far_out, "blk", far)
     far_fwd_in = lax.ppermute(far_fwd_out, "blk", far)
 
+    def split(place_ref, terms_ref, layers, keep_ref, send_ref):
+        own = place_ref[1]
+        for shift in range(events):
+            target = lax.rem(own + shift, events) if shift else own
+            start = pl.multiple_of(target * band, 8)
+            out = send_ref.at[shift - 1] if shift else keep_ref
+            for k in range(2):
+                for i, t in enumerate(layers):
+                    out[k, i] = terms_ref[k, t, pl.ds(start, band)]
+
     def first(
         place_ref, now_ref, prev_ref, forward_ref, dens_ref, lame_ref, shear_ref, near_ref,
-        now_v, fwd_v, lame_v, shear_v, scale_v, next_v, near_next, terms_v,
+        now_v, fwd_v, lame_v, shear_v, scale_v, next_v, near_next, terms_v, keep_ref, send_ref,
         prev_v, dens_v, normal_v, sem,
     ):
         moves = [
@@ -209,18 +223,30 @@
                 next_v[b, t] = new
                 if t >= last - 1:
                     near_next[3 * (last - t) + b] = new
-
-    now_v, fwd_v, lame_v, shear_v, scale_v, next_v, near_next, terms_v = call(
+        for t in early:
+            lame, shear = lame_v[at(t)], shear_v[at(t)]
+            fields = [tuple(next_v[b, t + d] for b in range(3)) for d in (-1, 0, 1)]
+            parts = strain_parts(*fields, tools)
+            other = strain_parts(fwd(1, t - 1), fwd(1, t), fwd(1, t + 1), tools)
+            pair = term_pair(parts, other, lame, shear)
+            for k in range(2):
+                terms_v[k, t] = terms_v[k, t] + pair[k]
+        split(place_ref, terms_v, early, keep_ref, send_ref)
+
+    early = list(range(3, last))
+    middle = [1, 2, last]
+    now_v, fwd_v, lame_v, shear_v, scale_v, next_v, near_next, terms_v, keep, send = call(
         first,
         [now.shape, forward.shape, density.shape, density.shape, density.shape, now.shape,
-         (6, *plane), (2, cells, *plane)],
+         (6, *plane), (2, cells, *plane), (2, len(early), band, lanes), (events - 1, 2, len(early), band, lanes)],
         (place, now, prev, forward, density, lame_first, shear_modulus, near_in),
         [SM] + [ANY] * 6 + [VM],
-        [VM] * 8,
+        [VM] * 10,
         [pltpu.VMEM(now.shape, jnp.float32), pltpu.VMEM(density.shape, jnp.float32),
          pltpu.VMEM((3, cells + 1, *plane), jnp.float32), pltpu.SemaphoreType.DMA((6,))],
     )
     near_next_in = lax.ppermute(near_next, "blk", near)
+    shared = [lax.ppermute(send[i], "event", others[i]) for i in range(events - 1)]
 
     def far_first(place_ref, now_v, lame_v, shear_v, scale_v, next_v, far_ref, far_next):
         sigma = sign(place_ref)
@@ -256,7 +282,7 @@
     def second(
         place_ref, now_v, fwd_v, lame_v, shear_v, scale_v, next_v, terms_v, far_next_ref, near_next_ref,
         near_ref, far_ref, far_fwd_ref,
-        final_v, keep_ref, send_ref, normal_v, total_v,
+        final_v, total_v, slope_v, keep_ref, send_ref, normal_v,
     ):
         sigma = sign(place_ref)
         tools = difference_tools(*plane)
@@ -298,10 +324,11 @@
                 force = cross_force(parts, normal, lame, shear, tools)
                 for b in range(3):
                     final_v[b, t] = force[b]
-                other = strain_parts(fwd(1, t - 1), fwd(1, t), fwd(1, t + 1), tools)
-                pair = term_pair(parts, other, lame, shear)
-                for k in range(2):
-                    total_v[k, t] = terms_v[k, t] + pair[k]
+                if t in middle:
+                    other = strain_parts(fwd(1, t - 1), fwd(1, t), fwd(1, t + 1), tools)
+                    pair = term_pair(parts, other, lame, shear)
+                    for k in range(2):
+                        total_v[k, t] = terms_v[k, t] + pair[k]
         for t in range(cells):
             for b in range(3):
                 force = normal_v[b, t + 1]
@@ -313,32 +340,55 @@
                 if b == 0:
                     old = old * sigma
                 final_v[b, t] = 2.0 * field(t)[b] - old + scale_v[t] * force
+        split(place_ref, total_v, middle, keep_ref, send_ref)
         parts = strain_parts(start(-1), start(0), start(1), tools)
         other = strain_parts(fwd(0, -1), fwd(0, 0), fwd(0, 1), tools)
-        pair = term_pair(parts, other, lame_v[at(0)], shear_v[at(0)])
+        lame, shear = lame_v[at(0)], shear_v[at(0)]
+        pair = term_pair(parts, other, lame, shear)
+        empty = jnp.zeros(plane, jnp.float32)
+        parts = strain_parts((empty, empty, empty), field(0), field(1), tools)
+        other = strain_parts(fwd(1, -1), fwd(1, 0), fwd(1, 1), tools)
+        rest = term_pair(parts, other, lame, shear)
         for k in range(2):
-            total_v[k, 0] = pair[k]
-        own = place_ref[1]
-        keep_ref[...] = total_v[:, :, pl.ds(pl.multiple_of(own * band, 8), band)]
-        for shift in range(1, events):
-            target = lax.rem(own + shift, events)
-            send_ref[shift - 1] = total_v[:, :, pl.ds(pl.multiple_of(target * band, 8), band)]
-
-    final_v, keep, send = call(
+            total_v[k, 0] = pair[k] + rest[k]
+        slope_v[0] = shear * ((0.5 * time_step) * other[0] - (time_step / 6.0) * other[6])
+        slope_v[1] = (0.25 * time_step) * shear * other[3]
+        slope_v[2] = (0.25 * time_step) * shear * other[4]
+        slope_v[3] = (0.25 * time_step) * (lame + (2.0 / 3.0) * shear) * other[6]
+
+    final_v, total_v, slope_v, keep_mid, send_mid = call(
         second,
-        [now.shape, (2, cells, band, lanes), (events - 1, 2, cells, band, lanes)],
+        [now.shape, (2, cells, *plane), (4, *plane),
+         (2, len(middle), band, lanes), (events - 1, 2, len(middle), band, lanes)],
         (place, now_v, fwd_v, lame_v, shear_v, scale_v, next_v, terms_v, far_next, near_next_in,
          near_in, far_in, far_fwd_in),
         [SM] + [VM] * 12,
-        [VM] * 3,
-        [pltpu.VMEM((3, cells + 1, *plane), jnp.float32), pltpu.VMEM((2, cells, *plane), jnp.float32)],
-    )
-    shared = [lax.ppermute(send[i], "event", others[i]) for i in range(events - 1)]
+        [VM] * 5,
+        [pltpu.VMEM((3, cells + 1, *plane), jnp.float32)],
+    )
+    shared_mid = [lax.ppermute(send_mid[i], "event", others[i]) for i in range(events - 1)]
+
+    def far_terms(place_ref, total_ref, slope_ref, far_next_in_ref, keep_ref, send_ref, total_v):
+        outer = (-far_next_in_ref[0], far_next_in_ref[1], far_next_in_ref[2])
+        shear_part = total_ref[0, 0]
+        for b in range(3):
+            shear_part = shear_part + slope_ref[b] * outer[b]
+        total_v[0, 0] = shear_part
+        total_v[1, 0] = total_ref[1, 0] + slope_ref[3] * outer[0]
+        split(place_ref, total_v, [0], keep_ref, send_ref)
+
+    far_keep, far_send = call(
+        far_terms,
+        [(2, 1, band, lanes), (events - 1, 2, 1, band, lanes)],
+        (place, total_v, slope_v, far_next_in),
+        [SM] + [VM] * 3,
+        [VM] * 2,
+        [pltpu.VMEM((2, 1, *plane), jnp.float32)],
+    )
+    far_shared = [lax.ppermute(far_send[i], "event", others[i]) for i in range(events - 1)]
 
     def far_second(
-        place_ref, now_v, fwd_v, lame_v, shear_v, scale_v, final_v, far_next_ref, next_v, far_ref, far_fwd_ref,
-        far_next_in_ref,
-        out_ref, keep_ref, send_ref, total_v,
+        place_ref, lame_v, shear_v, scale_v, final_v, far_next_ref, next_v, far_ref, far_next_in_ref, out_ref
     ):
         sigma = sign(place_ref)
         tools = difference_tools(*plane)
@@ -352,25 +402,11 @@
                 return (-far_next_in_ref[base], far_next_in_ref[base + 1], far_next_in_ref[base + 2])
             return tuple(far_next_ref[3 * t + b] for b in range(3))
 
-        def fwd(k, t):
-            if t < 0:
-                return (far_fwd_ref[3 * k] * sigma, far_fwd_ref[3 * k + 1], far_fwd_ref[3 * k + 2])
-            return (fwd_v[k, 0, at(t)] * sigma, fwd_v[k, 1, at(t)], fwd_v[k, 2, at(t)])
-
         outer = normal_stress(strain_parts(field(-2), field(-1), field(0), tools), far_ref[6], far_ref[7])
         lame, shear = lame_v[at(0)], shear_v[at(0)]
         parts = strain_parts(field(-1), field(0), field(1), tools)
         normal = normal_stress(parts, lame, shear)
         force = cross_force(parts, normal, lame, shear, tools)
-        other = strain_parts(fwd(1, -1), fwd(1, 0), fwd(1, 1), tools)
-        pair = term_pair(parts, other, lame, shear)
-        for k in range(2):
-            total_v[k] = pair[k]
-        own = place_ref[1]
-        keep_ref[...] = total_v[:, pl.ds(pl.multiple_of(own * band, 8), band)]
-        for shift in range(1, events):
-            target = lax.rem(own + shift, events)
-            send_ref[shift - 1] = total_v[:, pl.ds(pl.multiple_of(target * band, 8), band)]
         for t in range(cells):
             for b in range(3):
                 value = final_v[b, t]
@@ -382,36 +418,31 @@
                     value = value * sigma
                 out_ref[b, at(t)] = value
 
-    result, far_keep, far_send = call(
+    (result,) = call(
         far_second,
-        [now.shape, (2, band, lanes), (events - 1, 2, band, lanes)],
-        (place, now_v, fwd_v, lame_v, shear_v, scale_v, final_v, far_next, next_v, far_in, far_fwd_in,
-         far_next_in),
-        [SM] + [VM] * 11,
-        [None, VM, VM],
-        [pltpu.VMEM((2, *plane), jnp.float32)],
-    )
-    far_shared = [lax.ppermute(far_send[i], "event", others[i]) for i in range(events - 1)]
-
-    def finish(place_ref, keep_ref, far_keep_ref, *rest):
-        parts = rest[: 2 * (events - 1)]
-        outs = rest[2 * (events - 1) :]
-        for k in range(2):
-            for t in range(cells):
-                value = keep_ref[k, t]
-                for i in range(events - 1):
-                    value = value + parts[i][k, t]
-                if t == 0:
-                    value = value + far_keep_ref[k]
-                    for i in range(events - 1):
-                        value = value + parts[events - 1 + i][k]
-                outs[k][layer(place_ref, t)] = value
+        [now.shape],
+        (place, lame_v, shear_v, scale_v, final_v, far_next, next_v, far_in, far_next_in),
+        [SM] + [VM] * 8,
+        [None],
+    )
+
+    def finish(place_ref, *rest):
+        width = events
+        outs = rest[3 * width :]
+        for group, layers in enumerate((early, middle, [0])):
+            parts = rest[group * width : (group + 1) * width]
+            for k in range(2):
+                for i, t in enumerate(layers):
+                    value = parts[0][k, i]
+                    for part in parts[1:]:
+                        value = value + part[k, i]
+                    outs[k][layer(place_ref, t)] = value
 
     band_shear, band_bulk = call(
         finish,
         [(cells, band, lanes)] * 2,
-        (place, keep, far_keep, *shared, *far_shared),
-        [SM] + [VM] * (2 + 2 * (events - 1)),
+        (place, keep, *shared, keep_mid, *shared_mid, far_keep, *far_shared),
+        [SM] + [VM] * (3 * events),
         [None] * 2,
     )
     return (result[None], band_shear, band_bulk)

time: 39.5 us -> 29.7 us (0.75)
  waiting for transfers between devices: 13 us -> 0.71 us
  local copies, waits for them, and re-layouts: 4.45 us -> 0 us
  starting transfers between devices: 10.8 us -> 14.4 us
  Pallas kernels: 10.2 us -> 13.6 us
    ppermute x1, waiting for transfers between devices: 5.33 us -> 0.01 us  [local(): far_next_in = lax.ppermute(far_next, 'blk', far)]
    unnamed x12 -> x0, local copies, waits for them, and re-layouts: 4.45 us -> none
    pallas_call x6 -> x7, Pallas kernels: 10.2 us -> 13.6 us  [call(): pl.pallas_call(kernel, out_shape=shapes, in_specs=[pl.BlockSpec(memory_sp...]
    ppermute x1, waiting for transfers between devices: 2.92 us -> 0.01 us  [local(): far_fwd_in = lax.ppermute(far_fwd_out, 'blk', far)]
    ppermute x1, waiting for transfers between devices: 3.43 us -> 0.69 us  [local(): lax.ppermute(far_send[i], 'event', others[i])]
    ppermute x1, starting transfers between devices: 2.53 us -> 4.47 us  [local(): far_next_in = lax.ppermute(far_next, 'blk', far)]
    ppermute x1, waiting for transfers between devices: 1.35 us -> 0.01 us  [local(): far_in = lax.ppermute(far_out, 'blk', far)]
    ppermute x1, starting transfers between devices: 0.48 us -> 1.56 us  [local(): lax.ppermute(far_send[i], 'event', others[i])]
  transfers between devices with their start and end apart: 7 -> 8, of which waited for: 4 -> 1; matrix products, arithmetic and copies ran while one was open for 0% -> 0% of each run, Pallas kernels for 13% -> 35%
where the time goes in v2:
time: 29.7 us; the launch traced here: 29.5 us
  starting transfers between devices  14.4 us (48%)
  Pallas kernels  13.6 us (46%)
  waiting for transfers between devices  0.71 us (2%)
  between operations  0.69 us (2%)
    pallas_call x7, Pallas kernels, call(): pl.pallas_call(kernel, out_shape=shapes, in_specs=[pl.BlockSpec(memory_sp...  13.6 us
    ppermute x1, starting transfers between devices, local(): far_in = lax.ppermute(far_out, 'blk', far)  5.67 us
    ppermute x1, starting transfers between devices, local(): far_next_in = lax.ppermute(far_next, 'blk', far)  4.47 us
    ppermute x1, starting transfers between devices, local(): lax.ppermute(far_send[i], 'event', others[i])  1.56 us
    ppermute x1, starting transfers between devices, local(): lax.ppermute(send[i], 'event', others[i])  1.48 us
    ppermute x1, waiting for transfers between devices, local(): lax.ppermute(far_send[i], 'event', others[i])  0.69 us
    ppermute x1, starting transfers between devices, local(): lax.ppermute(send_mid[i], 'event', others[i])  0.6 us
  transfers between devices with their start and end apart: 8, of which 1 were waited for; matrix products, arithmetic and copies ran while one was open for 0% of the time, Pallas kernels for 35%

profile of v2, /device:TPU:0, one launch (start us, length us, event | category | flops | bytes accessed | tf_op | source)
XLA Modules:
  0.0 29.5 jit_solution(2044139400461082709)
XLA Ops:
  0.6 0.1 pad_add_fusion.place_ref
  0.7 1.9 %shard_map.85 = (f32[14,64,128]{2,1,0:T(8,128)S(1)}, f32[8,64,128]{2,1,0:T(8,128)S(1)}, f32[6,64,128]{2,1,0:T(8,128)S(1)}) custom-call(s32[2]{0:T(128)S(1)} %pad_add_fusion.place_ref, f32[3,8,64,128]{3,2,1,0:T(8,128)} %bitcast.14, f32[2,3,8,64,128]{4,3,2,1,0:T(8,128)} %bitcast.12, f32[8,64,128]{2,1,0:T(8,128)} %lame_ref.3, f32[8,64,128]{2,1,0:T(8,128)} %shear_ref.3), custom_call_target="tpu_custom_call" | custom-call | tf_op jit(solution)/shard_map/pallas_call | solution.py:75
  2.6 0.5 %collective-permute-start = (f32[14,64,128]{2,1,0:T(8,128)S(1)}, f32[14,64,128]{2,1,0:T(8,128)S(1)}, u32[]{:S(2)}, u32[]{:S(2)}) collective-permute-start(f32[14,64,128]{2,1,0:T(8,128)S(1)} %get-tuple-element.25), channel_id=1, source_target_pairs={{0,2},{2,0},{4,6},{6,4},{8,10},{10,8},{12,14},{14,12},{16,18},{18,... | collective-permute-start | bytes 1376264 | tf_op jit(solution)/shard_map/ppermute | solution.py:145
  3.1 5.7 %collective-permute-start.1 = (f32[8,64,128]{2,1,0:T(8,128)S(1)}, f32[8,64,128]{2,1,0:T(8,128)S(1)}, u32[]{:S(2)}, u32[]{:S(2)}) collective-permute-start(f32[8,64,128]{2,1,0:T(8,128)S(1)} %get-tuple-element.33), channel_id=1, source_target_pairs={{0,30},{2,4},{4,2},{6,8},{8,6},{10,12},{12,10},{14,16},{16,14},{18... | collective-permute-start | bytes 786440 | tf_op jit(solution)/shard_map/ppermute | solution.py:146
  8.8 0.0 collective-permute-start.3
  8.8 0.0 collective-permute-done.near_ref
  8.8 5.0 %shard_map.86 = (f32[3,8,64,128]{3,2,1,0:T(8,128)S(1)}, f32[2,3,8,64,128]{4,3,2,1,0:T(8,128)S(1)}, f32[8,64,128]{2,1,0:T(8,128)S(1)}, f32[8,64,128]{2,1,0:T(8,12...) custom-call(s32[2]{0:T(128)S(1)} %pad_add_fusion.place_ref, ...), custom_call_target="tpu_custom_call" | custom-call | tf_op jit(solution)/shard_map/pallas_call | solution.py:75
  13.9 0.1 collective-permute-start.2
  14.0 0.0 collective-permute-done.1.far_ref
  14.0 0.8 %shard_map.87.far_next_ref = f32[6,64,128]{2,1,0:T(8,128)S(1)} custom-call(s32[2]{0:T(128)S(1)} %pad_add_fusion.place_ref, f32[3,8,64,128]{3,2,1,0:T(8,128)S(1)} %get-tuple-element.29.now_v, f32[8,64,128]{2,1,0:T(8,128)S(1)} %get-tuple-element.26.lame_v, f32[8,64,128]{2,1,0:T(8,128)S(1)} %get-tuple-element.27.shear_v, ...), custom_call_target="tpu_custom_call" | custom-call | tf_op jit(solution)/shard_map/pallas_call | solution.py:75
  14.8 4.5 %collective-permute-start.4 = (f32[6,64,128]{2,1,0:T(8,128)S(1)}, f32[6,64,128]{2,1,0:T(8,128)S(1)}, u32[]{:S(2)}, u32[]{:S(2)}) collective-permute-start(f32[6,64,128]{2,1,0:T(8,128)S(1)} %shard_map.87.far_next_ref), channel_id=1, source_target_pairs={{0,30},{2,4},{4,2},{6,8},{8,6},{10,12},{12,10},{14,16},{16,14},{18... | collective-permute-start | bytes 589832 | tf_op jit(solution)/shard_map/ppermute | solution.py:280
  19.3 1.5 %collective-permute-start.5 = (f32[2,4,32,128]{3,2,1,0:T(8,128)S(1)}, f32[2,4,32,128]{3,2,1,0:T(8,128)S(1)}, u32[]{:S(2)}, u32[]{:S(2)}) collective-permute-start(f32[2,4,32,128]{3,2,1,0:T(8,128)S(1)} %bitcast.9), channel_id=1, source_target_pairs={{0,1},{1,0},{2,3},{3,2},{4,5},{5,4},{6,7},{7,6},{8,9},{9,8},{10,11... | collective-permute-start | bytes 393224 | tf_op jit(solution)/shard_map/ppermute | solution.py:249
  20.7 0.0 collective-permute-done.3.far_fwd_ref
  20.7 0.0 collective-permute-done.2.near_next_ref
  20.7 2.3 %shard_map.88 = (f32[3,8,64,128]{3,2,1,0:T(8,128)S(1)}, f32[2,8,64,128]{3,2,1,0:T(8,128)S(1)}, f32[4,64,128]{2,1,0:T(8,128)S(1)}, f32[2,3,32,128]{3,2,1,0:T(8,128)S(1)}, f32[1,2,3,32,128]{4,3,2,1,0:T(8,128)S(1)}) custom-call(s32[2]{0:T(128)S(1)} %pad_add_fusion.place_ref, f32[3,8,64,128]{3,2,1,0:T(8,128)S(1)} %get-tuple-element.29.now_v, ...), custom_call_target="tpu_custom_call" | custom-call | tf_op jit(solution)/shard_map/pallas_call | solution.py:75
  23.1 0.6 %collective-permute-start.6 = (f32[2,3,32,128]{3,2,1,0:T(8,128)S(1)}, f32[2,3,32,128]{3,2,1,0:T(8,128)S(1)}, u32[]{:S(2)}, u32[]{:S(2)}) collective-permute-start(f32[2,3,32,128]{3,2,1,0:T(8,128)S(1)} %bitcast.10), channel_id=1, source_target_pairs={{0,1},{1,0},{2,3},{3,2},{4,5},{5,4},{6,7},{7,6},{8,9},{9,8},{10,11... | collective-permute-start | bytes 294920 | tf_op jit(solution)/shard_map/ppermute | solution.py:369
  23.7 0.0 collective-permute-done.4.far_next_in_ref
  23.7 0.6 %shard_map.90 = (f32[2,1,32,128]{3,2,1,0:T(8,128)S(1)}, f32[1,2,1,32,128]{4,3,2,1,0:T(8,128)S(1)}) custom-call(s32[2]{0:T(128)S(1)} %pad_add_fusion.place_ref, f32[2,8,64,128]{3,2,1,0:T(8,128)S(1)} %get-tuple-element.41.total_ref, f32[4,64,128]{2,1,0:T(8,128)S(1)} %get-tuple-element.42.slope_ref, f32[6,64,128]{2,1,0:T(8,128)S(1)} %collective-permute-done.4.far_next_in_ref), custom_call_target="tpu_custom_call" | custom-call | tf_op jit(solution)/shard_map/pallas_call | solution.py:75
  24.2 1.6 %collective-permute-start.7 = (f32[2,1,32,128]{3,2,1,0:T(8,128)S(1)}, f32[2,1,32,128]{3,2,1,0:T(8,128)S(1)}, u32[]{:S(2)}, u32[]{:S(2)}) collective-permute-start(f32[2,1,32,128]{3,2,1,0:T(8,128)S(1)} %bitcast.11), channel_id=1, source_target_pairs={{0,1},{1,0},{2,3},{3,2},{4,5},{5,4},{6,7},{7,6},{8,9},{9,8},{10,11... | collective-permute-start | bytes 98312 | tf_op jit(solution)/shard_map/ppermute | solution.py:388
  25.8 1.7 %shard_map.89 = f32[3,8,64,128]{3,2,1,0:T(8,128)} custom-call(s32[2]{0:T(128)S(1)} %pad_add_fusion.place_ref, f32[8,64,128]{2,1,0:T(8,128)S(1)} %get-tuple-element.26.lame_v, f32[8,64,128]{2,1,0:T(8,128)S(1)} %get-tuple-element.27.shear_v, f32[8,64,128]{2,1,0:T(8,128)S(1)} %get-tuple-element.28.scale_v, f32[3,8,64,128]{3,2,1,0:T(8,128)S(1)} %get-tuple-element.36.final_v, ...), custom_call_target="tpu_custom_call" | custom-call | tf_op jit(solution)/shard_map/pallas_call | solution.py:75
  27.5 0.0 collective-permute-done.5.rest_1_
  27.5 0.7 %collective-permute-done.7.rest_5_ = f32[2,1,32,128]{3,2,1,0:T(8,128)S(1)} collective-permute-done((f32[2,1,32,128]{3,2,1,0:T(8,128)S(1)}, f32[2,1,32,128]{3,2,1,0:T(8,128)S(1)}, u32[]{:S(2)}, u32[]{:S(2)}) %collective-permute-start.7) | collective-permute-done | bytes 32800 | tf_op jit(solution)/shard_map/ppermute | solution.py:388
  28.2 0.0 collective-permute-done.6.rest_3_
  28.2 1.3 %shard_map.91 = (f32[8,32,128]{2,1,0:T(8,128)}, f32[8,32,128]{2,1,0:T(8,128)}) custom-call(s32[2]{0:T(128)S(1)} %pad_add_fusion.place_ref, f32[2,4,32,128]{3,2,1,0:T(8,128)S(1)} %get-tuple-element.37.rest_0_, f32[2,4,32,128]{3,2,1,0:T(8,128)S(1)} %collective-permute-done.5.rest_1_, f32[2,3,32,128]{3,2,1,0:T(8,128)S(1)} %get-tuple-element.39.rest_2_, ...), custom_call_target="tpu_custom_call" | custom-call | tf_op jit(solution)/shard_map/pallas_call | solution.py:75
Async XLA Ops:
  2.6 6.2 %collective-permute-start = (f32[14,64,128]{2,1,0:T(8,128)S(1)}, f32[14,64,128]{2,1,0:T(8,128)S(1)}, u32[]{:S(2)}, u32[]{:S(2)}) collective-permute-start(f32[14,64,128]{2,1,0:T(8,128)S(1)} %get-tuple-element.25), channel_id=1, source_target_pairs={{0,2},{2,0},{4,6},{6,4},{8,10},{10,8},{12,14},{14,12},{16,18},{18,... | collective-permute-start | bytes 1376264 | tf_op jit(solution)/shard_map/ppermute | solution.py:145
  3.1 10.8 %collective-permute-start.1 = (f32[8,64,128]{2,1,0:T(8,128)S(1)}, f32[8,64,128]{2,1,0:T(8,128)S(1)}, u32[]{:S(2)}, u32[]{:S(2)}) collective-permute-start(f32[8,64,128]{2,1,0:T(8,128)S(1)} %get-tuple-element.33), channel_id=1, source_target_pairs={{0,30},{2,4},{4,2},{6,8},{8,6},{10,12},{12,10},{14,16},{16,14},{18... | collective-permute-start | bytes 786440 | tf_op jit(solution)/shard_map/ppermute | solution.py:146
  8.8 11.9 %collective-permute-start.3 = (f32[6,64,128]{2,1,0:T(8,128)S(1)}, f32[6,64,128]{2,1,0:T(8,128)S(1)}, u32[]{:S(2)}, u32[]{:S(2)}) collective-permute-start(f32[6,64,128]{2,1,0:T(8,128)S(1)} %get-tuple-element.35), channel_id=1, source_target_pairs={{0,30},{2,4},{4,2},{6,8},{8,6},{10,12},{12,10},{14,16},{16,14},{18... | collective-permute-start | bytes 589832 | tf_op jit(solution)/shard_map/ppermute | solution.py:147
  13.9 6.9 %collective-permute-start.2 = (f32[6,64,128]{2,1,0:T(8,128)S(1)}, f32[6,64,128]{2,1,0:T(8,128)S(1)}, u32[]{:S(2)}, u32[]{:S(2)}) collective-permute-start(f32[6,64,128]{2,1,0:T(8,128)S(1)} %get-tuple-element.34), channel_id=1, source_target_pairs={{0,2},{2,0},{4,6},{6,4},{8,10},{10,8},{12,14},{14,12},{16,18},{18,... | collective-permute-start | bytes 589832 | tf_op jit(solution)/shard_map/ppermute | solution.py:248
  14.8 8.9 %collective-permute-start.4 = (f32[6,64,128]{2,1,0:T(8,128)S(1)}, f32[6,64,128]{2,1,0:T(8,128)S(1)}, u32[]{:S(2)}, u32[]{:S(2)}) collective-permute-start(f32[6,64,128]{2,1,0:T(8,128)S(1)} %shard_map.87.far_next_ref), channel_id=1, source_target_pairs={{0,30},{2,4},{4,2},{6,8},{8,6},{10,12},{12,10},{14,16},{16,14},{18... | collective-permute-start | bytes 589832 | tf_op jit(solution)/shard_map/ppermute | solution.py:280
  19.3 8.3 %collective-permute-start.5 = (f32[2,4,32,128]{3,2,1,0:T(8,128)S(1)}, f32[2,4,32,128]{3,2,1,0:T(8,128)S(1)}, u32[]{:S(2)}, u32[]{:S(2)}) collective-permute-start(f32[2,4,32,128]{3,2,1,0:T(8,128)S(1)} %bitcast.9), channel_id=1, source_target_pairs={{0,1},{1,0},{2,3},{3,2},{4,5},{5,4},{6,7},{7,6},{8,9},{9,8},{10,11... | collective-permute-start | bytes 393224 | tf_op jit(solution)/shard_map/ppermute | solution.py:249
  23.1 5.2 %collective-permute-start.6 = (f32[2,3,32,128]{3,2,1,0:T(8,128)S(1)}, f32[2,3,32,128]{3,2,1,0:T(8,128)S(1)}, u32[]{:S(2)}, u32[]{:S(2)}) collective-permute-start(f32[2,3,32,128]{3,2,1,0:T(8,128)S(1)} %bitcast.10), channel_id=1, source_target_pairs={{0,1},{1,0},{2,3},{3,2},{4,5},{5,4},{6,7},{7,6},{8,9},{9,8},{10,11... | collective-permute-start | bytes 294920 | tf_op jit(solution)/shard_map/ppermute | solution.py:369
  24.2 4.0 %collective-permute-start.7 = (f32[2,1,32,128]{3,2,1,0:T(8,128)S(1)}, f32[2,1,32,128]{3,2,1,0:T(8,128)S(1)}, u32[]{:S(2)}, u32[]{:S(2)}) collective-permute-start(f32[2,1,32,128]{3,2,1,0:T(8,128)S(1)} %bitcast.11), channel_id=1, source_target_pairs={{0,1},{1,0},{2,3},{3,2},{4,5},{5,4},{6,7},{7,6},{8,9},{9,8},{10,11... | collective-permute-start | bytes 98312 | tf_op jit(solution)/shard_map/ppermute | solution.py:388

commit v3 on v2

--- a/solution.py
+++ b/solution.py
@@ -23,11 +23,25 @@
         lower = jnp.where(lane == 0, 0.0, pltpu.roll(values, 1, 1))
         return upper - lower
 
-    return along_rows, along_lanes
+    key = lax.broadcasted_iota(jnp.int32, (3 * lanes, lanes), 0) % lanes
+    out = lax.broadcasted_iota(jnp.int32, (3 * lanes, lanes), 1)
+    weights = ((key == out + 1).astype(jnp.float32) - (key == out - 1).astype(jnp.float32)).astype(jnp.bfloat16)
+
+    def along_lanes_three(fields):
+        values = jnp.concatenate(fields, axis=0)
+        high = values.astype(jnp.bfloat16)
+        rest = values - high.astype(jnp.float32)
+        middle = rest.astype(jnp.bfloat16)
+        low = (rest - middle.astype(jnp.float32)).astype(jnp.bfloat16)
+        parts = jnp.concatenate([high, middle, low], axis=1)
+        result = jnp.dot(parts, weights, preferred_element_type=jnp.float32)
+        return [result[rows * b : rows * (b + 1)] for b in range(len(fields))]
+
+    return along_rows, along_lanes, along_lanes_three
 
 
 def strain_parts(before, middle, after, tools):
-    along_rows, along_lanes = tools
+    along_rows, along_lanes, along_lanes_three = tools
     first = after[0] - before[0]
     second = along_rows(middle[1])
     third = along_lanes(middle[2])
@@ -42,16 +56,17 @@
 
 
 def cross_force(parts, normal, lame, shear, tools):
-    along_rows, along_lanes = tools
+    along_rows, along_lanes, along_lanes_three = tools
     pressure = lame * parts[6]
     twice = 2.0 * shear
     s_22 = twice * parts[1] + pressure
     s_33 = twice * parts[2] + pressure
     s_23 = shear * parts[5]
+    third_of = along_lanes_three((normal[2], s_23, s_33))
     return (
-        along_rows(normal[1]) + along_lanes(normal[2]),
-        along_rows(s_22) + along_lanes(s_23),
-        along_rows(s_23) + along_lanes(s_33),
+        along_rows(normal[1]) + third_of[0],
+        along_rows(s_22) + third_of[1],
+        along_rows(s_23) + third_of[2],
     )
 
 
@@ -92,9 +107,6 @@
     plane = (rows, lanes)
     VM, SM, ANY = pltpu.VMEM, pltpu.SMEM, pl.ANY
 
-    odd = lax.rem(lax.axis_index("blk"), 2)
-    mine = lax.axis_index("event")
-    place = jnp.stack([odd, mine]).astype(jnp.int32)
     near = [(i, i + 1 - 2 * (i % 2)) for i in range(slabs)]
     far = [(i, (i - 1 + 2 * (i % 2)) % slabs) for i in range(slabs)]
     others = [
@@ -105,29 +117,36 @@
         pltpu.with_memory_space_constraint(x, pltpu.HBM)
         for x in (adjoint_now[0], adjoint_prev[0], forward_field[0], density, lame_first, shear_modulus)
     ]
-    now, prev, forward, density, lame_first, shear_modulus = in_hbm
+    now_hbm, prev, forward_hbm, density, lame_hbm, shear_hbm = in_hbm
+    now, forward = adjoint_now[0], forward_field[0]
+
+    def where():
+        return lax.rem(lax.axis_index("blk"), 2), lax.axis_index("event")
 
     def layer(place_ref, t):
         return t + place_ref[0] * (last - 2 * t)
 
+    def far_slot(place_ref, n):
+        return (1 - n) + place_ref[0] * (2 * n - 1)
+
+    def near_slot(place_ref, n):
+        return n + place_ref[0] * (1 - 2 * n)
+
     def sign(place_ref):
         return (1 - 2 * place_ref[0]).astype(jnp.float32)
 
-    def pack(place_ref, now_ref, forward_ref, lame_ref, shear_ref, near_ref, far_ref, far_fwd_ref, sem):
+    def pack(now_ref, forward_ref, lame_ref, shear_ref, near_ref, far_ref, far_fwd_ref, sem):
+        place_ref = where()
+        odd = place_ref[0]
+        faces = ((far_ref, layer(place_ref, 0), odd * (cells - 2)), (near_ref, layer(place_ref, last), (1 - odd) * (cells - 2)))
         copies = []
-
-        def face(t, step, out, fwd_out, fwd_base):
-            for slot in range(2):
-                copies.append((now_ref.at[:, layer(place_ref, t + slot * step)], out.at[pl.ds(3 * slot, 3)]))
-            copies.append((lame_ref.at[layer(place_ref, t)], out.at[6]))
-            copies.append((shear_ref.at[layer(place_ref, t)], out.at[7]))
-            for k in range(steps):
-                copies.append(
-                    (forward_ref.at[k, :, layer(place_ref, t)], fwd_out.at[pl.ds(fwd_base + 3 * k, 3)])
-                )
-
-        face(0, 1, far_ref, far_fwd_ref, 0)
-        face(last, -1, near_ref, near_ref, 8)
+        for out, at, low in faces:
+            copies.append((now_ref.at[:, pl.ds(low, 2)], out.at[pl.ds(0, 3)]))
+            copies.append((lame_ref.at[at], out.at[3, 0]))
+            copies.append((shear_ref.at[at], out.at[3, 1]))
+        copies.append((forward_ref.at[:, :, layer(place_ref, 0)], far_fwd_ref))
+        for k in range(steps):
+            copies.append((forward_ref.at[k, :, layer(place_ref, last)], near_ref.at[pl.ds(4, 3), k]))
         started = [pltpu.make_async_copy(src, dst, sem.at[i]) for i, (src, dst) in enumerate(copies)]
         for copy in started:
             copy.start()
@@ -136,11 +155,11 @@
 
     near_out, far_out, far_fwd_out = call(
         pack,
-        [(8 + 3 * steps, *plane), (8, *plane), (3 * steps, *plane)],
-        (place, now, forward, lame_first, shear_modulus),
-        [SM, ANY, ANY, ANY, ANY],
+        [(7, 2, *plane), (4, 2, *plane), (steps, 3, *plane)],
+        (now_hbm, forward_hbm, lame_hbm, shear_hbm),
+        [ANY, ANY, ANY, ANY],
         [VM, VM, VM],
-        [pltpu.SemaphoreType.DMA((8 + 2 * steps,))],
+        [pltpu.SemaphoreType.DMA((7 + steps,))],
     )
     near_in = lax.ppermute(near_out, "blk", near)
     far_in = lax.ppermute(far_out, "blk", far)
@@ -156,22 +175,19 @@
                 for i, t in enumerate(layers):
                     out[k, i] = terms_ref[k, t, pl.ds(start, band)]
 
-    def first(
-        place_ref, now_ref, prev_ref, forward_ref, dens_ref, lame_ref, shear_ref, near_ref,
-        now_v, fwd_v, lame_v, shear_v, scale_v, next_v, near_next, terms_v, keep_ref, send_ref,
+    def first(now_v, prev_ref, fwd_v, dens_ref, lame_v, shear_v, near_ref,
+        scale_v, next_v, near_next, terms_v, keep_ref, send_ref,
         prev_v, dens_v, normal_v, sem,
     ):
+        place_ref = where()
         moves = [
             pltpu.make_async_copy(src, dst, sem.at[i])
             for i, (src, dst) in enumerate(
-                [(now_ref, now_v), (lame_ref, lame_v), (shear_ref, shear_v), (forward_ref, fwd_v),
-                 (prev_ref, prev_v), (dens_ref, dens_v)]
+                [(dens_ref, dens_v), (prev_ref, prev_v)]
             )
         ]
         for move in moves:
             move.start()
-        for move in moves:
-            move.wait()
         sigma = sign(place_ref)
         tools = difference_tools(*plane)
 
@@ -181,23 +197,20 @@
         def field(t):
             if t <= last:
                 return (now_v[0, at(t)] * sigma, now_v[1, at(t)], now_v[2, at(t)])
-            base = 3 * (t - cells)
-            return (near_ref[base] * sigma, near_ref[base + 1], near_ref[base + 2])
+            slot = near_slot(place_ref, t - cells)
+            return (near_ref[0, slot] * sigma, near_ref[1, slot], near_ref[2, slot])
 
         def fwd(k, t):
             if t <= last:
                 return (fwd_v[k, 0, at(t)] * sigma, fwd_v[k, 1, at(t)], fwd_v[k, 2, at(t)])
-            base = 8 + 3 * k
-            return (near_ref[base] * sigma, near_ref[base + 1], near_ref[base + 2])
-
-        for t in range(cells):
-            scale_v[t] = (0.25 * step_squared) / dens_v[at(t)]
+            return (near_ref[4, k] * sigma, near_ref[5, k], near_ref[6, k])
+
         for t in range(1, cells + 1):
             parts = strain_parts(field(t - 1), field(t), field(t + 1), tools)
             if t <= last:
                 lame, shear = lame_v[at(t)], shear_v[at(t)]
             else:
-                lame, shear = near_ref[6], near_ref[7]
+                lame, shear = near_ref[3, 0], near_ref[3, 1]
             normal = normal_stress(parts, lame, shear)
             for b in range(3):
                 normal_v[b, t] = normal[b]
@@ -209,6 +222,10 @@
                 pair = term_pair(parts, other, lame, shear)
                 terms_v[0, t] = pair[0]
                 terms_v[1, t] = pair[1]
+        for move in moves:
+            move.wait()
+        for t in range(cells):
+            scale_v[t] = (0.25 * step_squared) / dens_v[at(t)]
         for t in range(cells):
             for b in range(3):
                 force = normal_v[b, t + 1]
@@ -235,20 +252,22 @@
 
     early = list(range(3, last))
     middle = [1, 2, last]
-    now_v, fwd_v, lame_v, shear_v, scale_v, next_v, near_next, terms_v, keep, send = call(
+    now_v, fwd_v, lame_v, shear_v = now, forward, lame_first, shear_modulus
+    scale_v, next_v, near_next, terms_v, keep, send = call(
         first,
-        [now.shape, forward.shape, density.shape, density.shape, density.shape, now.shape,
+        [density.shape, now.shape,
          (6, *plane), (2, cells, *plane), (2, len(early), band, lanes), (events - 1, 2, len(early), band, lanes)],
-        (place, now, prev, forward, density, lame_first, shear_modulus, near_in),
-        [SM] + [ANY] * 6 + [VM],
-        [VM] * 10,
+        (now, prev, forward, density, lame_first, shear_modulus, near_in),
+        [VM, ANY, VM, ANY, VM, VM, VM],
+        [VM] * 6,
         [pltpu.VMEM(now.shape, jnp.float32), pltpu.VMEM(density.shape, jnp.float32),
-         pltpu.VMEM((3, cells + 1, *plane), jnp.float32), pltpu.SemaphoreType.DMA((6,))],
+         pltpu.VMEM((3, cells + 1, *plane), jnp.float32), pltpu.SemaphoreType.DMA((2,))],
     )
     near_next_in = lax.ppermute(near_next, "blk", near)
     shared = [lax.ppermute(send[i], "event", others[i]) for i in range(events - 1)]
 
-    def far_first(place_ref, now_v, lame_v, shear_v, scale_v, next_v, far_ref, far_next):
+    def far_first(now_v, lame_v, shear_v, scale_v, next_v, far_ref, far_next):
+        place_ref = where()
         sigma = sign(place_ref)
         tools = difference_tools(*plane)
 
@@ -258,10 +277,10 @@
         def field(t):
             if t >= 0:
                 return (now_v[0, at(t)] * sigma, now_v[1, at(t)], now_v[2, at(t)])
-            base = 3 * (-1 - t)
-            return (far_ref[base] * sigma, far_ref[base + 1], far_ref[base + 2])
-
-        outer = normal_stress(strain_parts(field(-2), field(-1), field(0), tools), far_ref[6], far_ref[7])
+            slot = far_slot(place_ref, -1 - t)
+            return (far_ref[0, slot] * sigma, far_ref[1, slot], far_ref[2, slot])
+
+        outer = normal_stress(strain_parts(field(-2), field(-1), field(0), tools), far_ref[3, 0], far_ref[3, 1])
         lame, shear = lame_v[at(0)], shear_v[at(0)]
         parts = strain_parts(field(-1), field(0), field(1), tools)
         normal = normal_stress(parts, lame, shear)
@@ -273,17 +292,17 @@
     (far_next,) = call(
         far_first,
         [(6, *plane)],
-        (place, now_v, lame_v, shear_v, scale_v, next_v, far_in),
-        [SM] + [VM] * 6,
+        (now_v, lame_v, shear_v, scale_v, next_v, far_in),
+        [VM] * 6,
         [VM],
     )
     far_next_in = lax.ppermute(far_next, "blk", far)
 
-    def second(
-        place_ref, now_v, fwd_v, lame_v, shear_v, scale_v, next_v, terms_v, far_next_ref, near_next_ref,
+    def second(now_v, fwd_v, lame_v, shear_v, scale_v, next_v, terms_v, far_next_ref, near_next_ref,
         near_ref, far_ref, far_fwd_ref,
         final_v, total_v, slope_v, keep_ref, send_ref, normal_v,
     ):
+        place_ref = where()
         sigma = sign(place_ref)
         tools = difference_tools(*plane)
 
@@ -293,7 +312,8 @@
         def start(t):
             if t >= 0:
                 return (now_v[0, at(t)] * sigma, now_v[1, at(t)], now_v[2, at(t)])
-            return (far_ref[0] * sigma, far_ref[1], far_ref[2])
+            slot = far_slot(place_ref, 0)
+            return (far_ref[0, slot] * sigma, far_ref[1, slot], far_ref[2, slot])
 
         def field(t):
             if t < 2:
@@ -305,18 +325,17 @@
 
         def fwd(k, t):
             if t < 0:
-                return (far_fwd_ref[3 * k] * sigma, far_fwd_ref[3 * k + 1], far_fwd_ref[3 * k + 2])
+                return (far_fwd_ref[k, 0] * sigma, far_fwd_ref[k, 1], far_fwd_ref[k, 2])
             if t <= last:
                 return (fwd_v[k, 0, at(t)] * sigma, fwd_v[k, 1, at(t)], fwd_v[k, 2, at(t)])
-            base = 8 + 3 * k
-            return (near_ref[base] * sigma, near_ref[base + 1], near_ref[base + 2])
+            return (near_ref[4, k] * sigma, near_ref[5, k], near_ref[6, k])
 
         for t in range(1, cells + 1):
             parts = strain_parts(field(t - 1), field(t), field(t + 1), tools)
             if t <= last:
                 lame, shear = lame_v[at(t)], shear_v[at(t)]
             else:
-                lame, shear = near_ref[6], near_ref[7]
+                lame, shear = near_ref[3, 0], near_ref[3, 1]
             normal = normal_stress(parts, lame, shear)
             for b in range(3):
                 normal_v[b, t] = normal[b]
@@ -360,15 +379,16 @@
         second,
         [now.shape, (2, cells, *plane), (4, *plane),
          (2, len(middle), band, lanes), (events - 1, 2, len(middle), band, lanes)],
-        (place, now_v, fwd_v, lame_v, shear_v, scale_v, next_v, terms_v, far_next, near_next_in,
+        (now_v, fwd_v, lame_v, shear_v, scale_v, next_v, terms_v, far_next, near_next_in,
          near_in, far_in, far_fwd_in),
-        [SM] + [VM] * 12,
+        [VM] * 12,
         [VM] * 5,
         [pltpu.VMEM((3, cells + 1, *plane), jnp.float32)],
     )
     shared_mid = [lax.ppermute(send_mid[i], "event", others[i]) for i in range(events - 1)]
 
-    def far_terms(place_ref, total_ref, slope_ref, far_next_in_ref, keep_ref, send_ref, total_v):
+    def far_terms(total_ref, slope_ref, far_next_in_ref, keep_ref, send_ref, total_v):
+        place_ref = where()
         outer = (-far_next_in_ref[0], far_next_in_ref[1], far_next_in_ref[2])
         shear_part = total_ref[0, 0]
         for b in range(3):
@@ -380,16 +400,16 @@
     far_keep, far_send = call(
         far_terms,
         [(2, 1, band, lanes), (events - 1, 2, 1, band, lanes)],
-        (place, total_v, slope_v, far_next_in),
-        [SM] + [VM] * 3,
+        (total_v, slope_v, far_next_in),
+        [VM] * 3,
         [VM] * 2,
         [pltpu.VMEM((2, 1, *plane), jnp.float32)],
     )
     far_shared = [lax.ppermute(far_send[i], "event", others[i]) for i in range(events - 1)]
 
-    def far_second(
-        place_ref, lame_v, shear_v, scale_v, final_v, far_next_ref, next_v, far_ref, far_next_in_ref, out_ref
+    def far_second(lame_v, shear_v, scale_v, final_v, far_next_ref, next_v, far_ref, far_next_in_ref, out_ref
     ):
+        place_ref = where()
         sigma = sign(place_ref)
         tools = difference_tools(*plane)
 
@@ -402,7 +422,7 @@
                 return (-far_next_in_ref[base], far_next_in_ref[base + 1], far_next_in_ref[base + 2])
             return tuple(far_next_ref[3 * t + b] for b in range(3))
 
-        outer = normal_stress(strain_parts(field(-2), field(-1), field(0), tools), far_ref[6], far_ref[7])
+        outer = normal_stress(strain_parts(field(-2), field(-1), field(0), tools), far_ref[3, 0], far_ref[3, 1])
         lame, shear = lame_v[at(0)], shear_v[at(0)]
         parts = strain_parts(field(-1), field(0), field(1), tools)
         normal = normal_stress(parts, lame, shear)
@@ -421,12 +441,13 @@
     (result,) = call(
         far_second,
         [now.shape],
-        (place, lame_v, shear_v, scale_v, final_v, far_next, next_v, far_in, far_next_in),
-        [SM] + [VM] * 8,
+        (lame_v, shear_v, scale_v, final_v, far_next, next_v, far_in, far_next_in),
+        [VM] * 8,
         [None],
     )
 
-    def finish(place_ref, *rest):
+    def finish(*rest):
+        place_ref = where()
         width = events
         outs = rest[3 * width :]
         for group, layers in enumerate((early, middle, [0])):
@@ -441,8 +462,8 @@
     band_shear, band_bulk = call(
         finish,
         [(cells, band, lanes)] * 2,
-        (place, keep, *shared, keep_mid, *shared_mid, far_keep, *far_shared),
-        [SM] + [VM] * (3 * events),
+        (keep, *shared, keep_mid, *shared_mid, far_keep, *far_shared),
+        [VM] * (3 * events),
         [None] * 2,
     )
     return (result[None], band_shear, band_bulk)

time: 29.7 us -> 26.6 us (0.90)
  Pallas kernels: 13.6 us -> 8.43 us
  waiting for transfers between devices: 0.71 us -> 2.87 us
    pallas_call x7, Pallas kernels: 13.6 us -> 8.43 us  [call(): pl.pallas_call(kernel, out_shape=shapes, in_specs=[pl.BlockSpec(memory_sp...]
    ppermute x1, waiting for transfers between devices: 0.69 us -> 2 us  [local(): lax.ppermute(far_send[i], 'event', others[i])]
    ppermute x1, waiting for transfers between devices: 0.01 us -> 0.85 us  [local(): far_in = lax.ppermute(far_out, 'blk', far)]
  transfers between devices with their start and end apart: 8 -> 8, of which waited for: 1 -> 2; matrix products, arithmetic and copies ran while one was open for 0% -> 0% of each run, Pallas kernels for 35% -> 23%
where the time goes in v3:
time: 26.6 us; the launch traced here: 26.5 us
  starting transfers between devices  14.4 us (54%)
  Pallas kernels  8.43 us (32%)
  waiting for transfers between devices  2.87 us (11%)
  between operations  0.73 us (3%)
    pallas_call x7, Pallas kernels, call(): pl.pallas_call(kernel, out_shape=shapes, in_specs=[pl.BlockSpec(memory_sp...  8.43 us
    ppermute x1, starting transfers between devices, local(): far_in = lax.ppermute(far_out, 'blk', far)  5.67 us
    ppermute x1, starting transfers between devices, local(): far_next_in = lax.ppermute(far_next, 'blk', far)  4.49 us
    ppermute x1, waiting for transfers between devices, local(): lax.ppermute(far_send[i], 'event', others[i])  2 us
    ppermute x1, starting transfers between devices, local(): lax.ppermute(far_send[i], 'event', others[i])  1.56 us
    ppermute x1, starting transfers between devices, local(): lax.ppermute(send[i], 'event', others[i])  1.49 us
    ppermute x1, waiting for transfers between devices, local(): far_in = lax.ppermute(far_out, 'blk', far)  0.85 us
    ppermute x1, starting transfers between devices, local(): lax.ppermute(send_mid[i], 'event', others[i])  0.6 us
  transfers between devices with their start and end apart: 8, of which 2 were waited for; matrix products, arithmetic and copies ran while one was open for 0% of the time, Pallas kernels for 23%

profile of v3, /device:TPU:0, one launch (start us, length us, event | category | flops | bytes accessed | tf_op | source)
XLA Modules:
  0.0 26.5 jit_solution(12280332623447138774)
XLA Ops:
  0.6 0.0 copy-start.1
  0.6 0.0 copy-start
  0.7 0.0 copy-start.2
  0.7 0.0 copy-start.3
  0.7 1.5 %shard_map.85 = (f32[7,2,64,128]{3,2,1,0:T(8,128)S(1)}, f32[4,2,64,128]{3,2,1,0:T(8,128)S(1)}, f32[2,3,64,128]{3,2,1,0:T(8,128)S(1)}) custom-call(f32[3,8,64,128]{3,2,1,0:T(8,128)} %bitcast.10, f32[2,3,8,64,128]{4,3,2,1,0:T(8,128)} %bitcast.7, f32[8,64,128]{2,1,0:T(8,128)} %lame_v.7, f32[8,64,128]{2,1,0:T(8,128)} %shear_v.7), custom_call_target="tpu_custom_call" | custom-call | tf_op jit(solution)/shard_map/pallas_call | solution.py:90
  2.2 0.5 %collective-permute-start = (f32[7,2,64,128]{3,2,1,0:T(8,128)S(1)}, f32[7,2,64,128]{3,2,1,0:T(8,128)S(1)}, u32[]{:S(2)}, u32[]{:S(2)}) collective-permute-start(f32[7,2,64,128]{3,2,1,0:T(8,128)S(1)} %get-tuple-element.21), channel_id=1, source_target_pairs={{0,2},{2,0},{4,6},{6,4},{8,10},{10,8},{12,14},{14,12},{16,18},{18,... | collective-permute-start | bytes 1376264 | tf_op jit(solution)/shard_map/ppermute | solution.py:164
  2.7 5.7 %collective-permute-start.1 = (f32[4,2,64,128]{3,2,1,0:T(8,128)S(1)}, f32[4,2,64,128]{3,2,1,0:T(8,128)S(1)}, u32[]{:S(2)}, u32[]{:S(2)}) collective-permute-start(f32[4,2,64,128]{3,2,1,0:T(8,128)S(1)} %get-tuple-element.25), channel_id=1, source_target_pairs={{0,30},{2,4},{4,2},{6,8},{8,6},{10,12},{12,10},{14,16},{16,14},{18... | collective-permute-start | bytes 786440 | tf_op jit(solution)/shard_map/ppermute | solution.py:165
  8.3 0.0 collective-permute-start.3
  8.4 0.0 collective-permute-done.near_ref
  8.4 0.0 copy-done.1
  8.4 0.0 copy-done
  8.4 0.0 copy-done.2
  8.4 0.0 copy-done.3
  8.4 3.2 %shard_map.86 = (f32[8,64,128]{2,1,0:T(8,128)S(1)}, f32[3,8,64,128]{3,2,1,0:T(8,128)S(1)}, f32[6,64,128]{2,1,0:T(8,128)S(1)}, f32[2,8,64,128]{3,2,1,0:T(8,128)S(...) custom-call(f32[3,8,64,128]{3,2,1,0:T(8,128)S(1)} %bitcast.11, f32[3,8,64,128]{3,2,1,0:T(8,128)} %bitcast.17, ...), custom_call_target="tpu_custom_call" | custom-call | tf_op jit(solution)/shard_map/pallas_call | solution.py:90
  11.6 0.1 collective-permute-start.2
  11.7 0.9 %collective-permute-done.1.far_ref = f32[4,2,64,128]{3,2,1,0:T(8,128)S(1)} collective-permute-done((f32[4,2,64,128]{3,2,1,0:T(8,128)S(1)}, f32[4,2,64,128]{3,2,1,0:T(8,128)S(1)}, u32[]{:S(2)}, u32[]{:S(2)}) %collective-permute-start.1) | collective-permute-done | bytes 262176 | tf_op jit(solution)/shard_map/ppermute | solution.py:165
  12.5 0.3 %shard_map.87.far_next_ref = f32[6,64,128]{2,1,0:T(8,128)S(1)} custom-call(f32[3,8,64,128]{3,2,1,0:T(8,128)S(1)} %bitcast.12, f32[8,64,128]{2,1,0:T(8,128)S(1)} %copy-done.2, f32[8,64,128]{2,1,0:T(8,128)S(1)} %copy-done.3, f32[8,64,128]{2,1,0:T(8,128)S(1)} %get-tuple-element.22.scale_v, f32[3,8,64,128]{3,2,1,0:T(8,128)S(1)} %get-tuple-element.23.next_v, ...), custom_call_target="tpu_custom_call" | custom-call | tf_op jit(solution)/shard_map/pallas_call | solution.py:90
  12.8 4.5 %collective-permute-start.4 = (f32[6,64,128]{2,1,0:T(8,128)S(1)}, f32[6,64,128]{2,1,0:T(8,128)S(1)}, u32[]{:S(2)}, u32[]{:S(2)}) collective-permute-start(f32[6,64,128]{2,1,0:T(8,128)S(1)} %shard_map.87.far_next_ref), channel_id=1, source_target_pairs={{0,30},{2,4},{4,2},{6,8},{8,6},{10,12},{12,10},{14,16},{16,14},{18... | collective-permute-start | bytes 589832 | tf_op jit(solution)/shard_map/ppermute | solution.py:299
  17.3 1.5 %collective-permute-start.5 = (f32[2,4,32,128]{3,2,1,0:T(8,128)S(1)}, f32[2,4,32,128]{3,2,1,0:T(8,128)S(1)}, u32[]{:S(2)}, u32[]{:S(2)}) collective-permute-start(f32[2,4,32,128]{3,2,1,0:T(8,128)S(1)} %bitcast.14), channel_id=1, source_target_pairs={{0,1},{1,0},{2,3},{3,2},{4,5},{5,4},{6,7},{7,6},{8,9},{9,8},{10,11... | collective-permute-start | bytes 393224 | tf_op jit(solution)/shard_map/ppermute | solution.py:267
  18.8 0.0 collective-permute-done.3.far_fwd_ref
  18.8 0.0 collective-permute-done.2.near_next_ref
  18.8 1.6 %shard_map.88 = (f32[3,8,64,128]{3,2,1,0:T(8,128)S(1)}, f32[2,8,64,128]{3,2,1,0:T(8,128)S(1)}, f32[4,64,128]{2,1,0:T(8,128)S(1)}, f32[2,3,32,128]{3,2,1,0:T(8,128)S(1)}, f32[1,2,3,32,128]{4,3,2,1,0:T(8,128)S(1)}) custom-call(f32[3,8,64,128]{3,2,1,0:T(8,128)S(1)} %bitcast.13, f32[2,3,8,64,128]{4,3,2,1,0:T(8,128)S(1)} %bitcast.9, f32[8,64,128]{2,1,0:T(8,128)S(1)} %copy-done.2, ...), custom_call_target="tpu_custom_call" | custom-call | tf_op jit(solution)/shard_map/pallas_call | solution.py:90
  20.4 0.6 %collective-permute-start.6 = (f32[2,3,32,128]{3,2,1,0:T(8,128)S(1)}, f32[2,3,32,128]{3,2,1,0:T(8,128)S(1)}, u32[]{:S(2)}, u32[]{:S(2)}) collective-permute-start(f32[2,3,32,128]{3,2,1,0:T(8,128)S(1)} %bitcast.15), channel_id=1, source_target_pairs={{0,1},{1,0},{2,3},{3,2},{4,5},{5,4},{6,7},{7,6},{8,9},{9,8},{10,11... | collective-permute-start | bytes 294920 | tf_op jit(solution)/shard_map/ppermute | solution.py:388
  21.0 0.0 collective-permute-done.4.far_next_in_ref
  21.0 1.6 %collective-permute-start.7 = (f32[2,1,32,128]{3,2,1,0:T(8,128)S(1)}, f32[2,1,32,128]{3,2,1,0:T(8,128)S(1)}, u32[]{:S(2)}, u32[]{:S(2)}) collective-permute-start(f32[2,1,32,128]{3,2,1,0:T(8,128)S(1)} %bitcast.16), channel_id=1, source_target_pairs={{0,1},{1,0},{2,3},{3,2},{4,5},{5,4},{6,7},{7,6},{8,9},{9,8},{10,11... | collective-permute-start | bytes 98312 | tf_op jit(solution)/shard_map/ppermute | solution.py:408
  22.5 1.2 %shard_map.89 = f32[3,8,64,128]{3,2,1,0:T(8,128)} custom-call(f32[8,64,128]{2,1,0:T(8,128)S(1)} %copy-done.2, f32[8,64,128]{2,1,0:T(8,128)S(1)} %copy-done.3, f32[8,64,128]{2,1,0:T(8,128)S(1)} %get-tuple-element.22.scale_v, f32[3,8,64,128]{3,2,1,0:T(8,128)S(1)} %get-tuple-element.28.final_v, f32[6,64,128]{2,1,0:T(8,128)S(1)} %shard_map.87.far_next_ref, ...), custom_call_target="tpu_custom_call" | custom-call | tf_op jit(solution)/shard_map/pallas_call | solution.py:90
  23.7 0.0 collective-permute-done.5.rest_1_
  23.7 2.0 %collective-permute-done.7.rest_5_ = f32[2,1,32,128]{3,2,1,0:T(8,128)S(1)} collective-permute-done((f32[2,1,32,128]{3,2,1,0:T(8,128)S(1)}, f32[2,1,32,128]{3,2,1,0:T(8,128)S(1)}, u32[]{:S(2)}, u32[]{:S(2)}) %collective-permute-start.7) | collective-permute-done | bytes 32800 | tf_op jit(solution)/shard_map/ppermute | solution.py:408
  25.7 0.0 collective-permute-done.6.rest_3_
  25.7 0.7 %shard_map.91 = (f32[8,32,128]{2,1,0:T(8,128)}, f32[8,32,128]{2,1,0:T(8,128)}) custom-call(f32[2,4,32,128]{3,2,1,0:T(8,128)S(1)} %get-tuple-element.29.rest_0_, f32[2,4,32,128]{3,2,1,0:T(8,128)S(1)} %collective-permute-done.5.rest_1_, f32[2,3,32,128]{3,2,1,0:T(8,128)S(1)} %get-tuple-element.31.rest_2_, f32[2,3,32,128]{3,2,1,0:T(8,128)S(1)} %collective-permute-done.6.rest_3_, ...), custom_call_target="tpu_custom_call" | custom-call | tf_op jit(solution)/shard_map/pallas_call | solution.py:90
  (1 shorter events, 0.0 us)
Async XLA Ops:
  0.6 7.7 %copy-start.1 = (f32[1,3,8,64,128]{4,3,2,1,0:T(8,128)S(1)}, f32[1,3,8,64,128]{4,3,2,1,0:T(8,128)}, u32[]{:S(2)}) copy-start(f32[1,3,8,64,128]{4,3,2,1,0:T(8,128)} %param.6) | copy-start | bytes 2359300
  0.6 7.7 %copy-start = (f32[1,2,3,8,64,128]{5,4,3,2,1,0:T(8,128)S(1)}, f32[1,2,3,8,64,128]{5,4,3,2,1,0:T(8,128)}, u32[]{:S(2)}) copy-start(f32[1,2,3,8,64,128]{5,4,3,2,1,0:T(8,128)} %param.8) | copy-start | bytes 4718596
  0.7 7.7 %copy-start.2 = (f32[8,64,128]{2,1,0:T(8,128)S(1)}, f32[8,64,128]{2,1,0:T(8,128)}, u32[]{:S(2)}) copy-start(f32[8,64,128]{2,1,0:T(8,128)} %lame_v.7) | copy-start | bytes 786436
  0.7 7.7 %copy-start.3 = (f32[8,64,128]{2,1,0:T(8,128)S(1)}, f32[8,64,128]{2,1,0:T(8,128)}, u32[]{:S(2)}) copy-start(f32[8,64,128]{2,1,0:T(8,128)} %shear_v.7) | copy-start | bytes 786436
  2.2 6.2 %collective-permute-start = (f32[7,2,64,128]{3,2,1,0:T(8,128)S(1)}, f32[7,2,64,128]{3,2,1,0:T(8,128)S(1)}, u32[]{:S(2)}, u32[]{:S(2)}) collective-permute-start(f32[7,2,64,128]{3,2,1,0:T(8,128)S(1)} %get-tuple-element.21), channel_id=1, source_target_pairs={{0,2},{2,0},{4,6},{6,4},{8,10},{10,8},{12,14},{14,12},{16,18},{18,... | collective-permute-start | bytes 1376264 | tf_op jit(solution)/shard_map/ppermute | solution.py:164
  2.7 9.8 %collective-permute-start.1 = (f32[4,2,64,128]{3,2,1,0:T(8,128)S(1)}, f32[4,2,64,128]{3,2,1,0:T(8,128)S(1)}, u32[]{:S(2)}, u32[]{:S(2)}) collective-permute-start(f32[4,2,64,128]{3,2,1,0:T(8,128)S(1)} %get-tuple-element.25), channel_id=1, source_target_pairs={{0,30},{2,4},{4,2},{6,8},{8,6},{10,12},{12,10},{14,16},{16,14},{18... | collective-permute-start | bytes 786440 | tf_op jit(solution)/shard_map/ppermute | solution.py:165
  8.3 10.4 %collective-permute-start.3 = (f32[2,3,64,128]{3,2,1,0:T(8,128)S(1)}, f32[2,3,64,128]{3,2,1,0:T(8,128)S(1)}, u32[]{:S(2)}, u32[]{:S(2)}) collective-permute-start(f32[2,3,64,128]{3,2,1,0:T(8,128)S(1)} %get-tuple-element.27), channel_id=1, source_target_pairs={{0,30},{2,4},{4,2},{6,8},{8,6},{10,12},{12,10},{14,16},{16,14},{18... | collective-permute-start | bytes 589832 | tf_op jit(solution)/shard_map/ppermute | solution.py:166
  11.6 7.2 %collective-permute-start.2 = (f32[6,64,128]{2,1,0:T(8,128)S(1)}, f32[6,64,128]{2,1,0:T(8,128)S(1)}, u32[]{:S(2)}, u32[]{:S(2)}) collective-permute-start(f32[6,64,128]{2,1,0:T(8,128)S(1)} %get-tuple-element.26), channel_id=1, source_target_pairs={{0,2},{2,0},{4,6},{6,4},{8,10},{10,8},{12,14},{14,12},{16,18},{18,... | collective-permute-start | bytes 589832 | tf_op jit(solution)/shard_map/ppermute | solution.py:266
  12.8 8.2 %collective-permute-start.4 = (f32[6,64,128]{2,1,0:T(8,128)S(1)}, f32[6,64,128]{2,1,0:T(8,128)S(1)}, u32[]{:S(2)}, u32[]{:S(2)}) collective-permute-start(f32[6,64,128]{2,1,0:T(8,128)S(1)} %shard_map.87.far_next_ref), channel_id=1, source_target_pairs={{0,30},{2,4},{4,2},{6,8},{8,6},{10,12},{12,10},{14,16},{16,14},{18... | collective-permute-start | bytes 589832 | tf_op jit(solution)/shard_map/ppermute | solution.py:299
  17.3 6.5 %collective-permute-start.5 = (f32[2,4,32,128]{3,2,1,0:T(8,128)S(1)}, f32[2,4,32,128]{3,2,1,0:T(8,128)S(1)}, u32[]{:S(2)}, u32[]{:S(2)}) collective-permute-start(f32[2,4,32,128]{3,2,1,0:T(8,128)S(1)} %bitcast.14), channel_id=1, source_target_pairs={{0,1},{1,0},{2,3},{3,2},{4,5},{5,4},{6,7},{7,6},{8,9},{9,8},{10,11... | collective-permute-start | bytes 393224 | tf_op jit(solution)/shard_map/ppermute | solution.py:267
  20.4 5.4 %collective-permute-start.6 = (f32[2,3,32,128]{3,2,1,0:T(8,128)S(1)}, f32[2,3,32,128]{3,2,1,0:T(8,128)S(1)}, u32[]{:S(2)}, u32[]{:S(2)}) collective-permute-start(f32[2,3,32,128]{3,2,1,0:T(8,128)S(1)} %bitcast.15), channel_id=1, source_target_pairs={{0,1},{1,0},{2,3},{3,2},{4,5},{5,4},{6,7},{7,6},{8,9},{9,8},{10,11... | collective-permute-start | bytes 294920 | tf_op jit(solution)/shard_map/ppermute | solution.py:388
  21.0 4.8 %collective-permute-start.7 = (f32[2,1,32,128]{3,2,1,0:T(8,128)S(1)}, f32[2,1,32,128]{3,2,1,0:T(8,128)S(1)}, u32[]{:S(2)}, u32[]{:S(2)}) collective-permute-start(f32[2,1,32,128]{3,2,1,0:T(8,128)S(1)} %bitcast.16), channel_id=1, source_target_pairs={{0,1},{1,0},{2,3},{3,2},{4,5},{5,4},{6,7},{7,6},{8,9},{9,8},{10,11... | collective-permute-start | bytes 98312 | tf_op jit(solution)/shard_map/ppermute | solution.py:408

commit v4 on v3

v4 whole, which is shorter than its diff:
```python
import jax
import jax.numpy as jnp
from jax import lax
from jax.experimental import pallas as pl
from jax.experimental.pallas import tpu as pltpu
from jax.sharding import PartitionSpec as P

time_step = 0.3
step_squared = time_step * time_step


def difference_tools(rows, lanes):
    row = lax.broadcasted_iota(jnp.int32, (rows, lanes), 0)
    lane = lax.broadcasted_iota(jnp.int32, (rows, lanes), 1)

    def along_rows(values):
        upper = jnp.where(row == rows - 1, 0.0, pltpu.roll(values, rows - 1, 0))
        lower = jnp.where(row == 0, 0.0, pltpu.roll(values, 1, 0))
        return upper - lower

    def along_lanes(values):
        upper = jnp.where(lane == lanes - 1, 0.0, pltpu.roll(values, lanes - 1, 1))
        lower = jnp.where(lane == 0, 0.0, pltpu.roll(values, 1, 1))
        return upper - lower

    key = lax.broadcasted_iota(jnp.int32, (3 * lanes, lanes), 0) % lanes
    out = lax.broadcasted_iota(jnp.int32, (3 * lanes, lanes), 1)
    weights = ((key == out + 1).astype(jnp.float32) - (key == out - 1).astype(jnp.float32)).astype(jnp.bfloat16)

    def along_lanes_three(fields):
        values = jnp.concatenate(fields, axis=0)
        high = values.astype(jnp.bfloat16)
        rest = values - high.astype(jnp.float32)
        middle = rest.astype(jnp.bfloat16)
        low = (rest - middle.astype(jnp.float32)).astype(jnp.bfloat16)
        parts = jnp.concatenate([high, middle, low], axis=1)
        result = jnp.dot(parts, weights, preferred_element_type=jnp.float32)
        return [result[rows * b : rows * (b + 1)] for b in range(len(fields))]

    return along_rows, along_lanes, along_lanes_three


def strain_parts(before, middle, after, tools):
    along_rows, along_lanes, along_lanes_three = tools
    first = after[0] - before[0]
    second = along_rows(middle[1])
    third = along_lanes(middle[2])
    pair_12 = (after[1] - before[1]) + along_rows(middle[0])
    pair_13 = (after[2] - before[2]) + along_lanes(middle[0])
    pair_23 = along_rows(middle[2]) + along_lanes(middle[1])
    return (first, second, third, pair_12, pair_13, pair_23, first + second + third)


def normal_stress(parts, lame, shear):
    return (2.0 * shear * parts[0] + lame * parts[6], shear * parts[3], shear * parts[4])


def cross_force(parts, normal, lame, shear, tools):
    along_rows, along_lanes, along_lanes_three = tools
    pressure = lame * parts[6]
    twice = 2.0 * shear
    s_22 = twice * parts[1] + pressure
    s_33 = twice * parts[2] + pressure
    s_23 = shear * parts[5]
    third_of = along_lanes_three((normal[2], s_23, s_33))
    return (
        along_rows(normal[1]) + third_of[0],
        along_rows(s_22) + third_of[1],
        along_rows(s_23) + third_of[2],
    )


def term_pair(parts, other, lame, shear):
    straight = parts[0] * other[0] + parts[1] * other[1] + parts[2] * other[2]
    mixed = parts[3] * other[3] + parts[4] * other[4] + parts[5] * other[5]
    traces = parts[6] * other[6]
    shear_term = shear * (
        (-0.5 * time_step) * straight - (0.25 * time_step) * mixed + (time_step / 6.0) * traces
    )
    bulk_term = (-0.25 * time_step) * (lame + (2.0 / 3.0) * shear) * traces
    return shear_term, bulk_term


costs = {'pack': 1000000, 'inner_first': 100000000, 'near_first': 100000000, 'far_first': 10000000000, 'middle_terms': 1000000000, 'edge_terms': 10000000, 'second': 1000000000, 'far_terms': 10000000, 'store_second': 10000000, 'finish': 100000000}


def call(kernel, outs, args, in_spaces, out_spaces, scratch=(), vmem=40 << 20, aliases=None):
    shapes = [
        pltpu.VMEM(shape, jnp.float32) if space is pltpu.VMEM else jax.ShapeDtypeStruct(shape, jnp.float32)
        for shape, space in zip(outs, out_spaces)
    ]
    out_spaces = [space or pltpu.VMEM for space in out_spaces]
    return pl.pallas_call(
        kernel,
        out_shape=shapes,
        in_specs=[pl.BlockSpec(memory_space=space) for space in in_spaces],
        out_specs=[pl.BlockSpec(memory_space=space) for space in out_spaces],
        scratch_shapes=list(scratch),
        name=kernel.__name__,
        input_output_aliases=aliases or {},
        compiler_params=pltpu.CompilerParams(vmem_limit_bytes=vmem),
        cost_estimate=pl.CostEstimate(
            flops=costs.get(kernel.__name__, 1), bytes_accessed=costs.get(kernel.__name__, 1), transcendentals=0
        ),
    )(*args)


def local(adjoint_now, adjoint_prev, forward_field, density, lame_first, shear_modulus):
    slabs = lax.axis_size("blk")
    events = lax.axis_size("event")
    cells, rows, lanes = density.shape
    steps = forward_field.shape[1]
    last = cells - 1
    band = rows // events
    plane = (rows, lanes)
    VM, SM, ANY = pltpu.VMEM, pltpu.SMEM, pl.ANY

    near = [(i, i + 1 - 2 * (i % 2)) for i in range(slabs)]
    far = [(i, (i - 1 + 2 * (i % 2)) % slabs) for i in range(slabs)]
    others = [
        [(i, (i + shift) % events) for i in range(events)] for shift in range(1, events)
    ]

    in_hbm = [
        pltpu.with_memory_space_constraint(x, pltpu.HBM)
        for x in (adjoint_now[0], adjoint_prev[0], forward_field[0], density, lame_first, shear_modulus)
    ]
    now_hbm, prev, forward_hbm, density, lame_hbm, shear_hbm = in_hbm
    now, forward = adjoint_now[0], forward_field[0]

    def where():
        return lax.rem(lax.axis_index("blk"), 2), lax.axis_index("event")

    def layer(place_ref, t):
        return t + place_ref[0] * (last - 2 * t)

    def far_slot(place_ref, n):
        return (1 - n) + place_ref[0] * (2 * n - 1)

    def near_slot(place_ref, n):
        return n + place_ref[0] * (1 - 2 * n)

    def sign(place_ref):
        return (1 - 2 * place_ref[0]).astype(jnp.float32)

    def pack(now_ref, forward_ref, lame_ref, shear_ref, near_ref, far_ref, sem):
        place_ref = where()
        odd = place_ref[0]
        faces = ((far_ref, layer(place_ref, 0), odd * (cells - 2)), (near_ref, layer(place_ref, last), (1 - odd) * (cells - 2)))
        copies = []
        for out, at, low in faces:
            copies.append((now_ref.at[:, pl.ds(low, 2)], out.at[pl.ds(0, 3)]))
            copies.append((lame_ref.at[at], out.at[3, 0]))
            copies.append((shear_ref.at[at], out.at[3, 1]))
        for k in range(steps):
            copies.append((forward_ref.at[k, :, layer(place_ref, last)], near_ref.at[pl.ds(4, 3), k]))
        started = [pltpu.make_async_copy(src, dst, sem.at[i]) for i, (src, dst) in enumerate(copies)]
        for copy in started:
            copy.start()
        for copy in started:
            copy.wait()

    near_out, far_out = call(
        pack,
        [(7, 2, *plane), (4, 2, *plane)],
        (now_hbm, forward_hbm, lame_hbm, shear_hbm),
        [ANY, ANY, ANY, ANY],
        [VM, VM],
        [pltpu.SemaphoreType.DMA((6 + steps,))],
    )
    near_in = lax.ppermute(near_out, "blk", near)
    far_in = lax.ppermute(far_out, "blk", far)

    def split(place_ref, terms_ref, layers, keep_ref, send_ref):
        own = place_ref[1]
        for shift in range(events):
            target = lax.rem(own + shift, events) if shift else own
            start = pl.multiple_of(target * band, 8)
            out = send_ref.at[shift - 1] if shift else keep_ref
            for k in range(2):
                for i, t in enumerate(layers):
                    out[k, i] = terms_ref[k, t, pl.ds(start, band)]

    def inner_first(now_v, prev_ref, fwd_v, dens_ref, lame_v, shear_v,
        scale_v, next_v, terms_v, far_fwd_ref,
        prev_v, dens_v, normal_v, sem,
    ):
        place_ref = where()
        moves = [
            pltpu.make_async_copy(src, dst, sem.at[i])
            for i, (src, dst) in enumerate([(dens_ref, dens_v), (prev_ref, prev_v)])
        ]
        for move in moves:
            move.start()
        sigma = sign(place_ref)
        tools = difference_tools(*plane)

        def at(t):
            return layer(place_ref, t)

        def field(t):
            return (now_v[0, at(t)] * sigma, now_v[1, at(t)], now_v[2, at(t)])

        def fwd(k, t):
            return (fwd_v[k, 0, at(t)] * sigma, fwd_v[k, 1, at(t)], fwd_v[k, 2, at(t)])

        for k in range(steps):
            for b in range(3):
                far_fwd_ref[k, b] = fwd_v[k, b, at(0)]
        for t in range(1, last):
            parts = strain_parts(field(t - 1), field(t), field(t + 1), tools)
            lame, shear = lame_v[at(t)], shear_v[at(t)]
            normal = normal_stress(parts, lame, shear)
            force = cross_force(parts, normal, lame, shear, tools)
            for b in range(3):
                normal_v[b, t] = normal[b]
                next_v[b, t] = force[b]
            other = strain_parts(fwd(0, t - 1), fwd(0, t), fwd(0, t + 1), tools)
            pair = term_pair(parts, other, lame, shear)
            terms_v[0, t] = pair[0]
            terms_v[1, t] = pair[1]
        for move in moves:
            move.wait()
        for t in range(cells):
            scale_v[t] = (0.25 * step_squared) / dens_v[at(t)]
        for t in range(cells):
            for b in range(3):
                force = None
                if 0 < t < last:
                    force = next_v[b, t]
                if t < last - 1:
                    force = normal_v[b, t + 1] if force is None else force + normal_v[b, t + 1]
                if t > 1:
                    force = -normal_v[b, t - 1] if force is None else force - normal_v[b, t - 1]
                old = prev_v[b, at(t)]
                if b == 0:
                    old = old * sigma
                next_v[b, t] = 2.0 * field(t)[b] - old + scale_v[t] * force
        for t in range(3, last - 2):
            fields = [tuple(next_v[b, t + d] for b in range(3)) for d in (-1, 0, 1)]
            parts = strain_parts(*fields, tools)
            other = strain_parts(fwd(1, t - 1), fwd(1, t), fwd(1, t + 1), tools)
            pair = term_pair(parts, other, lame_v[at(t)], shear_v[at(t)])
            for k in range(2):
                terms_v[k, t] = terms_v[k, t] + pair[k]

    now_v, fwd_v, lame_v, shear_v = now, forward, lame_first, shear_modulus
    scale_v, next_v, terms_v, far_fwd_out = call(
        inner_first,
        [density.shape, now.shape, (2, last, *plane), (steps, 3, *plane)],
        (now, prev, forward, density, lame_first, shear_modulus),
        [VM, ANY, VM, ANY, VM, VM],
        [VM] * 4,
        [pltpu.VMEM(now.shape, jnp.float32), pltpu.VMEM(density.shape, jnp.float32),
         pltpu.VMEM((3, last, *plane), jnp.float32), pltpu.SemaphoreType.DMA((2,))],
    )

    far_fwd_in = lax.ppermute(far_fwd_out, "blk", far)

    early = list(range(3, last))
    middle = [1, 2, last]

    def near_first(now_v, fwd_v, lame_v, shear_v, scale_v, next_v, terms_v, near_ref,
        near_next, near_terms, keep_ref, send_ref,
        total_v,
    ):
        place_ref = where()
        sigma = sign(place_ref)
        tools = difference_tools(*plane)

        def at(t):
            return layer(place_ref, t)

        def field(t):
            if t <= last:
                return (now_v[0, at(t)] * sigma, now_v[1, at(t)], now_v[2, at(t)])
            slot = near_slot(place_ref, t - cells)
            return (near_ref[0, slot] * sigma, near_ref[1, slot], near_ref[2, slot])

        def fwd(k, t):
            if t <= last:
                return (fwd_v[k, 0, at(t)] * sigma, fwd_v[k, 1, at(t)], fwd_v[k, 2, at(t)])
            return (near_ref[4, k] * sigma, near_ref[5, k], near_ref[6, k])

        def new(t):
            if t < last - 1:
                return tuple(next_v[b, t] for b in range(3))
            return tuple(near_next[3 * (last - t) + b] for b in range(3))

        outer = normal_stress(
            strain_parts(field(last), field(cells), field(cells + 1), tools), near_ref[3, 0], near_ref[3, 1]
        )
        lame, shear = lame_v[at(last)], shear_v[at(last)]
        parts = strain_parts(field(last - 1), field(last), field(cells), tools)
        normal = normal_stress(parts, lame, shear)
        force = cross_force(parts, normal, lame, shear, tools)
        for b in range(3):
            near_next[b] = next_v[b, last] + scale_v[last] * (force[b] + outer[b])
            near_next[3 + b] = next_v[b, last - 1] + scale_v[last - 1] * normal[b]
        other = strain_parts(fwd(0, last - 1), fwd(0, last), fwd(0, cells), tools)
        pair = term_pair(parts, other, lame, shear)
        for k in range(2):
            near_terms[k] = pair[k]
            for t in range(3, last - 2):
                total_v[k, t] = terms_v[k, t]
        for t in range(last - 2, last):
            parts = strain_parts(new(t - 1), new(t), new(t + 1), tools)
            other = strain_parts(fwd(1, t - 1), fwd(1, t), fwd(1, t + 1), tools)
            pair = term_pair(parts, other, lame_v[at(t)], shear_v[at(t)])
            for k in range(2):
                total_v[k, t] = terms_v[k, t] + pair[k]
        split(place_ref, total_v, early, keep_ref, send_ref)

    near_next, near_terms, keep, send = call(
        near_first,
        [(6, *plane), (2, *plane), (2, len(early), band, lanes), (events - 1, 2, len(early), band, lanes)],
        (now_v, fwd_v, lame_v, shear_v, scale_v, next_v, terms_v, near_in),
        [VM] * 8,
        [VM] * 4,
        [pltpu.VMEM((2, cells, *plane), jnp.float32)],
    )
    near_next_in = lax.ppermute(near_next, "blk", near)
    shared = [lax.ppermute(send[i], "event", others[i]) for i in range(events - 1)]

    def far_first(now_v, lame_v, shear_v, scale_v, next_v, far_ref, after_ref, far_next, far_after):
        place_ref = where()
        sigma = sign(place_ref)
        tools = difference_tools(*plane)

        def at(t):
            return layer(place_ref, t)

        def field(t):
            if t >= 0:
                return (now_v[0, at(t)] * sigma, now_v[1, at(t)], now_v[2, at(t)])
            slot = far_slot(place_ref, -1 - t)
            return (far_ref[0, slot] * sigma, far_ref[1, slot], far_ref[2, slot])

        outer = normal_stress(strain_parts(field(-2), field(-1), field(0), tools), far_ref[3, 0], far_ref[3, 1])
        lame, shear = lame_v[at(0)], shear_v[at(0)]
        parts = strain_parts(field(-1), field(0), field(1), tools)
        normal = normal_stress(parts, lame, shear)
        force = cross_force(parts, normal, lame, shear, tools)
        for b in range(3):
            far_next[b] = next_v[b, 0] + scale_v[0] * (force[b] - outer[b])
            far_after[b] = next_v[b, 1] - scale_v[1] * normal[b]

    far_next, far_after = call(
        far_first,
        [(3, *plane), (3, *plane)],
        (now_v, lame_v, shear_v, scale_v, next_v, far_in, near_next),
        [VM] * 7,
        [VM] * 2,
    )
    far_next_in = lax.ppermute(far_next, "blk", far)
    far_after_in = lax.ppermute(far_after, "blk", far)

    def middle_terms(fwd_v, lame_v, shear_v, next_v, near_next_v, terms_v, near_terms, far_next_ref, far_after_ref, near_next_ref, near_ref,
        keep_ref, send_ref, total_v,
    ):
        place_ref = where()
        sigma = sign(place_ref)
        tools = difference_tools(*plane)

        def at(t):
            return layer(place_ref, t)

        def field(t):
            if t < 2:
                return tuple((far_after_ref if t else far_next_ref)[b] for b in range(3))
            if t < last - 1:
                return tuple(next_v[b, t] for b in range(3))
            if t <= last:
                return tuple(near_next_v[3 * (last - t) + b] for b in range(3))
            base = 3 * (t - cells)
            return (-near_next_ref[base], near_next_ref[base + 1], near_next_ref[base + 2])

        def fwd(k, t):
            if t <= last:
                return (fwd_v[k, 0, at(t)] * sigma, fwd_v[k, 1, at(t)], fwd_v[k, 2, at(t)])
            return (near_ref[4, k] * sigma, near_ref[5, k], near_ref[6, k])

        for t in middle:
            parts = strain_parts(field(t - 1), field(t), field(t + 1), tools)
            other = strain_parts(fwd(1, t - 1), fwd(1, t), fwd(1, t + 1), tools)
            pair = term_pair(parts, other, lame_v[at(t)], shear_v[at(t)])
            for k in range(2):
                total_v[k, t] = (near_terms[k] if t == last else terms_v[k, t]) + pair[k]
        split(place_ref, total_v, middle, keep_ref, send_ref)

    keep_mid, send_mid = call(
        middle_terms,
        [(2, len(middle), band, lanes), (events - 1, 2, len(middle), band, lanes)],
        (fwd_v, lame_v, shear_v, next_v, near_next, terms_v, near_terms, far_next, far_after, near_next_in, near_in),
        [VM] * 11,
        [VM] * 2,
        [pltpu.VMEM((2, cells, *plane), jnp.float32)],
    )
    shared_mid = [lax.ppermute(send_mid[i], "event", others[i]) for i in range(events - 1)]

    def edge_terms(now_v, fwd_v, lame_v, shear_v, far_next_ref, far_after_ref, far_ref, far_fwd_ref, after_ref,
        total_v, slope_v,
    ):
        place_ref = where()
        sigma = sign(place_ref)
        tools = difference_tools(*plane)

        def at(t):
            return layer(place_ref, t)

        def start(t):
            if t >= 0:
                return (now_v[0, at(t)] * sigma, now_v[1, at(t)], now_v[2, at(t)])
            slot = far_slot(place_ref, 0)
            return (far_ref[0, slot] * sigma, far_ref[1, slot], far_ref[2, slot])

        def field(t):
            return tuple((far_after_ref if t else far_next_ref)[b] for b in range(3))

        def fwd(k, t):
            if t < 0:
                return (far_fwd_ref[k, 0] * sigma, far_fwd_ref[k, 1], far_fwd_ref[k, 2])
            return (fwd_v[k, 0, at(t)] * sigma, fwd_v[k, 1, at(t)], fwd_v[k, 2, at(t)])

        parts = strain_parts(start(-1), start(0), start(1), tools)
        other = strain_parts(fwd(0, -1), fwd(0, 0), fwd(0, 1), tools)
        lame, shear = lame_v[at(0)], shear_v[at(0)]
        pair = term_pair(parts, other, lame, shear)
        empty = jnp.zeros(plane, jnp.float32)
        parts = strain_parts((empty, empty, empty), field(0), field(1), tools)
        other = strain_parts(fwd(1, -1), fwd(1, 0), fwd(1, 1), tools)
        rest = term_pair(parts, other, lame, shear)
        for k in range(2):
            total_v[k] = pair[k] + rest[k]
        slope_v[0] = shear * ((0.5 * time_step) * other[0] - (time_step / 6.0) * other[6])
        slope_v[1] = (0.25 * time_step) * shear * other[3]
        slope_v[2] = (0.25 * time_step) * shear * other[4]
        slope_v[3] = (0.25 * time_step) * (lame + (2.0 / 3.0) * shear) * other[6]

    total_v, slope_v = call(
        edge_terms,
        [(2, *plane), (4, *plane)],
        (now_v, fwd_v, lame_v, shear_v, far_next, far_after, far_in, far_fwd_in, keep_mid),
        [VM] * 9,
        [VM] * 2,
    )

    def far_terms(total_ref, slope_ref, far_next_in_ref, keep_ref, send_ref, total_v):
        place_ref = where()
        outer = (-far_next_in_ref[0], far_next_in_ref[1], far_next_in_ref[2])
        shear_part = total_ref[0]
        for b in range(3):
            shear_part = shear_part + slope_ref[b] * outer[b]
        total_v[0, 0] = shear_part
        total_v[1, 0] = total_ref[1] + slope_ref[3] * outer[0]
        split(place_ref, total_v, [0], keep_ref, send_ref)

    far_keep, far_send = call(
        far_terms,
        [(2, 1, band, lanes), (events - 1, 2, 1, band, lanes)],
        (total_v, slope_v, far_next_in),
        [VM] * 3,
        [VM] * 2,
        [pltpu.VMEM((2, 1, *plane), jnp.float32)],
    )
    far_shared = [lax.ppermute(far_send[i], "event", others[i]) for i in range(events - 1)]

    def second(now_v, lame_v, shear_v, scale_v, next_v, near_next_v, far_next_ref, far_after_ref, near_next_ref,
        near_ref, after_ref,
        final_v, face_v, normal_v, cross_v,
    ):
        place_ref = where()
        sigma = sign(place_ref)
        tools = difference_tools(*plane)

        def at(t):
            return layer(place_ref, t)

        def field(t):
            if t < 2:
                return tuple((far_after_ref if t else far_next_ref)[b] for b in range(3))
            if t < last - 1:
                return tuple(next_v[b, t] for b in range(3))
            if t <= last:
                return tuple(near_next_v[3 * (last - t) + b] for b in range(3))
            base = 3 * (t - cells)
            return (-near_next_ref[base], near_next_ref[base + 1], near_next_ref[base + 2])

        for t in range(1, cells + 1):
            parts = strain_parts(field(t - 1), field(t), field(t + 1), tools)
            if t <= last:
                lame, shear = lame_v[at(t)], shear_v[at(t)]
            else:
                lame, shear = near_ref[3, 0], near_ref[3, 1]
            normal = normal_stress(parts, lame, shear)
            for b in range(3):
                normal_v[b, t] = normal[b]
            if t <= last:
                force = cross_force(parts, normal, lame, shear, tools)
                for b in range(3):
                    cross_v[b, t] = force[b]
        for t in range(cells):
            for b in range(3):
                force = normal_v[b, t + 1]
                if t > 0:
                    force = force + cross_v[b, t]
                if t > 1:
                    force = force - normal_v[b, t - 1]
                old = now_v[b, at(t)]
                if b == 0:
                    old = old * sigma
                value = 2.0 * field(t)[b] - old + scale_v[t] * force
                if t < 2:
                    face_v[b, t] = value
                else:
                    final_v[b, at(t)] = value * sigma if b == 0 else value

    final_v, face_v = call(
        second,
        [now.shape, (3, 2, *plane)],
        (now_v, lame_v, shear_v, scale_v, next_v, near_next, far_next, far_after, near_next_in,
         near_in, far_keep),
        [VM] * 11,
        [VM] * 2,
        [pltpu.VMEM((3, cells + 1, *plane), jnp.float32), pltpu.VMEM(now.shape, jnp.float32)],
    )

    def store_second(final_v, out_ref, sem):
        place_ref = where()
        inner = pl.ds(2 - 2 * place_ref[0], cells - 2)
        copy = pltpu.make_async_copy(final_v.at[:, inner], out_ref.at[:, inner], sem)
        copy.start()
        copy.wait()

    (result,) = call(
        store_second, [now.shape], (final_v,), [VM], [ANY], [pltpu.SemaphoreType.DMA(())]
    )

    def finish(result_ref, lame_v, shear_v, scale_v, face_v, far_next_ref, far_after_ref, far_ref,
        far_next_in_ref, far_after_in_ref, *rest,
    ):
        pieces, (out_ref, *band_refs, edge_v, band_v, sem) = rest[: 3 * events], rest[3 * events :]
        place_ref = where()
        sigma = sign(place_ref)
        tools = difference_tools(*plane)

        def at(t):
            return layer(place_ref, t)

        def field(t):
            if t < 0:
                come = far_next_in_ref if t == -1 else far_after_in_ref
                return (-come[0], come[1], come[2])
            return tuple((far_after_ref if t else far_next_ref)[b] for b in range(3))

        outer = normal_stress(strain_parts(field(-2), field(-1), field(0), tools), far_ref[3, 0], far_ref[3, 1])
        lame, shear = lame_v[at(0)], shear_v[at(0)]
        parts = strain_parts(field(-1), field(0), field(1), tools)
        normal = normal_stress(parts, lame, shear)
        force = cross_force(parts, normal, lame, shear, tools)
        odd = place_ref[0]
        for b in range(3):
            first = face_v[b, 0] + scale_v[0] * (force[b] - outer[b])
            after = face_v[b, 1] - scale_v[1] * normal[b]
            edge_v[b, odd] = first * sigma if b == 0 else first
            edge_v[b, 1 - odd] = after * sigma if b == 0 else after
        copies = [pltpu.make_async_copy(edge_v, out_ref.at[:, pl.ds(odd * (cells - 2), 2)], sem.at[0])]
        copies[0].start()
        for k in range(2):
            for i, layers in enumerate((early, middle, [0])):
                own, *others_parts = pieces[i * events : (i + 1) * events]
                for j, t in enumerate(layers):
                    value = own[k, j]
                    for part in others_parts:
                        value = value + part[k, j]
                    band_v[k, at(t)] = value
            copies.append(pltpu.make_async_copy(band_v.at[k], band_refs[k], sem.at[1 + k]))
            copies[-1].start()
        for copy in copies:
            copy.wait()

    result, band_shear, band_bulk = call(
        finish,
        [now.shape, (cells, band, lanes), (cells, band, lanes)],
        (result, lame_v, shear_v, scale_v, face_v, far_next, far_after, far_in, far_next_in, far_after_in,
         keep, *shared, keep_mid, *shared_mid, far_keep, *far_shared),
        [ANY] + [VM] * (9 + 3 * events),
        [ANY] * 3,
        [pltpu.VMEM((3, 2, *plane), jnp.float32), pltpu.VMEM((2, cells, band, lanes), jnp.float32),
         pltpu.SemaphoreType.DMA((3,))],
        aliases={0: 0},
    )
    return (result[None], band_shear, band_bulk)


def solution(mesh):
    in_specs = (
        P("event", None, "blk", None, None),
        P("event", None, "blk", None, None),
        P("event", None, None, "blk", None, None),
        P("blk", None, None),
        P("blk", None, None),
        P("blk", None, None),
    )
    out_specs = (
        P("event", None, "blk", None, None),
        P("blk", "event", None),
        P("blk", "event", None),
    )
    return jax.shard_map(local, mesh=mesh, in_specs=in_specs, out_specs=out_specs, check_vma=False)
```

time: 26.6 us -> 25.8 us (0.970)
  waiting for transfers between devices: 2.87 us -> 1.47 us
  Pallas kernels: 8.43 us -> 8.83 us
    ppermute x1, waiting for transfers between devices: 2 us -> 0.61 us  [local(): lax.ppermute(far_send[i], 'event', others[i])]
    pallas_call x7 -> x10, Pallas kernels: 8.43 us -> 8.83 us  [call(): pl.pallas_call(kernel, out_shape=shapes, in_specs=[pl.BlockSpec(memory_sp...]
    ppermute x1, waiting for transfers between devices: 0.85 us -> 0.52 us  [local(): far_in = lax.ppermute(far_out, 'blk', far)]
    ppermute x0 -> x1, waiting for transfers between devices: none -> 0.33 us  [local(): far_after_in = lax.ppermute(far_after, 'blk', far)]
  transfers between devices with their start and end apart: 8 -> 9, of which waited for: 2 -> 3; matrix products, arithmetic and copies ran while one was open for 0% -> 0% of each run, Pallas kernels for 23% -> 25%
where the time goes in v4:
time: 25.8 us; the launch traced here: 25.6 us
  starting transfers between devices  14.6 us (57%)
  Pallas kernels  8.83 us (34%)
  waiting for transfers between devices  1.47 us (6%)
  between operations  0.75 us (3%)
    pallas_call x10, Pallas kernels, call(): pl.pallas_call(kernel, out_shape=shapes, in_specs=[pl.BlockSpec(memory_sp...  8.83 us
    ppermute x1, starting transfers between devices, local(): far_in = lax.ppermute(far_out, 'blk', far)  5.67 us
    ppermute x1, starting transfers between devices, local(): far_next_in = lax.ppermute(far_next, 'blk', far)  4.5 us
    ppermute x1, starting transfers between devices, local(): lax.ppermute(far_send[i], 'event', others[i])  1.56 us
    ppermute x1, starting transfers between devices, local(): lax.ppermute(send[i], 'event', others[i])  1.49 us
    ppermute x1, waiting for transfers between devices, local(): lax.ppermute(far_send[i], 'event', others[i])  0.61 us
    ppermute x1, starting transfers between devices, local(): lax.ppermute(send_mid[i], 'event', others[i])  0.6 us
    ppermute x1, waiting for transfers between devices, local(): far_in = lax.ppermute(far_out, 'blk', far)  0.52 us
  transfers between devices with their start and end apart: 9, of which 3 were waited for; matrix products, arithmetic and copies ran while one was open for 0% of the time, Pallas kernels for 25%

profile of v4, /device:TPU:0, one launch (start us, length us, event | category | flops | bytes accessed | tf_op | source)
XLA Modules:
  0.0 25.6 jit_solution(3806718725708710524)
XLA Ops:
  0.6 0.0 copy-start.1
  0.6 0.0 copy-start
  0.7 0.0 copy-start.2
  0.7 0.0 copy-start.3
  0.7 1.4 %pack.1 = (f32[7,2,64,128]{3,2,1,0:T(8,128)S(1)}, f32[4,2,64,128]{3,2,1,0:T(8,128)S(1)}) custom-call(f32[3,8,64,128]{3,2,1,0:T(8,128)} %bitcast.12, f32[2,3,8,64,128]{4,3,2,1,0:T(8,128)} %bitcast.7, f32[8,64,128]{2,1,0:T(8,128)} %lame_v.13, f32[8,64,128]{2,1,0:T(8,128)} %shear_v.13), custom_call_target="tpu_custom_call" | custom-call | flops 1000000 | bytes 1000000 | tf_op jit(solution)/shard_map/pack/pallas_call | solution.py:93
  2.1 0.5 %collective-permute-start = (f32[7,2,64,128]{3,2,1,0:T(8,128)S(1)}, f32[7,2,64,128]{3,2,1,0:T(8,128)S(1)}, u32[]{:S(2)}, u32[]{:S(2)}) collective-permute-start(f32[7,2,64,128]{3,2,1,0:T(8,128)S(1)} %get-tuple-element.29), channel_id=1, source_target_pairs={{0,2},{2,0},{4,6},{6,4},{8,10},{10,8},{12,14},{14,12},{16,18},{18,... | collective-permute-start | bytes 1376264 | tf_op jit(solution)/shard_map/ppermute | solution.py:171
  2.6 5.7 %collective-permute-start.1 = (f32[4,2,64,128]{3,2,1,0:T(8,128)S(1)}, f32[4,2,64,128]{3,2,1,0:T(8,128)S(1)}, u32[]{:S(2)}, u32[]{:S(2)}) collective-permute-start(f32[4,2,64,128]{3,2,1,0:T(8,128)S(1)} %get-tuple-element.31), channel_id=1, source_target_pairs={{0,30},{2,4},{4,2},{6,8},{8,6},{10,12},{12,10},{14,16},{16,14},{18... | collective-permute-start | bytes 786440 | tf_op jit(solution)/shard_map/ppermute | solution.py:172
  8.3 0.0 copy-done.1
  8.3 0.0 copy-done
  8.3 0.0 copy-done.2
  8.3 0.0 copy-done.3
  8.3 2.8 %inner_first.1 = (f32[8,64,128]{2,1,0:T(8,128)S(1)}, f32[3,8,64,128]{3,2,1,0:T(8,128)S(1)}, f32[2,7,64,128]{3,2,1,0:T(8,128)S(1)}, f32[2,3,64,128]{3,2,1,0:T(8,128)S(1)}) custom-call(f32[3,8,64,128]{3,2,1,0:T(8,128)S(1)} %bitcast.13, f32[3,8,64,128]{3,2,1,0:T(8,128)} %bitcast.22, f32[2,3,8,64,128]{4,3,2,1,0:T(8,128)S(1)} %bitcast.8, f32[8,64,128]{2,1,0:T(8,128)} %dens_ref.1, ...), custom_call_target="tpu_custom_call" | custom-call | flops 100000000 | bytes 100000000 | tf_op jit(solution)/shard_map/inner_first/pallas_call | solution.py:93
  11.1 0.1 collective-permute-start.3
  11.2 0.0 collective-permute-done.near_ref
  11.2 0.6 %near_first.1 = (f32[6,64,128]{2,1,0:T(8,128)S(1)}, f32[2,64,128]{2,1,0:T(8,128)S(1)}, f32[2,4,32,128]{3,2,1,0:T(8,128)S(1)}, f32[1,2,4,32,128]{4,3,2,1,0:T(8,128)S(1)}) custom-call(f32[3,8,64,128]{3,2,1,0:T(8,128)S(1)} %bitcast.14, f32[2,3,8,64,128]{4,3,2,1,0:T(8,128)S(1)} %bitcast.9, f32[8,64,128]{2,1,0:T(8,128)S(1)} %copy-done.2, ...), custom_call_target="tpu_custom_call" | custom-call | flops 100000000 | bytes 100000000 | tf_op jit(solution)/shard_map/near_first/pallas_call | solution.py:93
  11.8 0.1 collective-permute-start.2
  11.9 0.5 %collective-permute-done.1.far_ref = f32[4,2,64,128]{3,2,1,0:T(8,128)S(1)} collective-permute-done((f32[4,2,64,128]{3,2,1,0:T(8,128)S(1)}, f32[4,2,64,128]{3,2,1,0:T(8,128)S(1)}, u32[]{:S(2)}, u32[]{:S(2)}) %collective-permute-start.1) | collective-permute-done | bytes 262176 | tf_op jit(solution)/shard_map/ppermute | solution.py:172
  12.4 0.3 %far_first.1 = (f32[3,64,128]{2,1,0:T(8,128)S(1)}, f32[3,64,128]{2,1,0:T(8,128)S(1)}) custom-call(f32[3,8,64,128]{3,2,1,0:T(8,128)S(1)} %bitcast.15, f32[8,64,128]{2,1,0:T(8,128)S(1)} %copy-done.2, f32[8,64,128]{2,1,0:T(8,128)S(1)} %copy-done.3, f32[8,64,128]{2,1,0:T(8,128)S(1)} %get-tuple-element.26.scale_v, ...), custom_call_target="tpu_custom_call" | custom-call | flops 10000000000 | bytes 10000000000 | tf_op jit(solution)/shard_map/far_first/pallas_call | solution.py:93
  12.7 4.5 %collective-permute-start.4 = (f32[3,64,128]{2,1,0:T(8,128)S(1)}, f32[3,64,128]{2,1,0:T(8,128)S(1)}, u32[]{:S(2)}, u32[]{:S(2)}) collective-permute-start(f32[3,64,128]{2,1,0:T(8,128)S(1)} %get-tuple-element.32.far_next_ref), channel_id=1, source_target_pairs={{0,30},{2,4},{4,2},{6,8},{8,6},{10,12},{12,10},{14,16},{16,14},{18... | collective-permute-start | bytes 294920 | tf_op jit(solution)/shard_map/ppermute | solution.py:355
  17.2 0.1 collective-permute-start.5
  17.3 1.5 %collective-permute-start.6 = (f32[2,4,32,128]{3,2,1,0:T(8,128)S(1)}, f32[2,4,32,128]{3,2,1,0:T(8,128)S(1)}, u32[]{:S(2)}, u32[]{:S(2)}) collective-permute-start(f32[2,4,32,128]{3,2,1,0:T(8,128)S(1)} %bitcast.18), channel_id=1, source_target_pairs={{0,1},{1,0},{2,3},{3,2},{4,5},{5,4},{6,7},{7,6},{8,9},{9,8},{10,11... | collective-permute-start | bytes 393224 | tf_op jit(solution)/shard_map/ppermute | solution.py:323
  18.8 0.0 collective-permute-done.2.near_next_ref
  18.8 0.5 %middle_terms.1 = (f32[2,3,32,128]{3,2,1,0:T(8,128)S(1)}, f32[1,2,3,32,128]{4,3,2,1,0:T(8,128)S(1)}) custom-call(f32[2,3,8,64,128]{4,3,2,1,0:T(8,128)S(1)} %bitcast.10, f32[8,64,128]{2,1,0:T(8,128)S(1)} %copy-done.2, f32[8,64,128]{2,1,0:T(8,128)S(1)} %copy-done.3, f32[3,8,64,128]{3,2,1,0:T(8,128)S(1)} %get-tuple-element.27.next_v, ...), custom_call_target="tpu_custom_call" | custom-call | flops 1000000000 | bytes 1000000000 | tf_op jit(solution)/shard_map/middle_terms/pallas_call | solution.py:93
  19.3 0.6 %collective-permute-start.7 = (f32[2,3,32,128]{3,2,1,0:T(8,128)S(1)}, f32[2,3,32,128]{3,2,1,0:T(8,128)S(1)}, u32[]{:S(2)}, u32[]{:S(2)}) collective-permute-start(f32[2,3,32,128]{3,2,1,0:T(8,128)S(1)} %bitcast.19), channel_id=1, source_target_pairs={{0,1},{1,0},{2,3},{3,2},{4,5},{5,4},{6,7},{7,6},{8,9},{9,8},{10,11... | collective-permute-start | bytes 294920 | tf_op jit(solution)/shard_map/ppermute | solution.py:399
  19.9 0.0 collective-permute-done.3.far_fwd_ref
  19.9 0.3 %edge_terms.1 = (f32[2,64,128]{2,1,0:T(8,128)S(1)}, f32[4,64,128]{2,1,0:T(8,128)S(1)}) custom-call(f32[3,8,64,128]{3,2,1,0:T(8,128)S(1)} %bitcast.16, f32[2,3,8,64,128]{4,3,2,1,0:T(8,128)S(1)} %bitcast.11, f32[8,64,128]{2,1,0:T(8,128)S(1)} %copy-done.2, f32[8,64,128]{2,1,0:T(8,128)S(1)} %copy-done.3, f32[3,64,128]{2,1,0:T(8,128)S(1)} %get-tuple-element.32.far_next_ref, ...), custom_call_target="tpu_custom_call" | custom-call | flops 10000000 | bytes 10000000 | tf_op jit(solution)/shard_map/edge_terms/pallas_call | solution.py:93
  20.2 0.0 collective-permute-done.4.far_next_in_ref
  20.2 1.6 %collective-permute-start.8 = (f32[2,1,32,128]{3,2,1,0:T(8,128)S(1)}, f32[2,1,32,128]{3,2,1,0:T(8,128)S(1)}, u32[]{:S(2)}, u32[]{:S(2)}) collective-permute-start(f32[2,1,32,128]{3,2,1,0:T(8,128)S(1)} %bitcast.20), channel_id=1, source_target_pairs={{0,1},{1,0},{2,3},{3,2},{4,5},{5,4},{6,7},{7,6},{8,9},{9,8},{10,11... | collective-permute-start | bytes 98312 | tf_op jit(solution)/shard_map/ppermute | solution.py:466
  21.8 1.0 %second.1 = (f32[3,8,64,128]{3,2,1,0:T(8,128)S(1)}, f32[3,2,64,128]{3,2,1,0:T(8,128)S(1)}) custom-call(f32[3,8,64,128]{3,2,1,0:T(8,128)S(1)} %bitcast.17, f32[8,64,128]{2,1,0:T(8,128)S(1)} %copy-done.2, f32[8,64,128]{2,1,0:T(8,128)S(1)} %copy-done.3, f32[8,64,128]{2,1,0:T(8,128)S(1)} %get-tuple-element.26.scale_v, ...), custom_call_target="tpu_custom_call" | custom-call | flops 1000000000 | bytes 1000000000 | tf_op jit(solution)/shard_map/second/pallas_call | solution.py:93
  22.8 0.8 %store_second.1.result_ref = f32[3,8,64,128]{3,2,1,0:T(8,128)} custom-call(f32[3,8,64,128]{3,2,1,0:T(8,128)S(1)} %get-tuple-element.40.final_v), custom_call_target="tpu_custom_call" | custom-call | flops 10000000 | bytes 10000000 | tf_op jit(solution)/shard_map/store_second/pallas_call | solution.py:93
  23.6 0.3 %collective-permute-done.5.far_after_in_ref = f32[3,64,128]{2,1,0:T(8,128)S(1)} collective-permute-done((f32[3,64,128]{2,1,0:T(8,128)S(1)}, f32[3,64,128]{2,1,0:T(8,128)S(1)}, u32[]{:S(2)}, u32[]{:S(2)}) %collective-permute-start.5) | collective-permute-done | bytes 98336 | tf_op jit(solution)/shard_map/ppermute | solution.py:356
  24.0 0.0 collective-permute-done.6.rest_1_
  24.0 0.6 %collective-permute-done.8.rest_5_ = f32[2,1,32,128]{3,2,1,0:T(8,128)S(1)} collective-permute-done((f32[2,1,32,128]{3,2,1,0:T(8,128)S(1)}, f32[2,1,32,128]{3,2,1,0:T(8,128)S(1)}, u32[]{:S(2)}, u32[]{:S(2)}) %collective-permute-start.8) | collective-permute-done | bytes 32800 | tf_op jit(solution)/shard_map/ppermute | solution.py:466
  24.6 0.0 collective-permute-done.7.rest_3_
  24.6 1.1 %finish.1 = (f32[3,8,64,128]{3,2,1,0:T(8,128)}, f32[8,32,128]{2,1,0:T(8,128)}, f32[8,32,128]{2,1,0:T(8,128)}) custom-call(f32[3,8,64,128]{3,2,1,0:T(8,128)} %store_second.1.result_ref, f32[8,64,128]{2,1,0:T(8,128)S(1)} %copy-done.2, f32[8,64,128]{2,1,0:T(8,128)S(1)} %copy-done.3, ...), custom_call_target="tpu_custom_call", output_to_operand_aliasing={{0}: (0, {})} | custom-call | flops 100000000 | bytes 100000000 | tf_op jit(solution)/shard_map/finish/pallas_call | solution.py:93
  (1 shorter events, 0.0 us)
Async XLA Ops:
  0.6 7.6 %copy-start.1 = (f32[1,3,8,64,128]{4,3,2,1,0:T(8,128)S(1)}, f32[1,3,8,64,128]{4,3,2,1,0:T(8,128)}, u32[]{:S(2)}) copy-start(f32[1,3,8,64,128]{4,3,2,1,0:T(8,128)} %param.6) | copy-start | bytes 2359300
  0.6 7.6 %copy-start = (f32[1,2,3,8,64,128]{5,4,3,2,1,0:T(8,128)S(1)}, f32[1,2,3,8,64,128]{5,4,3,2,1,0:T(8,128)}, u32[]{:S(2)}) copy-start(f32[1,2,3,8,64,128]{5,4,3,2,1,0:T(8,128)} %param.8) | copy-start | bytes 4718596
  0.7 7.6 %copy-start.2 = (f32[8,64,128]{2,1,0:T(8,128)S(1)}, f32[8,64,128]{2,1,0:T(8,128)}, u32[]{:S(2)}) copy-start(f32[8,64,128]{2,1,0:T(8,128)} %lame_v.13) | copy-start | bytes 786436
  0.7 7.6 %copy-start.3 = (f32[8,64,128]{2,1,0:T(8,128)S(1)}, f32[8,64,128]{2,1,0:T(8,128)}, u32[]{:S(2)}) copy-start(f32[8,64,128]{2,1,0:T(8,128)} %shear_v.13) | copy-start | bytes 786436
  2.1 9.1 %collective-permute-start = (f32[7,2,64,128]{3,2,1,0:T(8,128)S(1)}, f32[7,2,64,128]{3,2,1,0:T(8,128)S(1)}, u32[]{:S(2)}, u32[]{:S(2)}) collective-permute-start(f32[7,2,64,128]{3,2,1,0:T(8,128)S(1)} %get-tuple-element.29), channel_id=1, source_target_pairs={{0,2},{2,0},{4,6},{6,4},{8,10},{10,8},{12,14},{14,12},{16,18},{18,... | collective-permute-start | bytes 1376264 | tf_op jit(solution)/shard_map/ppermute | solution.py:171
  2.6 9.8 %collective-permute-start.1 = (f32[4,2,64,128]{3,2,1,0:T(8,128)S(1)}, f32[4,2,64,128]{3,2,1,0:T(8,128)S(1)}, u32[]{:S(2)}, u32[]{:S(2)}) collective-permute-start(f32[4,2,64,128]{3,2,1,0:T(8,128)S(1)} %get-tuple-element.31), channel_id=1, source_target_pairs={{0,30},{2,4},{4,2},{6,8},{8,6},{10,12},{12,10},{14,16},{16,14},{18... | collective-permute-start | bytes 786440 | tf_op jit(solution)/shard_map/ppermute | solution.py:172
  11.1 8.8 %collective-permute-start.3 = (f32[2,3,64,128]{3,2,1,0:T(8,128)S(1)}, f32[2,3,64,128]{3,2,1,0:T(8,128)S(1)}, u32[]{:S(2)}, u32[]{:S(2)}) collective-permute-start(f32[2,3,64,128]{3,2,1,0:T(8,128)S(1)} %get-tuple-element.34), channel_id=1, source_target_pairs={{0,30},{2,4},{4,2},{6,8},{8,6},{10,12},{12,10},{14,16},{16,14},{18... | collective-permute-start | bytes 589832 | tf_op jit(solution)/shard_map/ppermute | solution.py:258
  11.8 7.0 %collective-permute-start.2 = (f32[6,64,128]{2,1,0:T(8,128)S(1)}, f32[6,64,128]{2,1,0:T(8,128)S(1)}, u32[]{:S(2)}, u32[]{:S(2)}) collective-permute-start(f32[6,64,128]{2,1,0:T(8,128)S(1)} %get-tuple-element.30.after_ref.near_next_v), channel_id=1, source_target_pairs={{0,2},{2,0},{4,6},{6,4},{8,10},{10,8},{12,14},{14,12},{16,18},{18,... | collective-permute-start | bytes 589832 | tf_op jit(solution)/shard_map/ppermute | solution.py:322
  12.7 7.5 %collective-permute-start.4 = (f32[3,64,128]{2,1,0:T(8,128)S(1)}, f32[3,64,128]{2,1,0:T(8,128)S(1)}, u32[]{:S(2)}, u32[]{:S(2)}) collective-permute-start(f32[3,64,128]{2,1,0:T(8,128)S(1)} %get-tuple-element.32.far_next_ref), channel_id=1, source_target_pairs={{0,30},{2,4},{4,2},{6,8},{8,6},{10,12},{12,10},{14,16},{16,14},{18... | collective-permute-start | bytes 294920 | tf_op jit(solution)/shard_map/ppermute | solution.py:355
  17.2 6.7 %collective-permute-start.5 = (f32[3,64,128]{2,1,0:T(8,128)S(1)}, f32[3,64,128]{2,1,0:T(8,128)S(1)}, u32[]{:S(2)}, u32[]{:S(2)}) collective-permute-start(f32[3,64,128]{2,1,0:T(8,128)S(1)} %get-tuple-element.33.far_after_ref), channel_id=1, source_target_pairs={{0,30},{2,4},{4,2},{6,8},{8,6},{10,12},{12,10},{14,16},{16,14},{18... | collective-permute-start | bytes 294920 | tf_op jit(solution)/shard_map/ppermute | solution.py:356
  17.3 6.7 %collective-permute-start.6 = (f32[2,4,32,128]{3,2,1,0:T(8,128)S(1)}, f32[2,4,32,128]{3,2,1,0:T(8,128)S(1)}, u32[]{:S(2)}, u32[]{:S(2)}) collective-permute-start(f32[2,4,32,128]{3,2,1,0:T(8,128)S(1)} %bitcast.18), channel_id=1, source_target_pairs={{0,1},{1,0},{2,3},{3,2},{4,5},{5,4},{6,7},{7,6},{8,9},{9,8},{10,11... | collective-permute-start | bytes 393224 | tf_op jit(solution)/shard_map/ppermute | solution.py:323
  19.3 5.3 %collective-permute-start.7 = (f32[2,3,32,128]{3,2,1,0:T(8,128)S(1)}, f32[2,3,32,128]{3,2,1,0:T(8,128)S(1)}, u32[]{:S(2)}, u32[]{:S(2)}) collective-permute-start(f32[2,3,32,128]{3,2,1,0:T(8,128)S(1)} %bitcast.19), channel_id=1, source_target_pairs={{0,1},{1,0},{2,3},{3,2},{4,5},{5,4},{6,7},{7,6},{8,9},{9,8},{10,11... | collective-permute-start | bytes 294920 | tf_op jit(solution)/shard_map/ppermute | solution.py:399
  20.2 4.3 %collective-permute-start.8 = (f32[2,1,32,128]{3,2,1,0:T(8,128)S(1)}, f32[2,1,32,128]{3,2,1,0:T(8,128)S(1)}, u32[]{:S(2)}, u32[]{:S(2)}) collective-permute-start(f32[2,1,32,128]{3,2,1,0:T(8,128)S(1)} %bitcast.20), channel_id=1, source_target_pairs={{0,1},{1,0},{2,3},{3,2},{4,5},{5,4},{6,7},{7,6},{8,9},{9,8},{10,11... | collective-permute-start | bytes 98312 | tf_op jit(solution)/shard_map/ppermute | solution.py:466

commit v5 on v4

--- a/solution.py
+++ b/solution.py
@@ -81,7 +81,7 @@
     return shear_term, bulk_term
 
 
-costs = {'pack': 1000000, 'inner_first': 100000000, 'near_first': 100000000, 'far_first': 10000000000, 'middle_terms': 1000000000, 'edge_terms': 10000000, 'second': 1000000000, 'far_terms': 10000000, 'store_second': 10000000, 'finish': 100000000}
+costs = {'pack': 1000000000, 'inner_first': 1000000000, 'near_first': 1000000, 'far_first': 10000000000, 'middle_terms': 10000000, 'edge_terms': 10000000, 'second': 100000000, 'far_terms': 10000000000, 'store_second': 100000000, 'far_second': 10000000000, 'finish': 100000}
 
 
 def call(kernel, outs, args, in_spaces, out_spaces, scratch=(), vmem=40 << 20, aliases=None):
@@ -143,32 +143,37 @@
     def sign(place_ref):
         return (1 - 2 * place_ref[0]).astype(jnp.float32)
 
-    def pack(now_ref, forward_ref, lame_ref, shear_ref, near_ref, far_ref, sem):
+    def pack(now_ref, forward_ref, lame_ref, shear_ref, near_ref, near_model_ref, near_fwd_ref, far_ref, sem):
         place_ref = where()
         odd = place_ref[0]
-        faces = ((far_ref, layer(place_ref, 0), odd * (cells - 2)), (near_ref, layer(place_ref, last), (1 - odd) * (cells - 2)))
-        copies = []
-        for out, at, low in faces:
-            copies.append((now_ref.at[:, pl.ds(low, 2)], out.at[pl.ds(0, 3)]))
-            copies.append((lame_ref.at[at], out.at[3, 0]))
-            copies.append((shear_ref.at[at], out.at[3, 1]))
-        for k in range(steps):
-            copies.append((forward_ref.at[k, :, layer(place_ref, last)], near_ref.at[pl.ds(4, 3), k]))
+        at, low = layer(place_ref, 0), odd * (cells - 2)
+        copies = [
+            (now_ref.at[:, pl.ds(low, 2)], far_ref.at[pl.ds(0, 3)]),
+            (lame_ref.at[at], far_ref.at[3, 0]),
+            (shear_ref.at[at], far_ref.at[3, 1]),
+        ]
+        at, low = layer(place_ref, last), (1 - odd) * (cells - 2)
+        copies.append((now_ref.at[:, pl.ds(low, 2)], near_ref))
+        copies.append((lame_ref.at[at], near_model_ref.at[0]))
+        copies.append((shear_ref.at[at], near_model_ref.at[1]))
+        copies.append((forward_ref.at[:, :, layer(place_ref, last)], near_fwd_ref))
         started = [pltpu.make_async_copy(src, dst, sem.at[i]) for i, (src, dst) in enumerate(copies)]
         for copy in started:
             copy.start()
         for copy in started:
             copy.wait()
 
-    near_out, far_out = call(
+    near_out, near_model_out, near_fwd_out, far_out = call(
         pack,
-        [(7, 2, *plane), (4, 2, *plane)],
+        [(3, 2, *plane), (2, *plane), (steps, 3, *plane), (4, 2, *plane)],
         (now_hbm, forward_hbm, lame_hbm, shear_hbm),
         [ANY, ANY, ANY, ANY],
-        [VM, VM],
-        [pltpu.SemaphoreType.DMA((6 + steps,))],
+        [VM] * 4,
+        [pltpu.SemaphoreType.DMA((7,))],
     )
     near_in = lax.ppermute(near_out, "blk", near)
+    near_model_in = lax.ppermute(near_model_out, "blk", near)
+    near_fwd_in = lax.ppermute(near_fwd_out, "blk", near)
     far_in = lax.ppermute(far_out, "blk", far)
 
     def split(place_ref, terms_ref, layers, keep_ref, send_ref):
@@ -236,13 +241,6 @@
                 if b == 0:
                     old = old * sigma
                 next_v[b, t] = 2.0 * field(t)[b] - old + scale_v[t] * force
-        for t in range(3, last - 2):
-            fields = [tuple(next_v[b, t + d] for b in range(3)) for d in (-1, 0, 1)]
-            parts = strain_parts(*fields, tools)
-            other = strain_parts(fwd(1, t - 1), fwd(1, t), fwd(1, t + 1), tools)
-            pair = term_pair(parts, other, lame_v[at(t)], shear_v[at(t)])
-            for k in range(2):
-                terms_v[k, t] = terms_v[k, t] + pair[k]
 
     now_v, fwd_v, lame_v, shear_v = now, forward, lame_first, shear_modulus
     scale_v, next_v, terms_v, far_fwd_out = call(
@@ -257,13 +255,9 @@
 
     far_fwd_in = lax.ppermute(far_fwd_out, "blk", far)
 
-    early = list(range(3, last))
-    middle = [1, 2, last]
-
-    def near_first(now_v, fwd_v, lame_v, shear_v, scale_v, next_v, terms_v, near_ref,
-        near_next, near_terms, keep_ref, send_ref,
-        total_v,
-    ):
+    middle = list(range(1, cells))
+
+    def near_first(now_v, lame_v, shear_v, scale_v, next_v, near_ref, near_model_ref, near_next):
         place_ref = where()
         sigma = sign(place_ref)
         tools = difference_tools(*plane)
@@ -277,18 +271,8 @@
             slot = near_slot(place_ref, t - cells)
             return (near_ref[0, slot] * sigma, near_ref[1, slot], near_ref[2, slot])
 
-        def fwd(k, t):
-            if t <= last:
-                return (fwd_v[k, 0, at(t)] * sigma, fwd_v[k, 1, at(t)], fwd_v[k, 2, at(t)])
-            return (near_ref[4, k] * sigma, near_ref[5, k], near_ref[6, k])
-
-        def new(t):
-            if t < last - 1:
-                return tuple(next_v[b, t] for b in range(3))
-            return tuple(near_next[3 * (last - t) + b] for b in range(3))
-
         outer = normal_stress(
-            strain_parts(field(last), field(cells), field(cells + 1), tools), near_ref[3, 0], near_ref[3, 1]
+            strain_parts(field(last), field(cells), field(cells + 1), tools), near_model_ref[0], near_model_ref[1]
         )
         lame, shear = lame_v[at(last)], shear_v[at(last)]
         parts = strain_parts(field(last - 1), field(last), field(cells), tools)
@@ -297,30 +281,15 @@
         for b in range(3):
             near_next[b] = next_v[b, last] + scale_v[last] * (force[b] + outer[b])
             near_next[3 + b] = next_v[b, last - 1] + scale_v[last - 1] * normal[b]
-        other = strain_parts(fwd(0, last - 1), fwd(0, last), fwd(0, cells), tools)
-        pair = term_pair(parts, other, lame, shear)
-        for k in range(2):
-            near_terms[k] = pair[k]
-            for t in range(3, last - 2):
-                total_v[k, t] = terms_v[k, t]
-        for t in range(last - 2, last):
-            parts = strain_parts(new(t - 1), new(t), new(t + 1), tools)
-            other = strain_parts(fwd(1, t - 1), fwd(1, t), fwd(1, t + 1), tools)
-            pair = term_pair(parts, other, lame_v[at(t)], shear_v[at(t)])
-            for k in range(2):
-                total_v[k, t] = terms_v[k, t] + pair[k]
-        split(place_ref, total_v, early, keep_ref, send_ref)
-
-    near_next, near_terms, keep, send = call(
+
+    (near_next,) = call(
         near_first,
-        [(6, *plane), (2, *plane), (2, len(early), band, lanes), (events - 1, 2, len(early), band, lanes)],
-        (now_v, fwd_v, lame_v, shear_v, scale_v, next_v, terms_v, near_in),
-        [VM] * 8,
-        [VM] * 4,
-        [pltpu.VMEM((2, cells, *plane), jnp.float32)],
+        [(6, *plane)],
+        (now_v, lame_v, shear_v, scale_v, next_v, near_in, near_model_in),
+        [VM] * 7,
+        [VM],
     )
     near_next_in = lax.ppermute(near_next, "blk", near)
-    shared = [lax.ppermute(send[i], "event", others[i]) for i in range(events - 1)]
 
     def far_first(now_v, lame_v, shear_v, scale_v, next_v, far_ref, after_ref, far_next, far_after):
         place_ref = where()
@@ -355,7 +324,8 @@
     far_next_in = lax.ppermute(far_next, "blk", far)
     far_after_in = lax.ppermute(far_after, "blk", far)
 
-    def middle_terms(fwd_v, lame_v, shear_v, next_v, near_next_v, terms_v, near_terms, far_next_ref, far_after_ref, near_next_ref, near_ref,
+    def middle_terms(now_v, fwd_v, lame_v, shear_v, next_v, near_next_v, terms_v, far_next_ref, far_after_ref, near_next_ref,
+        near_ref, near_fwd_ref,
         keep_ref, send_ref, total_v,
     ):
         place_ref = where()
@@ -378,21 +348,34 @@
         def fwd(k, t):
             if t <= last:
                 return (fwd_v[k, 0, at(t)] * sigma, fwd_v[k, 1, at(t)], fwd_v[k, 2, at(t)])
-            return (near_ref[4, k] * sigma, near_ref[5, k], near_ref[6, k])
+            return (near_fwd_ref[k, 0] * sigma, near_fwd_ref[k, 1], near_fwd_ref[k, 2])
+
+        def start(t):
+            if t <= last:
+                return (now_v[0, at(t)] * sigma, now_v[1, at(t)], now_v[2, at(t)])
+            slot = near_slot(place_ref, t - cells)
+            return (near_ref[0, slot] * sigma, near_ref[1, slot], near_ref[2, slot])
 
         for t in middle:
+            lame, shear = lame_v[at(t)], shear_v[at(t)]
+            if t < last:
+                total = (terms_v[0, t], terms_v[1, t])
+            else:
+                parts = strain_parts(start(t - 1), start(t), start(t + 1), tools)
+                other = strain_parts(fwd(0, t - 1), fwd(0, t), fwd(0, t + 1), tools)
+                total = term_pair(parts, other, lame, shear)
             parts = strain_parts(field(t - 1), field(t), field(t + 1), tools)
             other = strain_parts(fwd(1, t - 1), fwd(1, t), fwd(1, t + 1), tools)
-            pair = term_pair(parts, other, lame_v[at(t)], shear_v[at(t)])
+            pair = term_pair(parts, other, lame, shear)
             for k in range(2):
-                total_v[k, t] = (near_terms[k] if t == last else terms_v[k, t]) + pair[k]
+                total_v[k, t] = total[k] + pair[k]
         split(place_ref, total_v, middle, keep_ref, send_ref)
 
     keep_mid, send_mid = call(
         middle_terms,
         [(2, len(middle), band, lanes), (events - 1, 2, len(middle), band, lanes)],
-        (fwd_v, lame_v, shear_v, next_v, near_next, terms_v, near_terms, far_next, far_after, near_next_in, near_in),
-        [VM] * 11,
+        (now_v, fwd_v, lame_v, shear_v, next_v, near_next, terms_v, far_next, far_after, near_next_in, near_in, near_fwd_in),
+        [VM] * 12,
         [VM] * 2,
         [pltpu.VMEM((2, cells, *plane), jnp.float32)],
     )
@@ -466,7 +449,7 @@
     far_shared = [lax.ppermute(far_send[i], "event", others[i]) for i in range(events - 1)]
 
     def second(now_v, lame_v, shear_v, scale_v, next_v, near_next_v, far_next_ref, far_after_ref, near_next_ref,
-        near_ref, after_ref,
+        near_model_ref, after_ref,
         final_v, face_v, normal_v, cross_v,
     ):
         place_ref = where()
@@ -491,7 +474,7 @@
             if t <= last:
                 lame, shear = lame_v[at(t)], shear_v[at(t)]
             else:
-                lame, shear = near_ref[3, 0], near_ref[3, 1]
+                lame, shear = near_model_ref[0], near_model_ref[1]
             normal = normal_stress(parts, lame, shear)
             for b in range(3):
                 normal_v[b, t] = normal[b]
@@ -519,7 +502,7 @@
         second,
         [now.shape, (3, 2, *plane)],
         (now_v, lame_v, shear_v, scale_v, next_v, near_next, far_next, far_after, near_next_in,
-         near_in, far_keep),
+         near_model_in, far_keep),
         [VM] * 11,
         [VM] * 2,
         [pltpu.VMEM((3, cells + 1, *plane), jnp.float32), pltpu.VMEM(now.shape, jnp.float32)],
@@ -536,10 +519,10 @@
         store_second, [now.shape], (final_v,), [VM], [ANY], [pltpu.SemaphoreType.DMA(())]
     )
 
-    def finish(result_ref, lame_v, shear_v, scale_v, face_v, far_next_ref, far_after_ref, far_ref,
+    def far_second(lame_v, shear_v, scale_v, face_v, far_next_ref, far_after_ref, far_ref,
         far_next_in_ref, far_after_in_ref, *rest,
     ):
-        pieces, (out_ref, *band_refs, edge_v, band_v, sem) = rest[: 3 * events], rest[3 * events :]
+        pieces, (edge_v, sum_ref) = rest[:events], rest[events:]
         place_ref = where()
         sigma = sign(place_ref)
         tools = difference_tools(*plane)
@@ -564,16 +547,37 @@
             after = face_v[b, 1] - scale_v[1] * normal[b]
             edge_v[b, odd] = first * sigma if b == 0 else first
             edge_v[b, 1 - odd] = after * sigma if b == 0 else after
-        copies = [pltpu.make_async_copy(edge_v, out_ref.at[:, pl.ds(odd * (cells - 2), 2)], sem.at[0])]
+        for k in range(2):
+            for j in range(len(middle)):
+                value = pieces[0][k, j]
+                for piece in pieces[1:]:
+                    value = value + piece[k, j]
+                sum_ref[k, j] = value
+
+    edge, sum_mid = call(
+        far_second,
+        [(3, 2, *plane), (2, len(middle), band, lanes)],
+        (lame_v, shear_v, scale_v, face_v, far_next, far_after, far_in, far_next_in, far_after_in,
+         keep_mid, *shared_mid),
+        [VM] * (9 + events),
+        [VM] * 2,
+    )
+
+    def finish(result_ref, edge_v, *rest):
+        pieces, (out_ref, *band_refs, band_v, sem) = rest[: events + 1], rest[events + 1 :]
+        place_ref = where()
+        copies = [
+            pltpu.make_async_copy(edge_v, out_ref.at[:, pl.ds(place_ref[0] * (cells - 2), 2)], sem.at[0])
+        ]
         copies[0].start()
         for k in range(2):
-            for i, layers in enumerate((early, middle, [0])):
-                own, *others_parts = pieces[i * events : (i + 1) * events]
+            groups = (([0], pieces[:events]), (middle, pieces[events:]))
+            for layers, (own, *others_parts) in groups:
                 for j, t in enumerate(layers):
                     value = own[k, j]
                     for part in others_parts:
                         value = value + part[k, j]
-                    band_v[k, at(t)] = value
+                    band_v[k, layer(place_ref, t)] = value
             copies.append(pltpu.make_async_copy(band_v.at[k], band_refs[k], sem.at[1 + k]))
             copies[-1].start()
         for copy in copies:
@@ -582,12 +586,10 @@
     result, band_shear, band_bulk = call(
         finish,
         [now.shape, (cells, band, lanes), (cells, band, lanes)],
-        (result, lame_v, shear_v, scale_v, face_v, far_next, far_after, far_in, far_next_in, far_after_in,
-         keep, *shared, keep_mid, *shared_mid, far_keep, *far_shared),
-        [ANY] + [VM] * (9 + 3 * events),
+        (result, edge, far_keep, *far_shared, sum_mid),
+        [ANY] + [VM] * (2 + events),
         [ANY] * 3,
-        [pltpu.VMEM((3, 2, *plane), jnp.float32), pltpu.VMEM((2, cells, band, lanes), jnp.float32),
-         pltpu.SemaphoreType.DMA((3,))],
+        [pltpu.VMEM((2, cells, band, lanes), jnp.float32), pltpu.SemaphoreType.DMA((3,))],
         aliases={0: 0},
     )
     return (result[None], band_shear, band_bulk)

time: 25.8 us -> 25.5 us (0.988)
    ppermute x1, starting transfers between devices: 0.6 us -> 1.93 us  [local(): lax.ppermute(send_mid[i], 'event', others[i])]
    ppermute x1 -> x2, starting transfers between devices: 1.49 us -> 0.51 us  [the longest x1 0.51 us: local(): near_model_in = lax.ppermute(near_model_out, 'blk', near)]
    ppermute x1, waiting for transfers between devices: 0.01 us -> 0.91 us  [local(): lax.ppermute(send_mid[i], 'event', others[i])]
    ppermute x1, starting transfers between devices: 0.08 us -> 0.8 us  [local(): far_fwd_in = lax.ppermute(far_fwd_out, 'blk', far)]
    ppermute x1, waiting for transfers between devices: 0.61 us -> 0.08 us  [local(): lax.ppermute(far_send[i], 'event', others[i])]
    ppermute x1, waiting for transfers between devices: 0.52 us -> 0.01 us  [local(): far_in = lax.ppermute(far_out, 'blk', far)]
    ppermute x1, starting transfers between devices: 0.52 us -> 0.01 us  [local(): near_in = lax.ppermute(near_out, 'blk', near)]
    ppermute x1, starting transfers between devices: 1.56 us -> 1.16 us  [local(): lax.ppermute(far_send[i], 'event', others[i])]
  transfers between devices with their start and end apart: 9 -> 10, of which waited for: 3 -> 3; matrix products, arithmetic and copies ran while one was open for 0% -> 0% of each run, Pallas kernels for 25% -> 26%
where the time goes in v5:
time: 25.5 us; the launch traced here: 25.3 us
  starting transfers between devices  14.5 us (57%)
  Pallas kernels  8.79 us (34%)
  waiting for transfers between devices  1.23 us (5%)
  between operations  0.79 us (3%)
    pallas_call x11, Pallas kernels, call(): pl.pallas_call(kernel, out_shape=shapes, in_specs=[pl.BlockSpec(memory_sp...  8.79 us
    ppermute x1, starting transfers between devices, local(): far_in = lax.ppermute(far_out, 'blk', far)  5.51 us
    ppermute x1, starting transfers between devices, local(): far_next_in = lax.ppermute(far_next, 'blk', far)  4.45 us
    ppermute x1, starting transfers between devices, local(): lax.ppermute(send_mid[i], 'event', others[i])  1.93 us
    ppermute x1, starting transfers between devices, local(): lax.ppermute(far_send[i], 'event', others[i])  1.16 us
    ppermute x1, waiting for transfers between devices, local(): lax.ppermute(send_mid[i], 'event', others[i])  0.91 us
    ppermute x1, starting transfers between devices, local(): far_fwd_in = lax.ppermute(far_fwd_out, 'blk', far)  0.8 us
  transfers between devices with their start and end apart: 10, of which 3 were waited for; matrix products, arithmetic and copies ran while one was open for 0% of the time, Pallas kernels for 26%

profile of v5, /device:TPU:0, one launch (start us, length us, event | category | flops | bytes accessed | tf_op | source)
XLA Modules:
  0.0 25.3 jit_solution(15576771721628606082)
XLA Ops:
  0.6 0.0 copy-start
  0.6 0.0 copy-start.1
  0.7 0.0 copy-start.2
  0.7 0.0 copy-start.3
  0.7 1.4 %pack.1 = (f32[3,2,64,128]{3,2,1,0:T(8,128)S(1)}, f32[2,64,128]{2,1,0:T(8,128)S(1)}, f32[2,3,64,128]{3,2,1,0:T(8,128)S(1)}, f32[4,2,64,128]{3,2,1,0:T(8,128)S(1)}) custom-call(f32[3,8,64,128]{3,2,1,0:T(8,128)} %bitcast.6, f32[2,3,8,64,128]{4,3,2,1,0:T(8,128)} %bitcast.13, f32[8,64,128]{2,1,0:T(8,128)} %lame_v.13, f32[8,64,128]{2,1,0:T(8,128)} %shear_v.13), custom_call_target="tpu_custom_call" | custom-call | flops 1000000000 | bytes 1000000000 | tf_op jit(solution)/shard_map/pack/pallas_call | solution.py:93
  2.1 5.5 %collective-permute-start.2 = (f32[4,2,64,128]{3,2,1,0:T(8,128)S(1)}, f32[4,2,64,128]{3,2,1,0:T(8,128)S(1)}, u32[]{:S(2)}, u32[]{:S(2)}) collective-permute-start(f32[4,2,64,128]{3,2,1,0:T(8,128)S(1)} %get-tuple-element.30), channel_id=1, source_target_pairs={{0,30},{2,4},{4,2},{6,8},{8,6},{10,12},{12,10},{14,16},{16,14},{18... | collective-permute-start | bytes 786440 | tf_op jit(solution)/shard_map/ppermute | solution.py:177
  7.6 0.0 collective-permute-start
  7.6 0.5 %collective-permute-start.1 = (f32[2,64,128]{2,1,0:T(8,128)S(1)}, f32[2,64,128]{2,1,0:T(8,128)S(1)}, u32[]{:S(2)}, u32[]{:S(2)}) collective-permute-start(f32[2,64,128]{2,1,0:T(8,128)S(1)} %get-tuple-element.29), channel_id=1, source_target_pairs={{0,2},{2,0},{4,6},{6,4},{8,10},{10,8},{12,14},{14,12},{16,18},{18,... | collective-permute-start | bytes 196616 | tf_op jit(solution)/shard_map/ppermute | solution.py:175
  8.1 0.0 collective-permute-start.5
  8.1 0.0 copy-done
  8.1 0.0 copy-done.1
  8.1 0.0 copy-done.2
  8.1 0.0 copy-done.3
  8.1 2.5 %inner_first.1 = (f32[8,64,128]{2,1,0:T(8,128)S(1)}, f32[3,8,64,128]{3,2,1,0:T(8,128)S(1)}, f32[2,7,64,128]{3,2,1,0:T(8,128)S(1)}, f32[2,3,64,128]{3,2,1,0:T(8,128)S(1)}) custom-call(f32[3,8,64,128]{3,2,1,0:T(8,128)S(1)} %bitcast.7, f32[3,8,64,128]{3,2,1,0:T(8,128)} %bitcast.20, f32[2,3,8,64,128]{4,3,2,1,0:T(8,128)S(1)} %bitcast.14, f32[8,64,128]{2,1,0:T(8,128)} %dens_ref.1, ...), custom_call_target="tpu_custom_call" | custom-call | flops 1000000000 | bytes 1000000000 | tf_op jit(solution)/shard_map/inner_first/pallas_call | solution.py:93
  10.6 0.8 %collective-permute-start.4 = (f32[2,3,64,128]{3,2,1,0:T(8,128)S(1)}, f32[2,3,64,128]{3,2,1,0:T(8,128)S(1)}, u32[]{:S(2)}, u32[]{:S(2)}) collective-permute-start(f32[2,3,64,128]{3,2,1,0:T(8,128)S(1)} %get-tuple-element.33), channel_id=1, source_target_pairs={{0,30},{2,4},{4,2},{6,8},{8,6},{10,12},{12,10},{14,16},{16,14},{18... | collective-permute-start | bytes 589832 | tf_op jit(solution)/shard_map/ppermute | solution.py:256
  11.4 0.0 collective-permute-done.1.near_model_ref
  11.4 0.0 collective-permute-done.near_ref
  11.4 0.3 %near_first.1.after_ref.near_next_v = f32[6,64,128]{2,1,0:T(8,128)S(1)} custom-call(f32[3,8,64,128]{3,2,1,0:T(8,128)S(1)} %bitcast.8, f32[8,64,128]{2,1,0:T(8,128)S(1)} %copy-done.2, f32[8,64,128]{2,1,0:T(8,128)S(1)} %copy-done.3, f32[8,64,128]{2,1,0:T(8,128)S(1)} %get-tuple-element.26.scale_v, f32[3,8,64,128]{3,2,1,0:T(8,128)S(1)} %get-tuple-element.27.next_v, ...), custom_call_target="tpu_custom_call" | custom-call | flops 1000000 | bytes 1000000 | tf_op jit(solution)/shard_map/near_first/pallas_call | solution.py:93
  11.7 0.1 collective-permute-start.3
  11.8 0.0 collective-permute-done.2.far_ref
  11.8 0.3 %far_first.1 = (f32[3,64,128]{2,1,0:T(8,128)S(1)}, f32[3,64,128]{2,1,0:T(8,128)S(1)}) custom-call(f32[3,8,64,128]{3,2,1,0:T(8,128)S(1)} %bitcast.9, f32[8,64,128]{2,1,0:T(8,128)S(1)} %copy-done.2, f32[8,64,128]{2,1,0:T(8,128)S(1)} %copy-done.3, f32[8,64,128]{2,1,0:T(8,128)S(1)} %get-tuple-element.26.scale_v, f32[3,8,64,128]{3,2,1,0:T(8,128)S(1)} %get-tuple-element.27.next_v, ...), custom_call_target="tpu_custom_call" | custom-call | flops 10000000000 | bytes 10000000000 | tf_op jit(solution)/shard_map/far_first/pallas_call | solution.py:93
  12.1 4.5 %collective-permute-start.6 = (f32[3,64,128]{2,1,0:T(8,128)S(1)}, f32[3,64,128]{2,1,0:T(8,128)S(1)}, u32[]{:S(2)}, u32[]{:S(2)}) collective-permute-start(f32[3,64,128]{2,1,0:T(8,128)S(1)} %get-tuple-element.31.far_next_ref), channel_id=1, source_target_pairs={{0,30},{2,4},{4,2},{6,8},{8,6},{10,12},{12,10},{14,16},{16,14},{18... | collective-permute-start | bytes 294920 | tf_op jit(solution)/shard_map/ppermute | solution.py:324
  16.5 0.1 collective-permute-start.7
  16.6 0.0 collective-permute-done.5.near_fwd_ref
  16.6 0.0 collective-permute-done.3.near_next_ref
  16.6 1.1 %middle_terms.1 = (f32[2,7,32,128]{3,2,1,0:T(8,128)S(1)}, f32[1,2,7,32,128]{4,3,2,1,0:T(8,128)S(1)}) custom-call(f32[3,8,64,128]{3,2,1,0:T(8,128)S(1)} %bitcast.10, f32[2,3,8,64,128]{4,3,2,1,0:T(8,128)S(1)} %bitcast.15, f32[8,64,128]{2,1,0:T(8,128)S(1)} %copy-done.2, f32[8,64,128]{2,1,0:T(8,128)S(1)} %copy-done.3, ...), custom_call_target="tpu_custom_call" | custom-call | flops 10000000 | bytes 10000000 | tf_op jit(solution)/shard_map/middle_terms/pallas_call | solution.py:93
  17.8 1.9 %collective-permute-start.8 = (f32[2,7,32,128]{3,2,1,0:T(8,128)S(1)}, f32[2,7,32,128]{3,2,1,0:T(8,128)S(1)}, u32[]{:S(2)}, u32[]{:S(2)}) collective-permute-start(f32[2,7,32,128]{3,2,1,0:T(8,128)S(1)} %bitcast.17), channel_id=1, source_target_pairs={{0,1},{1,0},{2,3},{3,2},{4,5},{5,4},{6,7},{7,6},{8,9},{9,8},{10,11... | collective-permute-start | bytes 688136 | tf_op jit(solution)/shard_map/ppermute | solution.py:382
  19.7 0.0 collective-permute-done.4.far_fwd_ref
  19.7 0.3 %edge_terms.1 = (f32[2,64,128]{2,1,0:T(8,128)S(1)}, f32[4,64,128]{2,1,0:T(8,128)S(1)}) custom-call(f32[3,8,64,128]{3,2,1,0:T(8,128)S(1)} %bitcast.11, f32[2,3,8,64,128]{4,3,2,1,0:T(8,128)S(1)} %bitcast.16, f32[8,64,128]{2,1,0:T(8,128)S(1)} %copy-done.2, f32[8,64,128]{2,1,0:T(8,128)S(1)} %copy-done.3, f32[3,64,128]{2,1,0:T(8,128)S(1)} %get-tuple-element.31.far_next_ref, ...), custom_call_target="tpu_custom_call" | custom-call | flops 10000000 | bytes 10000000 | tf_op jit(solution)/shard_map/edge_terms/pallas_call | solution.py:93
  20.0 0.0 collective-permute-done.6.far_next_in_ref
  20.1 1.2 %collective-permute-start.9 = (f32[2,1,32,128]{3,2,1,0:T(8,128)S(1)}, f32[2,1,32,128]{3,2,1,0:T(8,128)S(1)}, u32[]{:S(2)}, u32[]{:S(2)}) collective-permute-start(f32[2,1,32,128]{3,2,1,0:T(8,128)S(1)} %bitcast.18), channel_id=1, source_target_pairs={{0,1},{1,0},{2,3},{3,2},{4,5},{5,4},{6,7},{7,6},{8,9},{9,8},{10,11... | collective-permute-start | bytes 98312 | tf_op jit(solution)/shard_map/ppermute | solution.py:449
  21.2 1.0 %second.1 = (f32[3,8,64,128]{3,2,1,0:T(8,128)S(1)}, f32[3,2,64,128]{3,2,1,0:T(8,128)S(1)}) custom-call(f32[3,8,64,128]{3,2,1,0:T(8,128)S(1)} %bitcast.12, f32[8,64,128]{2,1,0:T(8,128)S(1)} %copy-done.2, f32[8,64,128]{2,1,0:T(8,128)S(1)} %copy-done.3, f32[8,64,128]{2,1,0:T(8,128)S(1)} %get-tuple-element.26.scale_v, ...), custom_call_target="tpu_custom_call" | custom-call | flops 100000000 | bytes 100000000 | tf_op jit(solution)/shard_map/second/pallas_call | solution.py:93
  22.2 0.8 %store_second.1.result_ref = f32[3,8,64,128]{3,2,1,0:T(8,128)} custom-call(f32[3,8,64,128]{3,2,1,0:T(8,128)S(1)} %get-tuple-element.40.final_v), custom_call_target="tpu_custom_call" | custom-call | flops 100000000 | bytes 100000000 | tf_op jit(solution)/shard_map/store_second/pallas_call | solution.py:93
  23.1 0.2 collective-permute-done.7.far_after_in_ref
  23.3 0.9 %collective-permute-done.8.rest_1_ = f32[2,7,32,128]{3,2,1,0:T(8,128)S(1)} collective-permute-done((f32[2,7,32,128]{3,2,1,0:T(8,128)S(1)}, f32[2,7,32,128]{3,2,1,0:T(8,128)S(1)}, u32[]{:S(2)}, u32[]{:S(2)}) %collective-permute-start.8) | collective-permute-done | bytes 229408 | tf_op jit(solution)/shard_map/ppermute | solution.py:382
  24.2 0.3 %far_second.1 = (f32[3,2,64,128]{3,2,1,0:T(8,128)S(1)}, f32[2,7,32,128]{3,2,1,0:T(8,128)S(1)}) custom-call(f32[8,64,128]{2,1,0:T(8,128)S(1)} %copy-done.2, f32[8,64,128]{2,1,0:T(8,128)S(1)} %copy-done.3, f32[8,64,128]{2,1,0:T(8,128)S(1)} %get-tuple-element.26.scale_v, f32[3,2,64,128]{3,2,1,0:T(8,128)S(1)} %get-tuple-element.41.face_v, ...), custom_call_target="tpu_custom_call" | custom-call | flops 10000000000 | bytes 10000000000 | tf_op jit(solution)/shard_map/far_second/pallas_call | solution.py:93
  24.5 0.1 collective-permute-done.9.rest_1_
  24.5 0.8 %finish.1 = (f32[3,8,64,128]{3,2,1,0:T(8,128)}, f32[8,32,128]{2,1,0:T(8,128)}, f32[8,32,128]{2,1,0:T(8,128)}) custom-call(f32[3,8,64,128]{3,2,1,0:T(8,128)} %store_second.1.result_ref, f32[3,2,64,128]{3,2,1,0:T(8,128)S(1)} %get-tuple-element.43.edge_v, f32[2,1,32,128]{3,2,1,0:T(8,128)S(1)} %get-tuple-element.39.after_ref.rest_0_, ...), custom_call_target="tpu_custom_call", output_to_operand_aliasing={{0}: (0, {})} | custom-call | flops 100000 | bytes 100000 | tf_op jit(solution)/shard_map/finish/pallas_call | solution.py:93
  (1 shorter events, 0.0 us)
Async XLA Ops:
  0.6 7.5 %copy-start = (f32[1,3,8,64,128]{4,3,2,1,0:T(8,128)S(1)}, f32[1,3,8,64,128]{4,3,2,1,0:T(8,128)}, u32[]{:S(2)}) copy-start(f32[1,3,8,64,128]{4,3,2,1,0:T(8,128)} %param.6) | copy-start | bytes 2359300
  0.6 7.5 %copy-start.1 = (f32[1,2,3,8,64,128]{5,4,3,2,1,0:T(8,128)S(1)}, f32[1,2,3,8,64,128]{5,4,3,2,1,0:T(8,128)}, u32[]{:S(2)}) copy-start(f32[1,2,3,8,64,128]{5,4,3,2,1,0:T(8,128)} %param.8) | copy-start | bytes 4718596
  0.7 7.5 %copy-start.2 = (f32[8,64,128]{2,1,0:T(8,128)S(1)}, f32[8,64,128]{2,1,0:T(8,128)}, u32[]{:S(2)}) copy-start(f32[8,64,128]{2,1,0:T(8,128)} %lame_v.13) | copy-start | bytes 786436
  0.7 7.5 %copy-start.3 = (f32[8,64,128]{2,1,0:T(8,128)S(1)}, f32[8,64,128]{2,1,0:T(8,128)}, u32[]{:S(2)}) copy-start(f32[8,64,128]{2,1,0:T(8,128)} %shear_v.13) | copy-start | bytes 786436
  2.1 9.7 %collective-permute-start.2 = (f32[4,2,64,128]{3,2,1,0:T(8,128)S(1)}, f32[4,2,64,128]{3,2,1,0:T(8,128)S(1)}, u32[]{:S(2)}, u32[]{:S(2)}) collective-permute-start(f32[4,2,64,128]{3,2,1,0:T(8,128)S(1)} %get-tuple-element.30), channel_id=1, source_target_pairs={{0,30},{2,4},{4,2},{6,8},{8,6},{10,12},{12,10},{14,16},{16,14},{18... | collective-permute-start | bytes 786440 | tf_op jit(solution)/shard_map/ppermute | solution.py:177
  7.6 3.8 %collective-permute-start = (f32[3,2,64,128]{3,2,1,0:T(8,128)S(1)}, f32[3,2,64,128]{3,2,1,0:T(8,128)S(1)}, u32[]{:S(2)}, u32[]{:S(2)}) collective-permute-start(f32[3,2,64,128]{3,2,1,0:T(8,128)S(1)} %get-tuple-element.28), channel_id=1, source_target_pairs={{0,2},{2,0},{4,6},{6,4},{8,10},{10,8},{12,14},{14,12},{16,18},{18,... | collective-permute-start | bytes 589832 | tf_op jit(solution)/shard_map/ppermute | solution.py:174
  7.6 3.8 %collective-permute-start.1 = (f32[2,64,128]{2,1,0:T(8,128)S(1)}, f32[2,64,128]{2,1,0:T(8,128)S(1)}, u32[]{:S(2)}, u32[]{:S(2)}) collective-permute-start(f32[2,64,128]{2,1,0:T(8,128)S(1)} %get-tuple-element.29), channel_id=1, source_target_pairs={{0,2},{2,0},{4,6},{6,4},{8,10},{10,8},{12,14},{14,12},{16,18},{18,... | collective-permute-start | bytes 196616 | tf_op jit(solution)/shard_map/ppermute | solution.py:175
  8.1 8.5 %collective-permute-start.5 = (f32[2,3,64,128]{3,2,1,0:T(8,128)S(1)}, f32[2,3,64,128]{3,2,1,0:T(8,128)S(1)}, u32[]{:S(2)}, u32[]{:S(2)}) collective-permute-start(f32[2,3,64,128]{3,2,1,0:T(8,128)S(1)} %get-tuple-element.35), channel_id=1, source_target_pairs={{0,2},{2,0},{4,6},{6,4},{8,10},{10,8},{12,14},{14,12},{16,18},{18,... | collective-permute-start | bytes 589832 | tf_op jit(solution)/shard_map/ppermute | solution.py:176
  10.6 9.1 %collective-permute-start.4 = (f32[2,3,64,128]{3,2,1,0:T(8,128)S(1)}, f32[2,3,64,128]{3,2,1,0:T(8,128)S(1)}, u32[]{:S(2)}, u32[]{:S(2)}) collective-permute-start(f32[2,3,64,128]{3,2,1,0:T(8,128)S(1)} %get-tuple-element.33), channel_id=1, source_target_pairs={{0,30},{2,4},{4,2},{6,8},{8,6},{10,12},{12,10},{14,16},{16,14},{18... | collective-permute-start | bytes 589832 | tf_op jit(solution)/shard_map/ppermute | solution.py:256
  11.7 4.9 %collective-permute-start.3 = (f32[6,64,128]{2,1,0:T(8,128)S(1)}, f32[6,64,128]{2,1,0:T(8,128)S(1)}, u32[]{:S(2)}, u32[]{:S(2)}) collective-permute-start(f32[6,64,128]{2,1,0:T(8,128)S(1)} %near_first.1.after_ref.near_next_v), channel_id=1, source_target_pairs={{0,2},{2,0},{4,6},{6,4},{8,10},{10,8},{12,14},{14,12},{16,18},{18,... | collective-permute-start | bytes 589832 | tf_op jit(solution)/shard_map/ppermute | solution.py:292
  12.1 7.9 %collective-permute-start.6 = (f32[3,64,128]{2,1,0:T(8,128)S(1)}, f32[3,64,128]{2,1,0:T(8,128)S(1)}, u32[]{:S(2)}, u32[]{:S(2)}) collective-permute-start(f32[3,64,128]{2,1,0:T(8,128)S(1)} %get-tuple-element.31.far_next_ref), channel_id=1, source_target_pairs={{0,30},{2,4},{4,2},{6,8},{8,6},{10,12},{12,10},{14,16},{16,14},{18... | collective-permute-start | bytes 294920 | tf_op jit(solution)/shard_map/ppermute | solution.py:324
  16.5 6.7 %collective-permute-start.7 = (f32[3,64,128]{2,1,0:T(8,128)S(1)}, f32[3,64,128]{2,1,0:T(8,128)S(1)}, u32[]{:S(2)}, u32[]{:S(2)}) collective-permute-start(f32[3,64,128]{2,1,0:T(8,128)S(1)} %get-tuple-element.32.far_after_ref), channel_id=1, source_target_pairs={{0,30},{2,4},{4,2},{6,8},{8,6},{10,12},{12,10},{14,16},{16,14},{18... | collective-permute-start | bytes 294920 | tf_op jit(solution)/shard_map/ppermute | solution.py:325
  17.8 6.4 %collective-permute-start.8 = (f32[2,7,32,128]{3,2,1,0:T(8,128)S(1)}, f32[2,7,32,128]{3,2,1,0:T(8,128)S(1)}, u32[]{:S(2)}, u32[]{:S(2)}) collective-permute-start(f32[2,7,32,128]{3,2,1,0:T(8,128)S(1)} %bitcast.17), channel_id=1, source_target_pairs={{0,1},{1,0},{2,3},{3,2},{4,5},{5,4},{6,7},{7,6},{8,9},{9,8},{10,11... | collective-permute-start | bytes 688136 | tf_op jit(solution)/shard_map/ppermute | solution.py:382
  20.1 4.5 %collective-permute-start.9 = (f32[2,1,32,128]{3,2,1,0:T(8,128)S(1)}, f32[2,1,32,128]{3,2,1,0:T(8,128)S(1)}, u32[]{:S(2)}, u32[]{:S(2)}) collective-permute-start(f32[2,1,32,128]{3,2,1,0:T(8,128)S(1)} %bitcast.18), channel_id=1, source_target_pairs={{0,1},{1,0},{2,3},{3,2},{4,5},{5,4},{6,7},{7,6},{8,9},{9,8},{10,11... | collective-permute-start | bytes 98312 | tf_op jit(solution)/shard_map/ppermute | solution.py:449

commit v6 on v5

--- a/solution.py
+++ b/solution.py
@@ -81,7 +81,7 @@
     return shear_term, bulk_term
 
 
-costs = {'pack': 1000000000, 'inner_first': 1000000000, 'near_first': 1000000, 'far_first': 10000000000, 'middle_terms': 10000000, 'edge_terms': 10000000, 'second': 100000000, 'far_terms': 10000000000, 'store_second': 100000000, 'far_second': 10000000000, 'finish': 100000}
+costs = {'pack': 1000000000, 'inner_first': 1000000000, 'near_first': 1000000, 'far_first': 10000000000, 'middle_terms': 10000000, 'edge_terms': 10000000, 'second': 100000000, 'far_terms': 10000000000, 'store_second': 100000000, 'far_second': 1, 'finish': 100000}
 
 
 def call(kernel, outs, args, in_spaces, out_spaces, scratch=(), vmem=40 << 20, aliases=None):
@@ -143,7 +143,7 @@
     def sign(place_ref):
         return (1 - 2 * place_ref[0]).astype(jnp.float32)
 
-    def pack(now_ref, forward_ref, lame_ref, shear_ref, near_ref, near_model_ref, near_fwd_ref, far_ref, sem):
+    def pack(now_ref, lame_ref, shear_ref, near_ref, near_model_ref, far_ref, sem):
         place_ref = where()
         odd = place_ref[0]
         at, low = layer(place_ref, 0), odd * (cells - 2)
@@ -156,24 +156,22 @@
         copies.append((now_ref.at[:, pl.ds(low, 2)], near_ref))
         copies.append((lame_ref.at[at], near_model_ref.at[0]))
         copies.append((shear_ref.at[at], near_model_ref.at[1]))
-        copies.append((forward_ref.at[:, :, layer(place_ref, last)], near_fwd_ref))
         started = [pltpu.make_async_copy(src, dst, sem.at[i]) for i, (src, dst) in enumerate(copies)]
         for copy in started:
             copy.start()
         for copy in started:
             copy.wait()
 
-    near_out, near_model_out, near_fwd_out, far_out = call(
+    near_out, near_model_out, far_out = call(
         pack,
-        [(3, 2, *plane), (2, *plane), (steps, 3, *plane), (4, 2, *plane)],
-        (now_hbm, forward_hbm, lame_hbm, shear_hbm),
-        [ANY, ANY, ANY, ANY],
-        [VM] * 4,
-        [pltpu.SemaphoreType.DMA((7,))],
+        [(3, 2, *plane), (2, *plane), (4, 2, *plane)],
+        (now_hbm, lame_hbm, shear_hbm),
+        [ANY, ANY, ANY],
+        [VM] * 3,
+        [pltpu.SemaphoreType.DMA((6,))],
     )
     near_in = lax.ppermute(near_out, "blk", near)
     near_model_in = lax.ppermute(near_model_out, "blk", near)
-    near_fwd_in = lax.ppermute(near_fwd_out, "blk", near)
     far_in = lax.ppermute(far_out, "blk", far)
 
     def split(place_ref, terms_ref, layers, keep_ref, send_ref):
@@ -185,6 +183,8 @@
             for k in range(2):
                 for i, t in enumerate(layers):
                     out[k, i] = terms_ref[k, t, pl.ds(start, band)]
+
+    inner = range(3, last - 2)
 
     def inner_first(now_v, prev_ref, fwd_v, dens_ref, lame_v, shear_v,
         scale_v, next_v, terms_v, far_fwd_ref,
@@ -241,6 +241,13 @@
                 if b == 0:
                     old = old * sigma
                 next_v[b, t] = 2.0 * field(t)[b] - old + scale_v[t] * force
+        for t in inner:
+            fields = [tuple(next_v[b, t + d] for b in range(3)) for d in (-1, 0, 1)]
+            parts = strain_parts(*fields, tools)
+            other = strain_parts(fwd(1, t - 1), fwd(1, t), fwd(1, t + 1), tools)
+            pair = term_pair(parts, other, lame_v[at(t)], shear_v[at(t)])
+            for k in range(2):
+                terms_v[k, t] = terms_v[k, t] + pair[k]
 
     now_v, fwd_v, lame_v, shear_v = now, forward, lame_first, shear_modulus
     scale_v, next_v, terms_v, far_fwd_out = call(
@@ -257,7 +264,7 @@
 
     middle = list(range(1, cells))
 
-    def near_first(now_v, lame_v, shear_v, scale_v, next_v, near_ref, near_model_ref, near_next):
+    def near_first(now_v, fwd_v, lame_v, shear_v, scale_v, next_v, near_ref, near_model_ref, near_next):
         place_ref = where()
         sigma = sign(place_ref)
         tools = difference_tools(*plane)
@@ -281,12 +288,14 @@
         for b in range(3):
             near_next[b] = next_v[b, last] + scale_v[last] * (force[b] + outer[b])
             near_next[3 + b] = next_v[b, last - 1] + scale_v[last - 1] * normal[b]
+            for k in range(steps):
+                near_next[6 + 3 * k + b] = fwd_v[k, b, at(last)]
 
     (near_next,) = call(
         near_first,
-        [(6, *plane)],
-        (now_v, lame_v, shear_v, scale_v, next_v, near_in, near_model_in),
-        [VM] * 7,
+        [(6 + 3 * steps, *plane)],
+        (now_v, fwd_v, lame_v, shear_v, scale_v, next_v, near_in, near_model_in),
+        [VM] * 8,
         [VM],
     )
     near_next_in = lax.ppermute(near_next, "blk", near)
@@ -325,7 +334,7 @@
     far_after_in = lax.ppermute(far_after, "blk", far)
 
     def middle_terms(now_v, fwd_v, lame_v, shear_v, next_v, near_next_v, terms_v, far_next_ref, far_after_ref, near_next_ref,
-        near_ref, near_fwd_ref,
+        near_ref,
         keep_ref, send_ref, total_v,
     ):
         place_ref = where()
@@ -348,7 +357,7 @@
         def fwd(k, t):
             if t <= last:
                 return (fwd_v[k, 0, at(t)] * sigma, fwd_v[k, 1, at(t)], fwd_v[k, 2, at(t)])
-            return (near_fwd_ref[k, 0] * sigma, near_fwd_ref[k, 1], near_fwd_ref[k, 2])
+            return (near_next_ref[6 + 3 * k] * sigma, near_next_ref[7 + 3 * k], near_next_ref[8 + 3 * k])
 
         def start(t):
             if t <= last:
@@ -364,18 +373,20 @@
                 parts = strain_parts(start(t - 1), start(t), start(t + 1), tools)
                 other = strain_parts(fwd(0, t - 1), fwd(0, t), fwd(0, t + 1), tools)
                 total = term_pair(parts, other, lame, shear)
-            parts = strain_parts(field(t - 1), field(t), field(t + 1), tools)
-            other = strain_parts(fwd(1, t - 1), fwd(1, t), fwd(1, t + 1), tools)
-            pair = term_pair(parts, other, lame, shear)
+            if t not in inner:
+                parts = strain_parts(field(t - 1), field(t), field(t + 1), tools)
+                other = strain_parts(fwd(1, t - 1), fwd(1, t), fwd(1, t + 1), tools)
+                pair = term_pair(parts, other, lame, shear)
+                total = (total[0] + pair[0], total[1] + pair[1])
             for k in range(2):
-                total_v[k, t] = total[k] + pair[k]
+                total_v[k, t] = total[k]
         split(place_ref, total_v, middle, keep_ref, send_ref)
 
     keep_mid, send_mid = call(
         middle_terms,
         [(2, len(middle), band, lanes), (events - 1, 2, len(middle), band, lanes)],
-        (now_v, fwd_v, lame_v, shear_v, next_v, near_next, terms_v, far_next, far_after, near_next_in, near_in, near_fwd_in),
-        [VM] * 12,
+        (now_v, fwd_v, lame_v, shear_v, next_v, near_next, terms_v, far_next, far_after, near_next_in, near_in),
+        [VM] * 11,
         [VM] * 2,
         [pltpu.VMEM((2, cells, *plane), jnp.float32)],
     )
@@ -508,21 +519,21 @@
         [pltpu.VMEM((3, cells + 1, *plane), jnp.float32), pltpu.VMEM(now.shape, jnp.float32)],
     )
 
-    def store_second(final_v, out_ref, sem):
+    def store_second(final_v, out_ref, done_ref, sem):
         place_ref = where()
         inner = pl.ds(2 - 2 * place_ref[0], cells - 2)
         copy = pltpu.make_async_copy(final_v.at[:, inner], out_ref.at[:, inner], sem)
         copy.start()
         copy.wait()
-
-    (result,) = call(
-        store_second, [now.shape], (final_v,), [VM], [ANY], [pltpu.SemaphoreType.DMA(())]
+        done_ref[...] = jnp.zeros((8, lanes), jnp.float32)
+
+    result, done = call(
+        store_second, [now.shape, (8, lanes)], (final_v,), [VM], [ANY, VM], [pltpu.SemaphoreType.DMA(())]
     )
 
     def far_second(lame_v, shear_v, scale_v, face_v, far_next_ref, far_after_ref, far_ref,
-        far_next_in_ref, far_after_in_ref, *rest,
+        far_next_in_ref, far_after_in_ref, after_ref, edge_v,
     ):
-        pieces, (edge_v, sum_ref) = rest[:events], rest[events:]
         place_ref = where()
         sigma = sign(place_ref)
         tools = difference_tools(*plane)
@@ -547,24 +558,17 @@
             after = face_v[b, 1] - scale_v[1] * normal[b]
             edge_v[b, odd] = first * sigma if b == 0 else first
             edge_v[b, 1 - odd] = after * sigma if b == 0 else after
-        for k in range(2):
-            for j in range(len(middle)):
-                value = pieces[0][k, j]
-                for piece in pieces[1:]:
-                    value = value + piece[k, j]
-                sum_ref[k, j] = value
-
-    edge, sum_mid = call(
+
+    (edge,) = call(
         far_second,
-        [(3, 2, *plane), (2, len(middle), band, lanes)],
-        (lame_v, shear_v, scale_v, face_v, far_next, far_after, far_in, far_next_in, far_after_in,
-         keep_mid, *shared_mid),
-        [VM] * (9 + events),
-        [VM] * 2,
+        [(3, 2, *plane)],
+        (lame_v, shear_v, scale_v, face_v, far_next, far_after, far_in, far_next_in, far_after_in, done),
+        [VM] * 10,
+        [VM],
     )
 
     def finish(result_ref, edge_v, *rest):
-        pieces, (out_ref, *band_refs, band_v, sem) = rest[: events + 1], rest[events + 1 :]
+        pieces, (out_ref, *band_refs, band_v, sem) = rest[: 2 * events], rest[2 * events :]
         place_ref = where()
         copies = [
             pltpu.make_async_copy(edge_v, out_ref.at[:, pl.ds(place_ref[0] * (cells - 2), 2)], sem.at[0])
@@ -586,8 +590,8 @@
     result, band_shear, band_bulk = call(
         finish,
         [now.shape, (cells, band, lanes), (cells, band, lanes)],
-        (result, edge, far_keep, *far_shared, sum_mid),
-        [ANY] + [VM] * (2 + events),
+        (result, edge, far_keep, *far_shared, keep_mid, *shared_mid),
+        [ANY] + [VM] * (1 + 2 * events),
         [ANY] * 3,
         [pltpu.VMEM((2, cells, band, lanes), jnp.float32), pltpu.SemaphoreType.DMA((3,))],
         aliases={0: 0},

time: 25.5 us -> 25.1 us (0.984)
  waiting for transfers between devices: 1.23 us -> 0.88 us
    ppermute x1, waiting for transfers between devices: 0.91 us -> 0.01 us  [local(): lax.ppermute(send_mid[i], 'event', others[i])]
    ppermute x1, waiting for transfers between devices: 0.08 us -> 0.63 us  [local(): lax.ppermute(far_send[i], 'event', others[i])]
    ppermute x1, starting transfers between devices: 0.8 us -> 0.39 us  [local(): far_fwd_in = lax.ppermute(far_fwd_out, 'blk', far)]
    ppermute x1, starting transfers between devices: 1.16 us -> 1.57 us  [local(): lax.ppermute(far_send[i], 'event', others[i])]
  transfers between devices with their start and end apart: 10 -> 9, of which waited for: 3 -> 3; matrix products, arithmetic and copies ran while one was open for 0% -> 0% of each run, Pallas kernels for 26% -> 27%
where the time goes in v6:
time: 25.1 us; the launch traced here: 25 us
  starting transfers between devices  14.6 us (58%)
  Pallas kernels  8.77 us (35%)
  waiting for transfers between devices  0.88 us (4%)
  between operations  0.76 us (3%)
    pallas_call x11, Pallas kernels, call(): pl.pallas_call(kernel, out_shape=shapes, in_specs=[pl.BlockSpec(memory_sp...  8.77 us
    ppermute x1, starting transfers between devices, local(): far_in = lax.ppermute(far_out, 'blk', far)  5.51 us
    ppermute x1, starting transfers between devices, local(): far_next_in = lax.ppermute(far_next, 'blk', far)  4.51 us
    ppermute x1, starting transfers between devices, local(): lax.ppermute(send_mid[i], 'event', others[i])  1.92 us
    ppermute x1, starting transfers between devices, local(): lax.ppermute(far_send[i], 'event', others[i])  1.57 us
    ppermute x1, waiting for transfers between devices, local(): lax.ppermute(far_send[i], 'event', others[i])  0.63 us
    ppermute x1, starting transfers between devices, local(): near_model_in = lax.ppermute(near_model_out, 'blk', near)  0.51 us
  transfers between devices with their start and end apart: 9, of which 3 were waited for; matrix products, arithmetic and copies ran while one was open for 0% of the time, Pallas kernels for 27%

profile of v6, /device:TPU:0, one launch (start us, length us, event | category | flops | bytes accessed | tf_op | source)
XLA Modules:
  0.0 25.0 jit_solution(5079867050285685144)
XLA Ops:
  0.6 0.0 copy-start
  0.6 0.0 copy-start.1
  0.7 0.0 copy-start.2
  0.7 0.0 copy-start.3
  0.7 1.3 %pack.1 = (f32[3,2,64,128]{3,2,1,0:T(8,128)S(1)}, f32[2,64,128]{2,1,0:T(8,128)S(1)}, f32[4,2,64,128]{3,2,1,0:T(8,128)S(1)}) custom-call(f32[3,8,64,128]{3,2,1,0:T(8,128)} %bitcast.10, f32[8,64,128]{2,1,0:T(8,128)} %lame_v.13, f32[8,64,128]{2,1,0:T(8,128)} %shear_v.13), custom_call_target="tpu_custom_call" | custom-call | flops 1000000000 | bytes 1000000000 | tf_op jit(solution)/shard_map/pack/pallas_call | solution.py:93
  2.0 5.5 %collective-permute-start.2 = (f32[4,2,64,128]{3,2,1,0:T(8,128)S(1)}, f32[4,2,64,128]{3,2,1,0:T(8,128)S(1)}, u32[]{:S(2)}, u32[]{:S(2)}) collective-permute-start(f32[4,2,64,128]{3,2,1,0:T(8,128)S(1)} %get-tuple-element.29), channel_id=1, source_target_pairs={{0,30},{2,4},{4,2},{6,8},{8,6},{10,12},{12,10},{14,16},{16,14},{18... | collective-permute-start | bytes 786440 | tf_op jit(solution)/shard_map/ppermute | solution.py:175
  7.5 0.0 collective-permute-start
  7.5 0.5 %collective-permute-start.1 = (f32[2,64,128]{2,1,0:T(8,128)S(1)}, f32[2,64,128]{2,1,0:T(8,128)S(1)}, u32[]{:S(2)}, u32[]{:S(2)}) collective-permute-start(f32[2,64,128]{2,1,0:T(8,128)S(1)} %get-tuple-element.28), channel_id=1, source_target_pairs={{0,2},{2,0},{4,6},{6,4},{8,10},{10,8},{12,14},{14,12},{16,18},{18,... | collective-permute-start | bytes 196616 | tf_op jit(solution)/shard_map/ppermute | solution.py:174
  8.0 0.0 copy-done
  8.0 0.0 copy-done.1
  8.0 0.0 copy-done.2
  8.0 0.0 copy-done.3
  8.0 2.8 %inner_first.1 = (f32[8,64,128]{2,1,0:T(8,128)S(1)}, f32[3,8,64,128]{3,2,1,0:T(8,128)S(1)}, f32[2,7,64,128]{3,2,1,0:T(8,128)S(1)}, f32[2,3,64,128]{3,2,1,0:T(8,128)S(1)}) custom-call(f32[3,8,64,128]{3,2,1,0:T(8,128)S(1)} %bitcast.11, f32[3,8,64,128]{3,2,1,0:T(8,128)} %bitcast.20, f32[2,3,8,64,128]{4,3,2,1,0:T(8,128)S(1)} %bitcast.6, f32[8,64,128]{2,1,0:T(8,128)} %dens_ref.1, ...), custom_call_target="tpu_custom_call" | custom-call | flops 1000000000 | bytes 1000000000 | tf_op jit(solution)/shard_map/inner_first/pallas_call | solution.py:93
  10.8 0.4 %collective-permute-start.4 = (f32[2,3,64,128]{3,2,1,0:T(8,128)S(1)}, f32[2,3,64,128]{3,2,1,0:T(8,128)S(1)}, u32[]{:S(2)}, u32[]{:S(2)}) collective-permute-start(f32[2,3,64,128]{3,2,1,0:T(8,128)S(1)} %get-tuple-element.32), channel_id=1, source_target_pairs={{0,30},{2,4},{4,2},{6,8},{8,6},{10,12},{12,10},{14,16},{16,14},{18... | collective-permute-start | bytes 589832 | tf_op jit(solution)/shard_map/ppermute | solution.py:263
  11.2 0.0 collective-permute-done.1.near_model_ref
  11.2 0.0 collective-permute-done.near_ref
  11.2 0.3 %near_first.1.after_ref.near_next_v = f32[12,64,128]{2,1,0:T(8,128)S(1)} custom-call(f32[3,8,64,128]{3,2,1,0:T(8,128)S(1)} %bitcast.12, f32[2,3,8,64,128]{4,3,2,1,0:T(8,128)S(1)} %bitcast.7, f32[8,64,128]{2,1,0:T(8,128)S(1)} %copy-done.2, f32[8,64,128]{2,1,0:T(8,128)S(1)} %copy-done.3, f32[8,64,128]{2,1,0:T(8,128)S(1)} %get-tuple-element.25.scale_v, ...), custom_call_target="tpu_custom_call" | custom-call | flops 1000000 | bytes 1000000 | tf_op jit(solution)/shard_map/near_first/pallas_call | solution.py:93
  11.5 0.1 collective-permute-start.3
  11.6 0.1 collective-permute-done.2.far_ref
  11.6 0.3 %far_first.1 = (f32[3,64,128]{2,1,0:T(8,128)S(1)}, f32[3,64,128]{2,1,0:T(8,128)S(1)}) custom-call(f32[3,8,64,128]{3,2,1,0:T(8,128)S(1)} %bitcast.13, f32[8,64,128]{2,1,0:T(8,128)S(1)} %copy-done.2, f32[8,64,128]{2,1,0:T(8,128)S(1)} %copy-done.3, f32[8,64,128]{2,1,0:T(8,128)S(1)} %get-tuple-element.25.scale_v, ...), custom_call_target="tpu_custom_call" | custom-call | flops 10000000000 | bytes 10000000000 | tf_op jit(solution)/shard_map/far_first/pallas_call | solution.py:93
  11.9 4.5 %collective-permute-start.5 = (f32[3,64,128]{2,1,0:T(8,128)S(1)}, f32[3,64,128]{2,1,0:T(8,128)S(1)}, u32[]{:S(2)}, u32[]{:S(2)}) collective-permute-start(f32[3,64,128]{2,1,0:T(8,128)S(1)} %get-tuple-element.30.far_next_ref), channel_id=1, source_target_pairs={{0,30},{2,4},{4,2},{6,8},{8,6},{10,12},{12,10},{14,16},{16,14},{18... | collective-permute-start | bytes 294920 | tf_op jit(solution)/shard_map/ppermute | solution.py:333
  16.4 0.1 collective-permute-start.6
  16.5 0.0 collective-permute-done.3.near_next_ref
  16.5 0.9 %middle_terms.1 = (f32[2,7,32,128]{3,2,1,0:T(8,128)S(1)}, f32[1,2,7,32,128]{4,3,2,1,0:T(8,128)S(1)}) custom-call(f32[3,8,64,128]{3,2,1,0:T(8,128)S(1)} %bitcast.14, f32[2,3,8,64,128]{4,3,2,1,0:T(8,128)S(1)} %bitcast.8, f32[8,64,128]{2,1,0:T(8,128)S(1)} %copy-done.2, f32[8,64,128]{2,1,0:T(8,128)S(1)} %copy-done.3, ...), custom_call_target="tpu_custom_call" | custom-call | flops 10000000 | bytes 10000000 | tf_op jit(solution)/shard_map/middle_terms/pallas_call | solution.py:93
  17.4 1.9 %collective-permute-start.8 = (f32[2,7,32,128]{3,2,1,0:T(8,128)S(1)}, f32[2,7,32,128]{3,2,1,0:T(8,128)S(1)}, u32[]{:S(2)}, u32[]{:S(2)}) collective-permute-start(f32[2,7,32,128]{3,2,1,0:T(8,128)S(1)} %bitcast.17), channel_id=1, source_target_pairs={{0,1},{1,0},{2,3},{3,2},{4,5},{5,4},{6,7},{7,6},{8,9},{9,8},{10,11... | collective-permute-start | bytes 688136 | tf_op jit(solution)/shard_map/ppermute | solution.py:393
  19.3 0.0 collective-permute-done.4.far_fwd_ref
  19.3 0.3 %edge_terms.1 = (f32[2,64,128]{2,1,0:T(8,128)S(1)}, f32[4,64,128]{2,1,0:T(8,128)S(1)}) custom-call(f32[3,8,64,128]{3,2,1,0:T(8,128)S(1)} %bitcast.15, f32[2,3,8,64,128]{4,3,2,1,0:T(8,128)S(1)} %bitcast.9, f32[8,64,128]{2,1,0:T(8,128)S(1)} %copy-done.2, f32[8,64,128]{2,1,0:T(8,128)S(1)} %copy-done.3, f32[3,64,128]{2,1,0:T(8,128)S(1)} %get-tuple-element.30.far_next_ref, ...), custom_call_target="tpu_custom_call" | custom-call | flops 10000000 | bytes 10000000 | tf_op jit(solution)/shard_map/edge_terms/pallas_call | solution.py:93
  19.6 0.2 collective-permute-done.5.far_next_in_ref
  19.9 1.6 %collective-permute-start.7 = (f32[2,1,32,128]{3,2,1,0:T(8,128)S(1)}, f32[2,1,32,128]{3,2,1,0:T(8,128)S(1)}, u32[]{:S(2)}, u32[]{:S(2)}) collective-permute-start(f32[2,1,32,128]{3,2,1,0:T(8,128)S(1)} %bitcast.18), channel_id=1, source_target_pairs={{0,1},{1,0},{2,3},{3,2},{4,5},{5,4},{6,7},{7,6},{8,9},{9,8},{10,11... | collective-permute-start | bytes 98312 | tf_op jit(solution)/shard_map/ppermute | solution.py:460
  21.4 1.0 %second.1 = (f32[3,8,64,128]{3,2,1,0:T(8,128)S(1)}, f32[3,2,64,128]{3,2,1,0:T(8,128)S(1)}) custom-call(f32[3,8,64,128]{3,2,1,0:T(8,128)S(1)} %bitcast.16, f32[8,64,128]{2,1,0:T(8,128)S(1)} %copy-done.2, f32[8,64,128]{2,1,0:T(8,128)S(1)} %copy-done.3, f32[8,64,128]{2,1,0:T(8,128)S(1)} %get-tuple-element.25.scale_v, ...), custom_call_target="tpu_custom_call" | custom-call | flops 100000000 | bytes 100000000 | tf_op jit(solution)/shard_map/second/pallas_call | solution.py:93
  22.4 0.8 %store_second.1 = (f32[3,8,64,128]{3,2,1,0:T(8,128)}, f32[8,128]{1,0:T(8,128)S(1)}) custom-call(f32[3,8,64,128]{3,2,1,0:T(8,128)S(1)} %get-tuple-element.38.final_v), custom_call_target="tpu_custom_call" | custom-call | flops 100000000 | bytes 100000000 | tf_op jit(solution)/shard_map/store_second/pallas_call | solution.py:93
  23.3 0.0 collective-permute-done.6.far_after_in_ref
  23.3 0.3 %far_second.1.edge_v = f32[3,2,64,128]{3,2,1,0:T(8,128)S(1)} custom-call(f32[8,64,128]{2,1,0:T(8,128)S(1)} %copy-done.2, f32[8,64,128]{2,1,0:T(8,128)S(1)} %copy-done.3, f32[8,64,128]{2,1,0:T(8,128)S(1)} %get-tuple-element.25.scale_v, f32[3,2,64,128]{3,2,1,0:T(8,128)S(1)} %get-tuple-element.40.face_v, f32[3,64,128]{2,1,0:T(8,128)S(1)} %get-tuple-element.30.far_next_ref, ...), custom_call_target="tpu_custom_call" | custom-call | flops 1 | bytes 1 | tf_op jit(solution)/shard_map/far_second/pallas_call | solution.py:93
  23.5 0.6 %collective-permute-done.7.rest_1_ = f32[2,1,32,128]{3,2,1,0:T(8,128)S(1)} collective-permute-done((f32[2,1,32,128]{3,2,1,0:T(8,128)S(1)}, f32[2,1,32,128]{3,2,1,0:T(8,128)S(1)}, u32[]{:S(2)}, u32[]{:S(2)}) %collective-permute-start.7) | collective-permute-done | bytes 32800 | tf_op jit(solution)/shard_map/ppermute | solution.py:460
  24.2 0.0 collective-permute-done.8.rest_3_
  24.2 0.8 %finish.1 = (f32[3,8,64,128]{3,2,1,0:T(8,128)}, f32[8,32,128]{2,1,0:T(8,128)}, f32[8,32,128]{2,1,0:T(8,128)}) custom-call(f32[3,8,64,128]{3,2,1,0:T(8,128)} %get-tuple-element.39.result_ref, f32[3,2,64,128]{3,2,1,0:T(8,128)S(1)} %far_second.1.edge_v, f32[2,1,32,128]{3,2,1,0:T(8,128)S(1)} %get-tuple-element.37.after_ref.rest_0_, ...), custom_call_target="tpu_custom_call", output_to_operand_aliasing={{0}: (0, {})} | custom-call | flops 100000 | bytes 100000 | tf_op jit(solution)/shard_map/finish/pallas_call | solution.py:93
  (1 shorter events, 0.0 us)
Async XLA Ops:
  0.6 7.3 %copy-start = (f32[1,2,3,8,64,128]{5,4,3,2,1,0:T(8,128)S(1)}, f32[1,2,3,8,64,128]{5,4,3,2,1,0:T(8,128)}, u32[]{:S(2)}) copy-start(f32[1,2,3,8,64,128]{5,4,3,2,1,0:T(8,128)} %param.8) | copy-start | bytes 4718596
  0.6 7.3 %copy-start.1 = (f32[1,3,8,64,128]{4,3,2,1,0:T(8,128)S(1)}, f32[1,3,8,64,128]{4,3,2,1,0:T(8,128)}, u32[]{:S(2)}) copy-start(f32[1,3,8,64,128]{4,3,2,1,0:T(8,128)} %param.6) | copy-start | bytes 2359300
  0.7 7.3 %copy-start.2 = (f32[8,64,128]{2,1,0:T(8,128)S(1)}, f32[8,64,128]{2,1,0:T(8,128)}, u32[]{:S(2)}) copy-start(f32[8,64,128]{2,1,0:T(8,128)} %lame_v.13) | copy-start | bytes 786436
  0.7 7.3 %copy-start.3 = (f32[8,64,128]{2,1,0:T(8,128)S(1)}, f32[8,64,128]{2,1,0:T(8,128)}, u32[]{:S(2)}) copy-start(f32[8,64,128]{2,1,0:T(8,128)} %shear_v.13) | copy-start | bytes 786436
  2.0 9.7 %collective-permute-start.2 = (f32[4,2,64,128]{3,2,1,0:T(8,128)S(1)}, f32[4,2,64,128]{3,2,1,0:T(8,128)S(1)}, u32[]{:S(2)}, u32[]{:S(2)}) collective-permute-start(f32[4,2,64,128]{3,2,1,0:T(8,128)S(1)} %get-tuple-element.29), channel_id=1, source_target_pairs={{0,30},{2,4},{4,2},{6,8},{8,6},{10,12},{12,10},{14,16},{16,14},{18... | collective-permute-start | bytes 786440 | tf_op jit(solution)/shard_map/ppermute | solution.py:175
  7.5 3.7 %collective-permute-start = (f32[3,2,64,128]{3,2,1,0:T(8,128)S(1)}, f32[3,2,64,128]{3,2,1,0:T(8,128)S(1)}, u32[]{:S(2)}, u32[]{:S(2)}) collective-permute-start(f32[3,2,64,128]{3,2,1,0:T(8,128)S(1)} %get-tuple-element.27), channel_id=1, source_target_pairs={{0,2},{2,0},{4,6},{6,4},{8,10},{10,8},{12,14},{14,12},{16,18},{18,... | collective-permute-start | bytes 589832 | tf_op jit(solution)/shard_map/ppermute | solution.py:173
  7.5 3.7 %collective-permute-start.1 = (f32[2,64,128]{2,1,0:T(8,128)S(1)}, f32[2,64,128]{2,1,0:T(8,128)S(1)}, u32[]{:S(2)}, u32[]{:S(2)}) collective-permute-start(f32[2,64,128]{2,1,0:T(8,128)S(1)} %get-tuple-element.28), channel_id=1, source_target_pairs={{0,2},{2,0},{4,6},{6,4},{8,10},{10,8},{12,14},{14,12},{16,18},{18,... | collective-permute-start | bytes 196616 | tf_op jit(solution)/shard_map/ppermute | solution.py:174
  10.8 8.5 %collective-permute-start.4 = (f32[2,3,64,128]{3,2,1,0:T(8,128)S(1)}, f32[2,3,64,128]{3,2,1,0:T(8,128)S(1)}, u32[]{:S(2)}, u32[]{:S(2)}) collective-permute-start(f32[2,3,64,128]{3,2,1,0:T(8,128)S(1)} %get-tuple-element.32), channel_id=1, source_target_pairs={{0,30},{2,4},{4,2},{6,8},{8,6},{10,12},{12,10},{14,16},{16,14},{18... | collective-permute-start | bytes 589832 | tf_op jit(solution)/shard_map/ppermute | solution.py:263
  11.5 5.0 %collective-permute-start.3 = (f32[12,64,128]{2,1,0:T(8,128)S(1)}, f32[12,64,128]{2,1,0:T(8,128)S(1)}, u32[]{:S(2)}, u32[]{:S(2)}) collective-permute-start(f32[12,64,128]{2,1,0:T(8,128)S(1)} %near_first.1.after_ref.near_next_v), channel_id=1, source_target_pairs={{0,2},{2,0},{4,6},{6,4},{8,10},{10,8},{12,14},{14,12},{16,18},{18,... | collective-permute-start | bytes 1179656 | tf_op jit(solution)/shard_map/ppermute | solution.py:301
  11.9 7.9 %collective-permute-start.5 = (f32[3,64,128]{2,1,0:T(8,128)S(1)}, f32[3,64,128]{2,1,0:T(8,128)S(1)}, u32[]{:S(2)}, u32[]{:S(2)}) collective-permute-start(f32[3,64,128]{2,1,0:T(8,128)S(1)} %get-tuple-element.30.far_next_ref), channel_id=1, source_target_pairs={{0,30},{2,4},{4,2},{6,8},{8,6},{10,12},{12,10},{14,16},{16,14},{18... | collective-permute-start | bytes 294920 | tf_op jit(solution)/shard_map/ppermute | solution.py:333
  16.4 6.8 %collective-permute-start.6 = (f32[3,64,128]{2,1,0:T(8,128)S(1)}, f32[3,64,128]{2,1,0:T(8,128)S(1)}, u32[]{:S(2)}, u32[]{:S(2)}) collective-permute-start(f32[3,64,128]{2,1,0:T(8,128)S(1)} %get-tuple-element.31.far_after_ref), channel_id=1, source_target_pairs={{0,30},{2,4},{4,2},{6,8},{8,6},{10,12},{12,10},{14,16},{16,14},{18... | collective-permute-start | bytes 294920 | tf_op jit(solution)/shard_map/ppermute | solution.py:334
  17.4 6.8 %collective-permute-start.8 = (f32[2,7,32,128]{3,2,1,0:T(8,128)S(1)}, f32[2,7,32,128]{3,2,1,0:T(8,128)S(1)}, u32[]{:S(2)}, u32[]{:S(2)}) collective-permute-start(f32[2,7,32,128]{3,2,1,0:T(8,128)S(1)} %bitcast.17), channel_id=1, source_target_pairs={{0,1},{1,0},{2,3},{3,2},{4,5},{5,4},{6,7},{7,6},{8,9},{9,8},{10,11... | collective-permute-start | bytes 688136 | tf_op jit(solution)/shard_map/ppermute | solution.py:393
  19.9 4.3 %collective-permute-start.7 = (f32[2,1,32,128]{3,2,1,0:T(8,128)S(1)}, f32[2,1,32,128]{3,2,1,0:T(8,128)S(1)}, u32[]{:S(2)}, u32[]{:S(2)}) collective-permute-start(f32[2,1,32,128]{3,2,1,0:T(8,128)S(1)} %bitcast.18), channel_id=1, source_target_pairs={{0,1},{1,0},{2,3},{3,2},{4,5},{5,4},{6,7},{7,6},{8,9},{9,8},{10,11... | collective-permute-start | bytes 98312 | tf_op jit(solution)/shard_map/ppermute | solution.py:460

commit v7 on v6

--- a/solution.py
+++ b/solution.py
@@ -519,20 +519,19 @@
         [pltpu.VMEM((3, cells + 1, *plane), jnp.float32), pltpu.VMEM(now.shape, jnp.float32)],
     )
 
-    def store_second(final_v, out_ref, done_ref, sem):
+    def store_second(final_v, out_ref, sem):
         place_ref = where()
         inner = pl.ds(2 - 2 * place_ref[0], cells - 2)
         copy = pltpu.make_async_copy(final_v.at[:, inner], out_ref.at[:, inner], sem)
         copy.start()
         copy.wait()
-        done_ref[...] = jnp.zeros((8, lanes), jnp.float32)
-
-    result, done = call(
-        store_second, [now.shape, (8, lanes)], (final_v,), [VM], [ANY, VM], [pltpu.SemaphoreType.DMA(())]
-    )
-
-    def far_second(lame_v, shear_v, scale_v, face_v, far_next_ref, far_after_ref, far_ref,
-        far_next_in_ref, far_after_in_ref, after_ref, edge_v,
+
+    (result,) = call(
+        store_second, [now.shape], (final_v,), [VM], [ANY], [pltpu.SemaphoreType.DMA(())]
+    )
+
+    def far_second(result_ref, lame_v, shear_v, scale_v, face_v, far_next_ref, far_after_ref, far_ref,
+        far_next_in_ref, far_after_in_ref, out_ref, done_ref, edge_v, sem,
     ):
         place_ref = where()
         sigma = sign(place_ref)
@@ -558,22 +557,25 @@
             after = face_v[b, 1] - scale_v[1] * normal[b]
             edge_v[b, odd] = first * sigma if b == 0 else first
             edge_v[b, 1 - odd] = after * sigma if b == 0 else after
-
-    (edge,) = call(
+        copy = pltpu.make_async_copy(edge_v, out_ref.at[:, pl.ds(odd * (cells - 2), 2)], sem)
+        copy.start()
+        done_ref[...] = jnp.zeros((8, lanes), jnp.float32)
+        copy.wait()
+
+    result, done = call(
         far_second,
-        [(3, 2, *plane)],
-        (lame_v, shear_v, scale_v, face_v, far_next, far_after, far_in, far_next_in, far_after_in, done),
-        [VM] * 10,
-        [VM],
-    )
-
-    def finish(result_ref, edge_v, *rest):
-        pieces, (out_ref, *band_refs, band_v, sem) = rest[: 2 * events], rest[2 * events :]
-        place_ref = where()
-        copies = [
-            pltpu.make_async_copy(edge_v, out_ref.at[:, pl.ds(place_ref[0] * (cells - 2), 2)], sem.at[0])
-        ]
-        copies[0].start()
+        [now.shape, (8, lanes)],
+        (result, lame_v, shear_v, scale_v, face_v, far_next, far_after, far_in, far_next_in, far_after_in),
+        [ANY] + [VM] * 9,
+        [ANY, VM],
+        [pltpu.VMEM((3, 2, *plane), jnp.float32), pltpu.SemaphoreType.DMA(())],
+        aliases={0: 0},
+    )
+
+    def finish(after_ref, *rest):
+        pieces, (*band_refs, band_v, sem) = rest[: 2 * events], rest[2 * events :]
+        place_ref = where()
+        copies = []
         for k in range(2):
             groups = (([0], pieces[:events]), (middle, pieces[events:]))
             for layers, (own, *others_parts) in groups:
@@ -582,19 +584,18 @@
                     for part in others_parts:
                         value = value + part[k, j]
                     band_v[k, layer(place_ref, t)] = value
-            copies.append(pltpu.make_async_copy(band_v.at[k], band_refs[k], sem.at[1 + k]))
+            copies.append(pltpu.make_async_copy(band_v.at[k], band_refs[k], sem.at[k]))
             copies[-1].start()
         for copy in copies:
             copy.wait()
 
-    result, band_shear, band_bulk = call(
+    band_shear, band_bulk = call(
         finish,
-        [now.shape, (cells, band, lanes), (cells, band, lanes)],
-        (result, edge, far_keep, *far_shared, keep_mid, *shared_mid),
-        [ANY] + [VM] * (1 + 2 * events),
-        [ANY] * 3,
-        [pltpu.VMEM((2, cells, band, lanes), jnp.float32), pltpu.SemaphoreType.DMA((3,))],
-        aliases={0: 0},
+        [(cells, band, lanes)] * 2,
+        (done, far_keep, *far_shared, keep_mid, *shared_mid),
+        [VM] * (1 + 2 * events),
+        [ANY] * 2,
+        [pltpu.VMEM((2, cells, band, lanes), jnp.float32), pltpu.SemaphoreType.DMA((2,))],
     )
     return (result[None], band_shear, band_bulk)
 

time: 25.1 us -> 25.1 us (level)
  Pallas kernels: 8.77 us -> 9.39 us
  waiting for transfers between devices: 0.88 us -> 0.26 us
    ppermute x1, waiting for transfers between devices: 0.63 us -> 0.01 us  [local(): lax.ppermute(far_send[i], 'event', others[i])]
    pallas_call x11, Pallas kernels: 8.77 us -> 9.39 us  [call(): pl.pallas_call(kernel, out_shape=shapes, in_specs=[pl.BlockSpec(memory_sp...]
  transfers between devices with their start and end apart: 9 -> 9, of which waited for: 3 -> 2; matrix products, arithmetic and copies ran while one was open for 0% -> 0% of each run, Pallas kernels for 27% -> 30%
where the time goes in v7:
time: 25.1 us; the launch traced here: 25 us
  starting transfers between devices  14.6 us (58%)
  Pallas kernels  9.39 us (37%)
  between operations  0.77 us (3%)
  waiting for transfers between devices  0.26 us (1%)
    pallas_call x11, Pallas kernels, call(): pl.pallas_call(kernel, out_shape=shapes, in_specs=[pl.BlockSpec(memory_sp...  9.39 us
    ppermute x1, starting transfers between devices, local(): far_in = lax.ppermute(far_out, 'blk', far)  5.51 us
    ppermute x1, starting transfers between devices, local(): far_next_in = lax.ppermute(far_next, 'blk', far)  4.51 us
    ppermute x1, starting transfers between devices, local(): lax.ppermute(send_mid[i], 'event', others[i])  1.92 us
    ppermute x1, starting transfers between devices, local(): lax.ppermute(far_send[i], 'event', others[i])  1.57 us
    ppermute x1, starting transfers between devices, local(): near_model_in = lax.ppermute(near_model_out, 'blk', near)  0.51 us
  transfers between devices with their start and end apart: 9, of which 2 were waited for; matrix products, arithmetic and copies ran while one was open for 0% of the time, Pallas kernels for 30%

profile of v7, /device:TPU:0, one launch (start us, length us, event | category | flops | bytes accessed | tf_op | source)
XLA Modules:
  0.0 25.0 jit_solution(15077813054385138730)
XLA Ops:
  0.6 0.0 copy-start
  0.6 0.0 copy-start.1
  0.7 0.0 copy-start.2
  0.7 0.0 copy-start.3
  0.7 1.3 %pack.1 = (f32[3,2,64,128]{3,2,1,0:T(8,128)S(1)}, f32[2,64,128]{2,1,0:T(8,128)S(1)}, f32[4,2,64,128]{3,2,1,0:T(8,128)S(1)}) custom-call(f32[3,8,64,128]{3,2,1,0:T(8,128)} %bitcast.10, f32[8,64,128]{2,1,0:T(8,128)} %lame_v.13, f32[8,64,128]{2,1,0:T(8,128)} %shear_v.13), custom_call_target="tpu_custom_call" | custom-call | flops 1000000000 | bytes 1000000000 | tf_op jit(solution)/shard_map/pack/pallas_call | solution.py:93
  2.0 5.5 %collective-permute-start.2 = (f32[4,2,64,128]{3,2,1,0:T(8,128)S(1)}, f32[4,2,64,128]{3,2,1,0:T(8,128)S(1)}, u32[]{:S(2)}, u32[]{:S(2)}) collective-permute-start(f32[4,2,64,128]{3,2,1,0:T(8,128)S(1)} %get-tuple-element.28), channel_id=1, source_target_pairs={{0,30},{2,4},{4,2},{6,8},{8,6},{10,12},{12,10},{14,16},{16,14},{18... | collective-permute-start | bytes 786440 | tf_op jit(solution)/shard_map/ppermute | solution.py:175
  7.5 0.0 collective-permute-start
  7.5 0.5 %collective-permute-start.1 = (f32[2,64,128]{2,1,0:T(8,128)S(1)}, f32[2,64,128]{2,1,0:T(8,128)S(1)}, u32[]{:S(2)}, u32[]{:S(2)}) collective-permute-start(f32[2,64,128]{2,1,0:T(8,128)S(1)} %get-tuple-element.27), channel_id=1, source_target_pairs={{0,2},{2,0},{4,6},{6,4},{8,10},{10,8},{12,14},{14,12},{16,18},{18,... | collective-permute-start | bytes 196616 | tf_op jit(solution)/shard_map/ppermute | solution.py:174
  8.0 0.0 copy-done
  8.0 0.0 copy-done.1
  8.0 0.0 copy-done.2
  8.0 0.0 copy-done.3
  8.0 2.8 %inner_first.1 = (f32[8,64,128]{2,1,0:T(8,128)S(1)}, f32[3,8,64,128]{3,2,1,0:T(8,128)S(1)}, f32[2,7,64,128]{3,2,1,0:T(8,128)S(1)}, f32[2,3,64,128]{3,2,1,0:T(8,128)S(1)}) custom-call(f32[3,8,64,128]{3,2,1,0:T(8,128)S(1)} %bitcast.11, f32[3,8,64,128]{3,2,1,0:T(8,128)} %bitcast.20, f32[2,3,8,64,128]{4,3,2,1,0:T(8,128)S(1)} %bitcast.6, f32[8,64,128]{2,1,0:T(8,128)} %dens_ref.1, ...), custom_call_target="tpu_custom_call" | custom-call | flops 1000000000 | bytes 1000000000 | tf_op jit(solution)/shard_map/inner_first/pallas_call | solution.py:93
  10.8 0.4 %collective-permute-start.4 = (f32[2,3,64,128]{3,2,1,0:T(8,128)S(1)}, f32[2,3,64,128]{3,2,1,0:T(8,128)S(1)}, u32[]{:S(2)}, u32[]{:S(2)}) collective-permute-start(f32[2,3,64,128]{3,2,1,0:T(8,128)S(1)} %get-tuple-element.31), channel_id=1, source_target_pairs={{0,30},{2,4},{4,2},{6,8},{8,6},{10,12},{12,10},{14,16},{16,14},{18... | collective-permute-start | bytes 589832 | tf_op jit(solution)/shard_map/ppermute | solution.py:263
  11.2 0.0 collective-permute-done.1.near_model_ref
  11.2 0.0 collective-permute-done.near_ref
  11.2 0.3 %near_first.1.after_ref.near_next_v = f32[12,64,128]{2,1,0:T(8,128)S(1)} custom-call(f32[3,8,64,128]{3,2,1,0:T(8,128)S(1)} %bitcast.12, f32[2,3,8,64,128]{4,3,2,1,0:T(8,128)S(1)} %bitcast.7, f32[8,64,128]{2,1,0:T(8,128)S(1)} %copy-done.2, f32[8,64,128]{2,1,0:T(8,128)S(1)} %copy-done.3, f32[8,64,128]{2,1,0:T(8,128)S(1)} %get-tuple-element.24.scale_v, ...), custom_call_target="tpu_custom_call" | custom-call | flops 1000000 | bytes 1000000 | tf_op jit(solution)/shard_map/near_first/pallas_call | solution.py:93
  11.5 0.1 collective-permute-start.3
  11.6 0.1 collective-permute-done.2.far_ref
  11.6 0.3 %far_first.1 = (f32[3,64,128]{2,1,0:T(8,128)S(1)}, f32[3,64,128]{2,1,0:T(8,128)S(1)}) custom-call(f32[3,8,64,128]{3,2,1,0:T(8,128)S(1)} %bitcast.13, f32[8,64,128]{2,1,0:T(8,128)S(1)} %copy-done.2, f32[8,64,128]{2,1,0:T(8,128)S(1)} %copy-done.3, f32[8,64,128]{2,1,0:T(8,128)S(1)} %get-tuple-element.24.scale_v, ...), custom_call_target="tpu_custom_call" | custom-call | flops 10000000000 | bytes 10000000000 | tf_op jit(solution)/shard_map/far_first/pallas_call | solution.py:93
  11.9 4.5 %collective-permute-start.5 = (f32[3,64,128]{2,1,0:T(8,128)S(1)}, f32[3,64,128]{2,1,0:T(8,128)S(1)}, u32[]{:S(2)}, u32[]{:S(2)}) collective-permute-start(f32[3,64,128]{2,1,0:T(8,128)S(1)} %get-tuple-element.29.far_next_ref), channel_id=1, source_target_pairs={{0,30},{2,4},{4,2},{6,8},{8,6},{10,12},{12,10},{14,16},{16,14},{18... | collective-permute-start | bytes 294920 | tf_op jit(solution)/shard_map/ppermute | solution.py:333
  16.4 0.1 collective-permute-start.6
  16.5 0.0 collective-permute-done.3.near_next_ref
  16.5 0.9 %middle_terms.1 = (f32[2,7,32,128]{3,2,1,0:T(8,128)S(1)}, f32[1,2,7,32,128]{4,3,2,1,0:T(8,128)S(1)}) custom-call(f32[3,8,64,128]{3,2,1,0:T(8,128)S(1)} %bitcast.14, f32[2,3,8,64,128]{4,3,2,1,0:T(8,128)S(1)} %bitcast.8, f32[8,64,128]{2,1,0:T(8,128)S(1)} %copy-done.2, f32[8,64,128]{2,1,0:T(8,128)S(1)} %copy-done.3, ...), custom_call_target="tpu_custom_call" | custom-call | flops 10000000 | bytes 10000000 | tf_op jit(solution)/shard_map/middle_terms/pallas_call | solution.py:93
  17.4 1.9 %collective-permute-start.8 = (f32[2,7,32,128]{3,2,1,0:T(8,128)S(1)}, f32[2,7,32,128]{3,2,1,0:T(8,128)S(1)}, u32[]{:S(2)}, u32[]{:S(2)}) collective-permute-start(f32[2,7,32,128]{3,2,1,0:T(8,128)S(1)} %bitcast.17), channel_id=1, source_target_pairs={{0,1},{1,0},{2,3},{3,2},{4,5},{5,4},{6,7},{7,6},{8,9},{9,8},{10,11... | collective-permute-start | bytes 688136 | tf_op jit(solution)/shard_map/ppermute | solution.py:393
  19.3 0.0 collective-permute-done.4.far_fwd_ref
  19.3 0.3 %edge_terms.1 = (f32[2,64,128]{2,1,0:T(8,128)S(1)}, f32[4,64,128]{2,1,0:T(8,128)S(1)}) custom-call(f32[3,8,64,128]{3,2,1,0:T(8,128)S(1)} %bitcast.15, f32[2,3,8,64,128]{4,3,2,1,0:T(8,128)S(1)} %bitcast.9, f32[8,64,128]{2,1,0:T(8,128)S(1)} %copy-done.2, f32[8,64,128]{2,1,0:T(8,128)S(1)} %copy-done.3, f32[3,64,128]{2,1,0:T(8,128)S(1)} %get-tuple-element.29.far_next_ref, ...), custom_call_target="tpu_custom_call" | custom-call | flops 10000000 | bytes 10000000 | tf_op jit(solution)/shard_map/edge_terms/pallas_call | solution.py:93
  19.6 0.2 collective-permute-done.5.far_next_in_ref
  19.9 1.6 %collective-permute-start.7 = (f32[2,1,32,128]{3,2,1,0:T(8,128)S(1)}, f32[2,1,32,128]{3,2,1,0:T(8,128)S(1)}, u32[]{:S(2)}, u32[]{:S(2)}) collective-permute-start(f32[2,1,32,128]{3,2,1,0:T(8,128)S(1)} %bitcast.18), channel_id=1, source_target_pairs={{0,1},{1,0},{2,3},{3,2},{4,5},{5,4},{6,7},{7,6},{8,9},{9,8},{10,11... | collective-permute-start | bytes 98312 | tf_op jit(solution)/shard_map/ppermute | solution.py:460
  21.4 1.0 %second.1 = (f32[3,8,64,128]{3,2,1,0:T(8,128)S(1)}, f32[3,2,64,128]{3,2,1,0:T(8,128)S(1)}) custom-call(f32[3,8,64,128]{3,2,1,0:T(8,128)S(1)} %bitcast.16, f32[8,64,128]{2,1,0:T(8,128)S(1)} %copy-done.2, f32[8,64,128]{2,1,0:T(8,128)S(1)} %copy-done.3, f32[8,64,128]{2,1,0:T(8,128)S(1)} %get-tuple-element.24.scale_v, ...), custom_call_target="tpu_custom_call" | custom-call | flops 100000000 | bytes 100000000 | tf_op jit(solution)/shard_map/second/pallas_call | solution.py:93
  22.4 0.8 %store_second.1.result_ref = f32[3,8,64,128]{3,2,1,0:T(8,128)} custom-call(f32[3,8,64,128]{3,2,1,0:T(8,128)S(1)} %get-tuple-element.37.final_v), custom_call_target="tpu_custom_call" | custom-call | flops 100000000 | bytes 100000000 | tf_op jit(solution)/shard_map/store_second/pallas_call | solution.py:93
  23.3 0.0 collective-permute-done.6.far_after_in_ref
  23.3 1.0 %far_second.1 = (f32[3,8,64,128]{3,2,1,0:T(8,128)}, f32[8,128]{1,0:T(8,128)S(1)}) custom-call(f32[3,8,64,128]{3,2,1,0:T(8,128)} %store_second.1.result_ref, f32[8,64,128]{2,1,0:T(8,128)S(1)} %copy-done.2, f32[8,64,128]{2,1,0:T(8,128)S(1)} %copy-done.3, f32[8,64,128]{2,1,0:T(8,128)S(1)} %get-tuple-element.24.scale_v, ...), custom_call_target="tpu_custom_call", output_to_operand_aliasing={{0}: (0, {})} | custom-call | flops 1 | bytes 1 | tf_op jit(solution)/shard_map/far_second/pallas_call | solution.py:93
  24.2 0.0 collective-permute-done.7.rest_1_
  24.2 0.0 collective-permute-done.8.rest_3_
  24.3 0.7 %finish.1 = (f32[8,32,128]{2,1,0:T(8,128)}, f32[8,32,128]{2,1,0:T(8,128)}) custom-call(f32[8,128]{1,0:T(8,128)S(1)} %get-tuple-element.40.after_ref, f32[2,1,32,128]{3,2,1,0:T(8,128)S(1)} %get-tuple-element.36.after_ref.rest_0_, f32[2,1,32,128]{3,2,1,0:T(8,128)S(1)} %collective-permute-done.7.rest_1_, ...), custom_call_target="tpu_custom_call" | custom-call | flops 100000 | bytes 100000 | tf_op jit(solution)/shard_map/finish/pallas_call | solution.py:93
  (1 shorter events, 0.0 us)
Async XLA Ops:
  0.6 7.3 %copy-start = (f32[1,2,3,8,64,128]{5,4,3,2,1,0:T(8,128)S(1)}, f32[1,2,3,8,64,128]{5,4,3,2,1,0:T(8,128)}, u32[]{:S(2)}) copy-start(f32[1,2,3,8,64,128]{5,4,3,2,1,0:T(8,128)} %param.8) | copy-start | bytes 4718596
  0.6 7.3 %copy-start.1 = (f32[1,3,8,64,128]{4,3,2,1,0:T(8,128)S(1)}, f32[1,3,8,64,128]{4,3,2,1,0:T(8,128)}, u32[]{:S(2)}) copy-start(f32[1,3,8,64,128]{4,3,2,1,0:T(8,128)} %param.6) | copy-start | bytes 2359300
  0.7 7.3 %copy-start.2 = (f32[8,64,128]{2,1,0:T(8,128)S(1)}, f32[8,64,128]{2,1,0:T(8,128)}, u32[]{:S(2)}) copy-start(f32[8,64,128]{2,1,0:T(8,128)} %lame_v.13) | copy-start | bytes 786436
  0.7 7.3 %copy-start.3 = (f32[8,64,128]{2,1,0:T(8,128)S(1)}, f32[8,64,128]{2,1,0:T(8,128)}, u32[]{:S(2)}) copy-start(f32[8,64,128]{2,1,0:T(8,128)} %shear_v.13) | copy-start | bytes 786436
  2.0 9.7 %collective-permute-start.2 = (f32[4,2,64,128]{3,2,1,0:T(8,128)S(1)}, f32[4,2,64,128]{3,2,1,0:T(8,128)S(1)}, u32[]{:S(2)}, u32[]{:S(2)}) collective-permute-start(f32[4,2,64,128]{3,2,1,0:T(8,128)S(1)} %get-tuple-element.28), channel_id=1, source_target_pairs={{0,30},{2,4},{4,2},{6,8},{8,6},{10,12},{12,10},{14,16},{16,14},{18... | collective-permute-start | bytes 786440 | tf_op jit(solution)/shard_map/ppermute | solution.py:175
  7.5 3.7 %collective-permute-start = (f32[3,2,64,128]{3,2,1,0:T(8,128)S(1)}, f32[3,2,64,128]{3,2,1,0:T(8,128)S(1)}, u32[]{:S(2)}, u32[]{:S(2)}) collective-permute-start(f32[3,2,64,128]{3,2,1,0:T(8,128)S(1)} %get-tuple-element.26), channel_id=1, source_target_pairs={{0,2},{2,0},{4,6},{6,4},{8,10},{10,8},{12,14},{14,12},{16,18},{18,... | collective-permute-start | bytes 589832 | tf_op jit(solution)/shard_map/ppermute | solution.py:173
  7.5 3.7 %collective-permute-start.1 = (f32[2,64,128]{2,1,0:T(8,128)S(1)}, f32[2,64,128]{2,1,0:T(8,128)S(1)}, u32[]{:S(2)}, u32[]{:S(2)}) collective-permute-start(f32[2,64,128]{2,1,0:T(8,128)S(1)} %get-tuple-element.27), channel_id=1, source_target_pairs={{0,2},{2,0},{4,6},{6,4},{8,10},{10,8},{12,14},{14,12},{16,18},{18,... | collective-permute-start | bytes 196616 | tf_op jit(solution)/shard_map/ppermute | solution.py:174
  10.8 8.5 %collective-permute-start.4 = (f32[2,3,64,128]{3,2,1,0:T(8,128)S(1)}, f32[2,3,64,128]{3,2,1,0:T(8,128)S(1)}, u32[]{:S(2)}, u32[]{:S(2)}) collective-permute-start(f32[2,3,64,128]{3,2,1,0:T(8,128)S(1)} %get-tuple-element.31), channel_id=1, source_target_pairs={{0,30},{2,4},{4,2},{6,8},{8,6},{10,12},{12,10},{14,16},{16,14},{18... | collective-permute-start | bytes 589832 | tf_op jit(solution)/shard_map/ppermute | solution.py:263
  11.5 5.0 %collective-permute-start.3 = (f32[12,64,128]{2,1,0:T(8,128)S(1)}, f32[12,64,128]{2,1,0:T(8,128)S(1)}, u32[]{:S(2)}, u32[]{:S(2)}) collective-permute-start(f32[12,64,128]{2,1,0:T(8,128)S(1)} %near_first.1.after_ref.near_next_v), channel_id=1, source_target_pairs={{0,2},{2,0},{4,6},{6,4},{8,10},{10,8},{12,14},{14,12},{16,18},{18,... | collective-permute-start | bytes 1179656 | tf_op jit(solution)/shard_map/ppermute | solution.py:301
  11.9 7.9 %collective-permute-start.5 = (f32[3,64,128]{2,1,0:T(8,128)S(1)}, f32[3,64,128]{2,1,0:T(8,128)S(1)}, u32[]{:S(2)}, u32[]{:S(2)}) collective-permute-start(f32[3,64,128]{2,1,0:T(8,128)S(1)} %get-tuple-element.29.far_next_ref), channel_id=1, source_target_pairs={{0,30},{2,4},{4,2},{6,8},{8,6},{10,12},{12,10},{14,16},{16,14},{18... | collective-permute-start | bytes 294920 | tf_op jit(solution)/shard_map/ppermute | solution.py:333
  16.4 6.8 %collective-permute-start.6 = (f32[3,64,128]{2,1,0:T(8,128)S(1)}, f32[3,64,128]{2,1,0:T(8,128)S(1)}, u32[]{:S(2)}, u32[]{:S(2)}) collective-permute-start(f32[3,64,128]{2,1,0:T(8,128)S(1)} %get-tuple-element.30.far_after_ref), channel_id=1, source_target_pairs={{0,30},{2,4},{4,2},{6,8},{8,6},{10,12},{12,10},{14,16},{16,14},{18... | collective-permute-start | bytes 294920 | tf_op jit(solution)/shard_map/ppermute | solution.py:334
  17.4 6.9 %collective-permute-start.8 = (f32[2,7,32,128]{3,2,1,0:T(8,128)S(1)}, f32[2,7,32,128]{3,2,1,0:T(8,128)S(1)}, u32[]{:S(2)}, u32[]{:S(2)}) collective-permute-start(f32[2,7,32,128]{3,2,1,0:T(8,128)S(1)} %bitcast.17), channel_id=1, source_target_pairs={{0,1},{1,0},{2,3},{3,2},{4,5},{5,4},{6,7},{7,6},{8,9},{9,8},{10,11... | collective-permute-start | bytes 688136 | tf_op jit(solution)/shard_map/ppermute | solution.py:393
  19.9 4.4 %collective-permute-start.7 = (f32[2,1,32,128]{3,2,1,0:T(8,128)S(1)}, f32[2,1,32,128]{3,2,1,0:T(8,128)S(1)}, u32[]{:S(2)}, u32[]{:S(2)}) collective-permute-start(f32[2,1,32,128]{3,2,1,0:T(8,128)S(1)} %bitcast.18), channel_id=1, source_target_pairs={{0,1},{1,0},{2,3},{3,2},{4,5},{5,4},{6,7},{7,6},{8,9},{9,8},{10,11... | collective-permute-start | bytes 98312 | tf_op jit(solution)/shard_map/ppermute | solution.py:460

commit v8 on v7

--- a/solution.py
+++ b/solution.py
@@ -55,14 +55,15 @@
     return (2.0 * shear * parts[0] + lame * parts[6], shear * parts[3], shear * parts[4])
 
 
-def cross_force(parts, normal, lame, shear, tools):
+def cross_force(parts, normal, lame, shear, tools, matrix=True):
     along_rows, along_lanes, along_lanes_three = tools
     pressure = lame * parts[6]
     twice = 2.0 * shear
     s_22 = twice * parts[1] + pressure
     s_33 = twice * parts[2] + pressure
     s_23 = shear * parts[5]
-    third_of = along_lanes_three((normal[2], s_23, s_33))
+    fields = (normal[2], s_23, s_33)
+    third_of = along_lanes_three(fields) if matrix else [along_lanes(field) for field in fields]
     return (
         along_rows(normal[1]) + third_of[0],
         along_rows(s_22) + third_of[1],
@@ -284,7 +285,7 @@
         lame, shear = lame_v[at(last)], shear_v[at(last)]
         parts = strain_parts(field(last - 1), field(last), field(cells), tools)
         normal = normal_stress(parts, lame, shear)
-        force = cross_force(parts, normal, lame, shear, tools)
+        force = cross_force(parts, normal, lame, shear, tools, False)
         for b in range(3):
             near_next[b] = next_v[b, last] + scale_v[last] * (force[b] + outer[b])
             near_next[3 + b] = next_v[b, last - 1] + scale_v[last - 1] * normal[b]
@@ -318,7 +319,7 @@
         lame, shear = lame_v[at(0)], shear_v[at(0)]
         parts = strain_parts(field(-1), field(0), field(1), tools)
         normal = normal_stress(parts, lame, shear)
-        force = cross_force(parts, normal, lame, shear, tools)
+        force = cross_force(parts, normal, lame, shear, tools, False)
         for b in range(3):
             far_next[b] = next_v[b, 0] + scale_v[0] * (force[b] - outer[b])
             far_after[b] = next_v[b, 1] - scale_v[1] * normal[b]

time: 25.1 us -> 25.1 us (level)
  transfers between devices with their start and end apart: 9 -> 9, of which waited for: 2 -> 2; matrix products, arithmetic and copies ran while one was open for 0% -> 0% of each run, Pallas kernels for 30% -> 29%
where the time goes in v8:
time: 25.1 us; the launch traced here: 25 us
  starting transfers between devices  14.6 us (58%)
  Pallas kernels  9.36 us (37%)
  between operations  0.77 us (3%)
  waiting for transfers between devices  0.29 us (1%)
    pallas_call x11, Pallas kernels, call(): pl.pallas_call(kernel, out_shape=shapes, in_specs=[pl.BlockSpec(memory_sp...  9.36 us
    ppermute x1, starting transfers between devices, local(): far_in = lax.ppermute(far_out, 'blk', far)  5.51 us
    ppermute x1, starting transfers between devices, local(): far_next_in = lax.ppermute(far_next, 'blk', far)  4.51 us
    ppermute x1, starting transfers between devices, local(): lax.ppermute(send_mid[i], 'event', others[i])  1.92 us
    ppermute x1, starting transfers between devices, local(): lax.ppermute(far_send[i], 'event', others[i])  1.57 us
    ppermute x1, starting transfers between devices, local(): near_model_in = lax.ppermute(near_model_out, 'blk', near)  0.51 us
  transfers between devices with their start and end apart: 9, of which 2 were waited for; matrix products, arithmetic and copies ran while one was open for 0% of the time, Pallas kernels for 29%

profile of v8, /device:TPU:0, one launch (start us, length us, event | category | flops | bytes accessed | tf_op | source)
XLA Modules:
  0.0 25.0 jit_solution(9343418580183240640)
XLA Ops:
  0.6 0.0 copy-start
  0.6 0.0 copy-start.1
  0.7 0.0 copy-start.2
  0.7 0.0 copy-start.3
  0.7 1.3 %pack.1 = (f32[3,2,64,128]{3,2,1,0:T(8,128)S(1)}, f32[2,64,128]{2,1,0:T(8,128)S(1)}, f32[4,2,64,128]{3,2,1,0:T(8,128)S(1)}) custom-call(f32[3,8,64,128]{3,2,1,0:T(8,128)} %bitcast.10, f32[8,64,128]{2,1,0:T(8,128)} %lame_v.13, f32[8,64,128]{2,1,0:T(8,128)} %shear_v.13), custom_call_target="tpu_custom_call" | custom-call | flops 1000000000 | bytes 1000000000 | tf_op jit(solution)/shard_map/pack/pallas_call | solution.py:94
  2.0 5.5 %collective-permute-start.2 = (f32[4,2,64,128]{3,2,1,0:T(8,128)S(1)}, f32[4,2,64,128]{3,2,1,0:T(8,128)S(1)}, u32[]{:S(2)}, u32[]{:S(2)}) collective-permute-start(f32[4,2,64,128]{3,2,1,0:T(8,128)S(1)} %get-tuple-element.28), channel_id=1, source_target_pairs={{0,30},{2,4},{4,2},{6,8},{8,6},{10,12},{12,10},{14,16},{16,14},{18... | collective-permute-start | bytes 786440 | tf_op jit(solution)/shard_map/ppermute | solution.py:176
  7.5 0.0 collective-permute-start
  7.5 0.5 %collective-permute-start.1 = (f32[2,64,128]{2,1,0:T(8,128)S(1)}, f32[2,64,128]{2,1,0:T(8,128)S(1)}, u32[]{:S(2)}, u32[]{:S(2)}) collective-permute-start(f32[2,64,128]{2,1,0:T(8,128)S(1)} %get-tuple-element.27), channel_id=1, source_target_pairs={{0,2},{2,0},{4,6},{6,4},{8,10},{10,8},{12,14},{14,12},{16,18},{18,... | collective-permute-start | bytes 196616 | tf_op jit(solution)/shard_map/ppermute | solution.py:175
  8.0 0.0 copy-done
  8.0 0.0 copy-done.1
  8.0 0.0 copy-done.2
  8.0 0.0 copy-done.3
  8.0 2.8 %inner_first.1 = (f32[8,64,128]{2,1,0:T(8,128)S(1)}, f32[3,8,64,128]{3,2,1,0:T(8,128)S(1)}, f32[2,7,64,128]{3,2,1,0:T(8,128)S(1)}, f32[2,3,64,128]{3,2,1,0:T(8,128)S(1)}) custom-call(f32[3,8,64,128]{3,2,1,0:T(8,128)S(1)} %bitcast.11, f32[3,8,64,128]{3,2,1,0:T(8,128)} %bitcast.20, f32[2,3,8,64,128]{4,3,2,1,0:T(8,128)S(1)} %bitcast.6, f32[8,64,128]{2,1,0:T(8,128)} %dens_ref.1, ...), custom_call_target="tpu_custom_call" | custom-call | flops 1000000000 | bytes 1000000000 | tf_op jit(solution)/shard_map/inner_first/pallas_call | solution.py:94
  10.8 0.4 %collective-permute-start.4 = (f32[2,3,64,128]{3,2,1,0:T(8,128)S(1)}, f32[2,3,64,128]{3,2,1,0:T(8,128)S(1)}, u32[]{:S(2)}, u32[]{:S(2)}) collective-permute-start(f32[2,3,64,128]{3,2,1,0:T(8,128)S(1)} %get-tuple-element.31), channel_id=1, source_target_pairs={{0,30},{2,4},{4,2},{6,8},{8,6},{10,12},{12,10},{14,16},{16,14},{18... | collective-permute-start | bytes 589832 | tf_op jit(solution)/shard_map/ppermute | solution.py:264
  11.2 0.0 collective-permute-done.1.near_model_ref
  11.2 0.0 collective-permute-done.near_ref
  11.2 0.3 %near_first.1.after_ref.near_next_v = f32[12,64,128]{2,1,0:T(8,128)S(1)} custom-call(f32[3,8,64,128]{3,2,1,0:T(8,128)S(1)} %bitcast.12, f32[2,3,8,64,128]{4,3,2,1,0:T(8,128)S(1)} %bitcast.7, f32[8,64,128]{2,1,0:T(8,128)S(1)} %copy-done.2, f32[8,64,128]{2,1,0:T(8,128)S(1)} %copy-done.3, f32[8,64,128]{2,1,0:T(8,128)S(1)} %get-tuple-element.24.scale_v, ...), custom_call_target="tpu_custom_call" | custom-call | flops 1000000 | bytes 1000000 | tf_op jit(solution)/shard_map/near_first/pallas_call | solution.py:94
  11.5 0.1 collective-permute-start.3
  11.5 0.1 collective-permute-done.2.far_ref
  11.6 0.3 %far_first.1 = (f32[3,64,128]{2,1,0:T(8,128)S(1)}, f32[3,64,128]{2,1,0:T(8,128)S(1)}) custom-call(f32[3,8,64,128]{3,2,1,0:T(8,128)S(1)} %bitcast.13, f32[8,64,128]{2,1,0:T(8,128)S(1)} %copy-done.2, f32[8,64,128]{2,1,0:T(8,128)S(1)} %copy-done.3, f32[8,64,128]{2,1,0:T(8,128)S(1)} %get-tuple-element.24.scale_v, ...), custom_call_target="tpu_custom_call" | custom-call | flops 10000000000 | bytes 10000000000 | tf_op jit(solution)/shard_map/far_first/pallas_call | solution.py:94
  11.9 4.5 %collective-permute-start.5 = (f32[3,64,128]{2,1,0:T(8,128)S(1)}, f32[3,64,128]{2,1,0:T(8,128)S(1)}, u32[]{:S(2)}, u32[]{:S(2)}) collective-permute-start(f32[3,64,128]{2,1,0:T(8,128)S(1)} %get-tuple-element.29.far_next_ref), channel_id=1, source_target_pairs={{0,30},{2,4},{4,2},{6,8},{8,6},{10,12},{12,10},{14,16},{16,14},{18... | collective-permute-start | bytes 294920 | tf_op jit(solution)/shard_map/ppermute | solution.py:334
  16.4 0.1 collective-permute-start.6
  16.5 0.0 collective-permute-done.3.near_next_ref
  16.5 0.9 %middle_terms.1 = (f32[2,7,32,128]{3,2,1,0:T(8,128)S(1)}, f32[1,2,7,32,128]{4,3,2,1,0:T(8,128)S(1)}) custom-call(f32[3,8,64,128]{3,2,1,0:T(8,128)S(1)} %bitcast.14, f32[2,3,8,64,128]{4,3,2,1,0:T(8,128)S(1)} %bitcast.8, f32[8,64,128]{2,1,0:T(8,128)S(1)} %copy-done.2, f32[8,64,128]{2,1,0:T(8,128)S(1)} %copy-done.3, ...), custom_call_target="tpu_custom_call" | custom-call | flops 10000000 | bytes 10000000 | tf_op jit(solution)/shard_map/middle_terms/pallas_call | solution.py:94
  17.4 1.9 %collective-permute-start.8 = (f32[2,7,32,128]{3,2,1,0:T(8,128)S(1)}, f32[2,7,32,128]{3,2,1,0:T(8,128)S(1)}, u32[]{:S(2)}, u32[]{:S(2)}) collective-permute-start(f32[2,7,32,128]{3,2,1,0:T(8,128)S(1)} %bitcast.17), channel_id=1, source_target_pairs={{0,1},{1,0},{2,3},{3,2},{4,5},{5,4},{6,7},{7,6},{8,9},{9,8},{10,11... | collective-permute-start | bytes 688136 | tf_op jit(solution)/shard_map/ppermute | solution.py:394
  19.3 0.0 collective-permute-done.4.far_fwd_ref
  19.3 0.3 %edge_terms.1 = (f32[2,64,128]{2,1,0:T(8,128)S(1)}, f32[4,64,128]{2,1,0:T(8,128)S(1)}) custom-call(f32[3,8,64,128]{3,2,1,0:T(8,128)S(1)} %bitcast.15, f32[2,3,8,64,128]{4,3,2,1,0:T(8,128)S(1)} %bitcast.9, f32[8,64,128]{2,1,0:T(8,128)S(1)} %copy-done.2, f32[8,64,128]{2,1,0:T(8,128)S(1)} %copy-done.3, f32[3,64,128]{2,1,0:T(8,128)S(1)} %get-tuple-element.29.far_next_ref, ...), custom_call_target="tpu_custom_call" | custom-call | flops 10000000 | bytes 10000000 | tf_op jit(solution)/shard_map/edge_terms/pallas_call | solution.py:94
  19.6 0.2 collective-permute-done.5.far_next_in_ref
  19.9 1.6 %collective-permute-start.7 = (f32[2,1,32,128]{3,2,1,0:T(8,128)S(1)}, f32[2,1,32,128]{3,2,1,0:T(8,128)S(1)}, u32[]{:S(2)}, u32[]{:S(2)}) collective-permute-start(f32[2,1,32,128]{3,2,1,0:T(8,128)S(1)} %bitcast.18), channel_id=1, source_target_pairs={{0,1},{1,0},{2,3},{3,2},{4,5},{5,4},{6,7},{7,6},{8,9},{9,8},{10,11... | collective-permute-start | bytes 98312 | tf_op jit(solution)/shard_map/ppermute | solution.py:461
  21.4 1.0 %second.1 = (f32[3,8,64,128]{3,2,1,0:T(8,128)S(1)}, f32[3,2,64,128]{3,2,1,0:T(8,128)S(1)}) custom-call(f32[3,8,64,128]{3,2,1,0:T(8,128)S(1)} %bitcast.16, f32[8,64,128]{2,1,0:T(8,128)S(1)} %copy-done.2, f32[8,64,128]{2,1,0:T(8,128)S(1)} %copy-done.3, f32[8,64,128]{2,1,0:T(8,128)S(1)} %get-tuple-element.24.scale_v, ...), custom_call_target="tpu_custom_call" | custom-call | flops 100000000 | bytes 100000000 | tf_op jit(solution)/shard_map/second/pallas_call | solution.py:94
  22.4 0.8 %store_second.1.result_ref = f32[3,8,64,128]{3,2,1,0:T(8,128)} custom-call(f32[3,8,64,128]{3,2,1,0:T(8,128)S(1)} %get-tuple-element.37.final_v), custom_call_target="tpu_custom_call" | custom-call | flops 100000000 | bytes 100000000 | tf_op jit(solution)/shard_map/store_second/pallas_call | solution.py:94
  23.3 0.0 collective-permute-done.6.far_after_in_ref
  23.3 1.0 %far_second.1 = (f32[3,8,64,128]{3,2,1,0:T(8,128)}, f32[8,128]{1,0:T(8,128)S(1)}) custom-call(f32[3,8,64,128]{3,2,1,0:T(8,128)} %store_second.1.result_ref, f32[8,64,128]{2,1,0:T(8,128)S(1)} %copy-done.2, f32[8,64,128]{2,1,0:T(8,128)S(1)} %copy-done.3, f32[8,64,128]{2,1,0:T(8,128)S(1)} %get-tuple-element.24.scale_v, ...), custom_call_target="tpu_custom_call", output_to_operand_aliasing={{0}: (0, {})} | custom-call | flops 1 | bytes 1 | tf_op jit(solution)/shard_map/far_second/pallas_call | solution.py:94
  24.2 0.0 collective-permute-done.7.rest_1_
  24.2 0.0 collective-permute-done.8.rest_3_
  24.3 0.7 %finish.1 = (f32[8,32,128]{2,1,0:T(8,128)}, f32[8,32,128]{2,1,0:T(8,128)}) custom-call(f32[8,128]{1,0:T(8,128)S(1)} %get-tuple-element.40.after_ref, f32[2,1,32,128]{3,2,1,0:T(8,128)S(1)} %get-tuple-element.36.after_ref.rest_0_, f32[2,1,32,128]{3,2,1,0:T(8,128)S(1)} %collective-permute-done.7.rest_1_, ...), custom_call_target="tpu_custom_call" | custom-call | flops 100000 | bytes 100000 | tf_op jit(solution)/shard_map/finish/pallas_call | solution.py:94
  (1 shorter events, 0.0 us)
Async XLA Ops:
  0.6 7.3 %copy-start = (f32[1,2,3,8,64,128]{5,4,3,2,1,0:T(8,128)S(1)}, f32[1,2,3,8,64,128]{5,4,3,2,1,0:T(8,128)}, u32[]{:S(2)}) copy-start(f32[1,2,3,8,64,128]{5,4,3,2,1,0:T(8,128)} %param.8) | copy-start | bytes 4718596
  0.6 7.3 %copy-start.1 = (f32[1,3,8,64,128]{4,3,2,1,0:T(8,128)S(1)}, f32[1,3,8,64,128]{4,3,2,1,0:T(8,128)}, u32[]{:S(2)}) copy-start(f32[1,3,8,64,128]{4,3,2,1,0:T(8,128)} %param.6) | copy-start | bytes 2359300
  0.7 7.3 %copy-start.2 = (f32[8,64,128]{2,1,0:T(8,128)S(1)}, f32[8,64,128]{2,1,0:T(8,128)}, u32[]{:S(2)}) copy-start(f32[8,64,128]{2,1,0:T(8,128)} %lame_v.13) | copy-start | bytes 786436
  0.7 7.3 %copy-start.3 = (f32[8,64,128]{2,1,0:T(8,128)S(1)}, f32[8,64,128]{2,1,0:T(8,128)}, u32[]{:S(2)}) copy-start(f32[8,64,128]{2,1,0:T(8,128)} %shear_v.13) | copy-start | bytes 786436
  2.0 9.7 %collective-permute-start.2 = (f32[4,2,64,128]{3,2,1,0:T(8,128)S(1)}, f32[4,2,64,128]{3,2,1,0:T(8,128)S(1)}, u32[]{:S(2)}, u32[]{:S(2)}) collective-permute-start(f32[4,2,64,128]{3,2,1,0:T(8,128)S(1)} %get-tuple-element.28), channel_id=1, source_target_pairs={{0,30},{2,4},{4,2},{6,8},{8,6},{10,12},{12,10},{14,16},{16,14},{18... | collective-permute-start | bytes 786440 | tf_op jit(solution)/shard_map/ppermute | solution.py:176
  7.5 3.7 %collective-permute-start = (f32[3,2,64,128]{3,2,1,0:T(8,128)S(1)}, f32[3,2,64,128]{3,2,1,0:T(8,128)S(1)}, u32[]{:S(2)}, u32[]{:S(2)}) collective-permute-start(f32[3,2,64,128]{3,2,1,0:T(8,128)S(1)} %get-tuple-element.26), channel_id=1, source_target_pairs={{0,2},{2,0},{4,6},{6,4},{8,10},{10,8},{12,14},{14,12},{16,18},{18,... | collective-permute-start | bytes 589832 | tf_op jit(solution)/shard_map/ppermute | solution.py:174
  7.5 3.7 %collective-permute-start.1 = (f32[2,64,128]{2,1,0:T(8,128)S(1)}, f32[2,64,128]{2,1,0:T(8,128)S(1)}, u32[]{:S(2)}, u32[]{:S(2)}) collective-permute-start(f32[2,64,128]{2,1,0:T(8,128)S(1)} %get-tuple-element.27), channel_id=1, source_target_pairs={{0,2},{2,0},{4,6},{6,4},{8,10},{10,8},{12,14},{14,12},{16,18},{18,... | collective-permute-start | bytes 196616 | tf_op jit(solution)/shard_map/ppermute | solution.py:175
  10.8 8.5 %collective-permute-start.4 = (f32[2,3,64,128]{3,2,1,0:T(8,128)S(1)}, f32[2,3,64,128]{3,2,1,0:T(8,128)S(1)}, u32[]{:S(2)}, u32[]{:S(2)}) collective-permute-start(f32[2,3,64,128]{3,2,1,0:T(8,128)S(1)} %get-tuple-element.31), channel_id=1, source_target_pairs={{0,30},{2,4},{4,2},{6,8},{8,6},{10,12},{12,10},{14,16},{16,14},{18... | collective-permute-start | bytes 589832 | tf_op jit(solution)/shard_map/ppermute | solution.py:264
  11.5 5.0 %collective-permute-start.3 = (f32[12,64,128]{2,1,0:T(8,128)S(1)}, f32[12,64,128]{2,1,0:T(8,128)S(1)}, u32[]{:S(2)}, u32[]{:S(2)}) collective-permute-start(f32[12,64,128]{2,1,0:T(8,128)S(1)} %near_first.1.after_ref.near_next_v), channel_id=1, source_target_pairs={{0,2},{2,0},{4,6},{6,4},{8,10},{10,8},{12,14},{14,12},{16,18},{18,... | collective-permute-start | bytes 1179656 | tf_op jit(solution)/shard_map/ppermute | solution.py:302
  11.9 7.9 %collective-permute-start.5 = (f32[3,64,128]{2,1,0:T(8,128)S(1)}, f32[3,64,128]{2,1,0:T(8,128)S(1)}, u32[]{:S(2)}, u32[]{:S(2)}) collective-permute-start(f32[3,64,128]{2,1,0:T(8,128)S(1)} %get-tuple-element.29.far_next_ref), channel_id=1, source_target_pairs={{0,30},{2,4},{4,2},{6,8},{8,6},{10,12},{12,10},{14,16},{16,14},{18... | collective-permute-start | bytes 294920 | tf_op jit(solution)/shard_map/ppermute | solution.py:334
  16.4 6.9 %collective-permute-start.6 = (f32[3,64,128]{2,1,0:T(8,128)S(1)}, f32[3,64,128]{2,1,0:T(8,128)S(1)}, u32[]{:S(2)}, u32[]{:S(2)}) collective-permute-start(f32[3,64,128]{2,1,0:T(8,128)S(1)} %get-tuple-element.30.far_after_ref), channel_id=1, source_target_pairs={{0,30},{2,4},{4,2},{6,8},{8,6},{10,12},{12,10},{14,16},{16,14},{18... | collective-permute-start | bytes 294920 | tf_op jit(solution)/shard_map/ppermute | solution.py:335
  17.4 6.9 %collective-permute-start.8 = (f32[2,7,32,128]{3,2,1,0:T(8,128)S(1)}, f32[2,7,32,128]{3,2,1,0:T(8,128)S(1)}, u32[]{:S(2)}, u32[]{:S(2)}) collective-permute-start(f32[2,7,32,128]{3,2,1,0:T(8,128)S(1)} %bitcast.17), channel_id=1, source_target_pairs={{0,1},{1,0},{2,3},{3,2},{4,5},{5,4},{6,7},{7,6},{8,9},{9,8},{10,11... | collective-permute-start | bytes 688136 | tf_op jit(solution)/shard_map/ppermute | solution.py:394
  19.9 4.4 %collective-permute-start.7 = (f32[2,1,32,128]{3,2,1,0:T(8,128)S(1)}, f32[2,1,32,128]{3,2,1,0:T(8,128)S(1)}, u32[]{:S(2)}, u32[]{:S(2)}) collective-permute-start(f32[2,1,32,128]{3,2,1,0:T(8,128)S(1)} %bitcast.18), channel_id=1, source_target_pairs={{0,1},{1,0},{2,3},{3,2},{4,5},{5,4},{6,7},{7,6},{8,9},{9,8},{10,11... | collective-permute-start | bytes 98312 | tf_op jit(solution)/shard_map/ppermute | solution.py:461
